TPU v7x, 32 devices: a whole 2x2x4 slice. The times are simulated.
32 devices in a mesh: groups: 2 (over y), ctx: 4 (over z), head: 4 (over x, core).
Axes of the slice: x: 2, y: 2, z: 4, core: 2. Of those that a mesh axis runs over, the one named last changes fastest.
Arguments:
- queries: bfloat16 [4096, 4096], P(('groups', 'ctx', 'head')), parts along dimension 0, may hold values from -6 to 6
- keys_in: bfloat16 [4096, 4096], P(('groups', 'ctx', 'head')), parts along dimension 0, may hold values from -6 to 6
- values: bfloat16 [4096, 4096], P(('groups', 'ctx', 'head')), parts along dimension 0, may hold values from -6 to 6
- doc_lengths: int32 [10], P('groups'), parts along dimension 0, may hold values from 1 to 512, 2048 in all
- rms_gain: float32 [4096], replicated, may hold values from 0.1 to 1.9
Outputs:
- mixed: bfloat16 [4096, 4096], P(('groups', 'ctx', 'head')), parts along dimension 0
There are 2 independent parts, one for each index of `groups`. A program takes and returns all parts, laid end to end along the dimension named above; an argument that names none is the same for every part. Nothing has to cross between parts.
Inputs may be any that keep to these rules, and one draw needn't show every extreme that they name: `doc_lengths`: the lengths of the 5 documents sum to 2048, and the longest has exactly 512 tokens.
All inputs are finite; a program needn't handle non-finite values.
Results may differ from a plain program's by a relative error of at most 0.006.
Values may be sent and summed in bfloat16 or wider, within the bound.
No kernel may reach another device: no remote copies, remote signals or barrier semaphores. Data moves between devices by JAX's collectives and lax.ppermute only.
A program may use at most 64 MiB of HBM per device.

v0:
```python
import jax
import jax.numpy as jnp
from jax import lax
from jax.sharding import PartitionSpec as P

DH = 128


def doc_ids(doc_ends, positions):
    counted = jnp.sum((positions[:, None] >= doc_ends[None, :]).astype(jnp.int32), axis=1)
    return jnp.where(positions < 0, -1, counted)


def local_part(q_shard, k_shard, v_shard, segment):
    shard_rows = q_shard.shape[0]
    block_rows = min(512, shard_rows)
    order = jnp.arange(shard_rows, dtype=jnp.int32)
    pieces = []
    for block_id in range(shard_rows // block_rows):
        first_row = block_id * block_rows
        last_row = first_row + block_rows
        scores = jnp.einsum(
            "qhd,khd->hqk",
            q_shard[first_row:last_row],
            k_shard[:last_row],
            preferred_element_type=jnp.float32,
        )
        allowed = (segment[first_row:last_row, None] == segment[None, :last_row]) & (
            order[first_row:last_row, None] >= order[None, :last_row]
        )
        weights = jnp.where(allowed[None], scores, 0.0).astype(jnp.bfloat16)
        pieces.append(
            jnp.einsum(
                "hqk,khd->qhd", weights, v_shard[:last_row], preferred_element_type=jnp.float32
            )
        )
    return jnp.concatenate(pieces, axis=0)


def per_device(queries, keys_in, values, doc_lengths, rms_gain):
    head_parts = lax.axis_size("head")
    row_count, full_width = queries.shape
    local_heads = full_width // (head_parts * DH)
    shard_rows = row_count * head_parts
    shard_start = lax.axis_index("ctx") * shard_rows
    doc_ends = jnp.cumsum(doc_lengths)
    split_shape = (row_count, head_parts, local_heads, DH)
    q_part = lax.all_to_all(
        queries.reshape(split_shape), "head", split_axis=1, concat_axis=0, tiled=True
    )
    k_part = lax.all_to_all(
        keys_in.reshape(split_shape), "head", split_axis=1, concat_axis=0, tiled=True
    )
    v_part = lax.all_to_all(
        values.reshape(split_shape), "head", split_axis=1, concat_axis=0, tiled=True
    )
    q_shard = jax.nn.silu(q_part[:, 0].astype(jnp.float32)).astype(jnp.bfloat16)
    k_shard = jax.nn.silu(k_part[:, 0].astype(jnp.float32)).astype(jnp.bfloat16)
    v_shard = v_part[:, 0]
    positions = shard_start + jnp.arange(shard_rows, dtype=jnp.int32)
    segment = doc_ids(doc_ends, positions)
    before = doc_ids(doc_ends, jnp.reshape(shard_start - 1, (1,)))[0]
    local = local_part(q_shard, k_shard, v_shard, segment)
    keep = (segment == segment[-1])[:, None, None]
    masked_keys = jnp.where(keep, k_shard, jnp.zeros_like(k_shard))
    tail = jnp.einsum("shd,she->hde", masked_keys, v_shard, preferred_element_type=jnp.float32)
    reset_flag = jnp.reshape((segment[-1] != before).astype(jnp.float32), (1,))
    all_flags = lax.all_gather(reset_flag, "ctx", axis=0, tiled=True)
    my_shard = lax.axis_index("ctx")
    shard_ids = jnp.arange(all_flags.shape[0], dtype=jnp.int32)
    last_reset = jnp.max(jnp.where((shard_ids < my_shard) & (all_flags > 0), shard_ids, 0))
    piece = lax.all_gather(tail[None], "ctx", axis=0, tiled=True)
    piece_ids = jnp.arange(piece.shape[0], dtype=jnp.int32)
    weight = ((piece_ids < my_shard) & (piece_ids >= last_reset)).astype(jnp.float32)
    carried = jnp.einsum("n,nhde->hde", weight, piece, precision=lax.Precision.HIGHEST)
    inter = jnp.einsum(
        "shd,hde->she", q_shard.astype(jnp.float32), carried, precision=lax.Precision.HIGHEST
    )
    joined = (segment == before)[:, None, None]
    attended = (local + jnp.where(joined, inter, 0.0)).astype(jnp.bfloat16)
    regrouped = lax.all_to_all(attended[:, None], "head", split_axis=0, concat_axis=1, tiled=True)
    output = regrouped.reshape(row_count, full_width).astype(jnp.float32)
    meansq = jnp.mean(output * output, axis=1, keepdims=True)
    return (output * lax.rsqrt(meansq + 1e-05) * rms_gain).astype(jnp.bfloat16)


def solution(mesh):
    return jax.shard_map(
        per_device,
        mesh=mesh,
        in_specs=(
            P(("groups", "ctx", "head"), None),
            P(("groups", "ctx", "head"), None),
            P(("groups", "ctx", "head"), None),
            P("groups"),
            P(),
        ),
        out_specs=P(("groups", "ctx", "head"), None),
        check_vma=False,
    )
```

profile of v0, /device:TPU:0, one launch (start us, length us, event | category | flops | bytes accessed | tf_op | source)
XLA Modules:
  0.0 142.2 jit_solution(3803284936650284072)
XLA Ops:
  6.5 1.6 %copy.44 = bf16[128,4096]{0,1:T(8,128)(2,1)S(1)} copy(bf16[128,4096]{1,0:T(8,128)(2,1)} %param.7) | data formatting | bytes 2097152 | tf_op args[2]
  8.2 0.0 copy-start.5
  8.2 0.0 copy-start.1
  8.2 1.3 copy.45
  9.5 4.2 %all-to-all-start.2 = ((bf16[128,4,8,128]{3,0,2,1:T(8,128)(2,1)}), bf16[128,4,8,128]{3,0,2,1:T(8,128)(2,1)S(1)}, u32[]{:S(2)}, u32[]{:S(2)}) async-start(bf16[128,4,8,128]{3,0,2,1:T(8,128)(2,1)} %copy.45), calls=%async_computation.2 | async-start | bytes 2097152 | tf_op jit(solution)/shard_map/all_to_all | solution.py:54
  13.7 0.0 copy-done.5
  13.7 0.2 reduce-window.4
  13.9 0.0 copy-done.1
  13.9 0.7 copy.40
  14.5 1.5 %copy.41 = bf16[128,4,8,128]{3,2,0,1:T(8,128)(2,1)} copy(bf16[128,4,8,128]{0,3,2,1:T(8,128)(2,1)S(1)} %bitcast.59) | data formatting | bytes 2097152 | tf_op jit(solution)/shard_map/reshape | solution.py:52
  16.0 12.1 %all-to-all-done.2 = bf16[128,4,8,128]{3,0,2,1:T(8,128)(2,1)S(1)} async-done(((bf16[128,4,8,128]{3,0,2,1:T(8,128)(2,1)}), bf16[128,4,8,128]{3,0,2,1:T(8,128)(2,1)S(1)}, u32[]{:S(2)}, u32[]{:S(2)}) %all-to-all-start.2) | async-done | bytes 1048608 | tf_op jit(solution)/shard_map/all_to_all | solution.py:54
  28.2 3.5 %all-to-all-start.1 = ((bf16[128,4,8,128]{3,2,0,1:T(8,128)(2,1)}), bf16[128,4,8,128]{3,2,0,1:T(8,128)(2,1)S(1)}, u32[]{:S(2)}, u32[]{:S(2)}) async-start(bf16[128,4,8,128]{3,2,0,1:T(8,128)(2,1)} %copy.41), calls=%async_computation.1 | async-start | bytes 2097152 | tf_op jit(solution)/shard_map/all_to_all | solution.py:51
  31.7 0.0 all-gather.3.cloned.1.call-start
  31.7 0.6 fusion.19
  33.0 0.1 convert_reduce_fusion
  33.1 0.5 slice.4
  33.7 0.5 broadcast_compare_fusion
  34.2 1.0 copy.46
  35.3 10.8 %all-to-all-done.1 = bf16[128,4,8,128]{3,2,0,1:T(8,128)(2,1)S(1)} async-done(((bf16[128,4,8,128]{3,2,0,1:T(8,128)(2,1)}), bf16[128,4,8,128]{3,2,0,1:T(8,128)(2,1)S(1)}, u32[]{:S(2)}, u32[]{:S(2)}) %all-to-all-start.1) | async-done | bytes 1048608 | tf_op jit(solution)/shard_map/all_to_all | solution.py:51
  46.1 0.1 bitcast_convert_fusion
  46.3 1.1 copy-done.2
  47.3 1.8 %fusion.9 = f32[8,128,128]{2,1,0:T(8,128)} fusion(bf16[512,8,128]{2,0,1:T(8,128)(2,1)S(1)} %bitcast.66, pred[512]{0:T(512)(128)(4,1)S(1)} %broadcast_compare_fusion, f32[512,8,128]{2,1,0:T(8,128)S(1)} %bitcast.61), kind=kOutput, calls=%fused_computation.16 | convolution fusion | flops 137363456 | bytes 3670528 | tf_op jit(solution)/shard_map/shd,she->hde/dot_general | solution.py:66
  49.1 0.0 all-gather.3.cloned.1.call-update
  49.1 1.6 %copy.36 = bf16[128,4096]{0,1:T(8,128)(2,1)S(1)} copy(bf16[128,4096]{1,0:T(8,128)(2,1)} %param.5) | data formatting | bytes 2097152 | tf_op args[0]
  50.8 0.0 copy-start.6
  50.8 1.5 %copy.37 = bf16[128,4,8,128]{3,2,0,1:T(8,128)(2,1)} copy(bf16[128,4,8,128]{0,3,2,1:T(8,128)(2,1)S(1)} %bitcast.60) | data formatting | bytes 2097152 | tf_op jit(solution)/shard_map/reshape | solution.py:49
  52.2 3.5 %all-to-all-start = ((bf16[128,4,8,128]{3,2,0,1:T(8,128)(2,1)}), bf16[128,4,8,128]{3,2,0,1:T(8,128)(2,1)S(1)}, u32[]{:S(2)}, u32[]{:S(2)}) async-start(bf16[128,4,8,128]{3,2,0,1:T(8,128)(2,1)} %copy.37), calls=%async_computation | async-start | bytes 2097152 | tf_op jit(solution)/shard_map/all_to_all | solution.py:48
  56.3 0.0 copy-done.6
  56.3 0.6 dynamic-slice
  56.9 0.7 dynamic-update-slice
  57.7 13.2 %all-reduce = f32[4]{0:T(128)S(1)} all-reduce(f32[4]{0:T(128)S(1)} %dynamic-update-slice), channel_id=1, replica_groups=mesh['groups'=2,'ctx'=4,'head'=4] {'ctx'}, use_global_device_ids=true, to_apply=%add | all-reduce | flops 4 | bytes 32
  70.9 0.6 fusion.20
  71.5 0.2 fusion.12
  71.7 0.0 all-to-all-done
  71.7 1.4 %bitcast_convert_fusion.1 = f32[128,4,1,8,128]{4,3,0,1,2:T(8,128)} fusion(bf16[128,4,8,128]{3,2,0,1:T(8,128)(2,1)S(1)} %all-to-all-done), kind=kLoop, calls=%fused_computation.15 | loop fusion | flops 524288 | bytes 3145728 | tf_op jit(solution)/shard_map/convert_element_type | solution.py:57
  73.1 23.4 %all-gather.3.cloned.1.call-done = f32[32,128,128]{2,1,0:T(8,128)} async-done(((f32[8,128,128]{2,1,0:T(8,128)}), f32[32,128,128]{2,1,0:T(8,128)}) %all-gather.3.cloned.1.call-update) | async-done | bytes 2097168 | tf_op jit(solution)/shard_map/all_gather | solution.py:72
  96.5 5.5 %fusion.6 = f32[1,8,128,128]{3,0,2,1:T(1,128)S(1)} fusion(f32[4,8,128,128]{3,2,1,0:T(8,128)} %bitcast.63, s32[]{:T(128)} %fusion.20, s32[]{:T(128)S(6)} %axis_index.19), kind=kOutput, calls=%fused_computation.7 | convolution fusion | flops 6291468 | bytes 2621448 | tf_op jit(solution)/shard_map/n,nhde->hde/dot_general | solution.py:75
  102.0 0.0 copy-start.3
  102.0 2.7 %fusion.26 = f32[8,128,512]{1,2,0:T(8,128)} fusion(f32[8,128,128]{2,1,0:T(8,128)S(1)} %bitcast.68, f32[512,8,128]{2,1,0:T(8,128)S(1)} %bitcast.65), kind=kOutput, calls=%fused_computation.43 | convolution fusion | flops 807927808 | bytes 4718592 | tf_op jit(solution)/shard_map/shd,hde->she/dot_general | solution.py:76
  104.7 5.8 %fusion.8 = bf16[512,1,8,128]{3,0,2,1:T(8,128)(2,1)} fusion(f32[8,128,512]{1,2,0:T(8,128)} %fusion.26, bf16[512,8,128]{2,0,1:T(8,128)(2,1)S(1)} %bitcast.67, pred[512,512]{1,0:T(8,128)(4,1)S(1)} %fusion.12, pred[512]{0:T(512)(128)(4,1)S(1)} %get-tuple-element.5, f32[512,8,128]{2,1,0:T(8,128)S(1)} %bitcast.62, f32[512,8,128]{2,1,0:T(8,128)} %bitcast.64), kind=kOutput, calls=%fused_computation.13 | convolution fusion | flops 1084751872 | bytes 8651264 | tf_op jit(solution)/shard_map/hqk,khd->qhd/dot_general | solution.py:33
  110.5 1.9 %copy.49 = bf16[512,1,8,128]{3,2,1,0:T(8,128)(2,1)S(1)} copy(bf16[512,1,8,128]{3,0,2,1:T(8,128)(2,1)} %fusion.8) | data formatting | bytes 2097152 | tf_op jit(solution)/shard_map/broadcast_in_dim | solution.py:81
  112.4 17.0 %all_to_all.42 = bf16[512,1,8,128]{3,2,1,0:T(8,128)(2,1)S(1)} all-to-all(bf16[512,1,8,128]{3,2,1,0:T(8,128)(2,1)S(1)} %copy.49), channel_id=1, replica_groups=mesh['groups'=2,'ctx'=4,'head'=4] {'head'}, dimensions={0} | all-to-all | bytes 2097152 | tf_op jit(solution)/shard_map/all_to_all | solution.py:81
  129.4 1.0 multiply_reduce_fusion
  130.5 0.1 convert_element_type.102
  130.7 1.6 %copy.50 = f32[128,4,1,8,128]{4,3,1,0,2:T(8,128)} copy(f32[128,4,1,8,128]{4,3,0,1,2:T(8,128)S(1)} %bitcast.56) | data formatting | bytes 4194304 | tf_op jit(solution)/shard_map/convert_element_type | solution.py:82
  132.3 1.8 %reshape.162 = f32[128,4096]{1,0:T(8,128)S(1)} reshape(f32[128,4,1,8,128]{4,3,1,0,2:T(8,128)} %copy.50) | data formatting | bytes 4194304 | tf_op jit(solution)/shard_map/convert_element_type | solution.py:82
  134.1 0.0 copy-done.4
  134.1 1.3 multiply_convert_fusion
  (10 shorter events, 0.1 us)
Async XLA Ops:
  8.2 5.5 %copy-start.5 = (s32[5]{0:T(128)S(1)}, s32[5]{0:T(128)}, u32[]{:S(2)}) copy-start(s32[5]{0:T(128)} %param.8) | copy-start | bytes 64
  8.2 5.7 %copy-start.1 = (bf16[128,4096]{1,0:T(8,128)(2,1)S(1)}, bf16[128,4096]{1,0:T(8,128)(2,1)}, u32[]{:S(2)}) copy-start(bf16[128,4096]{1,0:T(8,128)(2,1)} %param.6) | copy-start | bytes 3145732
  9.5 18.7 %all-to-all-start.2 = ((bf16[128,4,8,128]{3,0,2,1:T(8,128)(2,1)}), bf16[128,4,8,128]{3,0,2,1:T(8,128)(2,1)S(1)}, u32[]{:S(2)}, u32[]{:S(2)}) async-start(bf16[128,4,8,128]{3,0,2,1:T(8,128)(2,1)} %copy.45), calls=%async_computation.2 | async-start | bytes 2097152 | tf_op jit(solution)/shard_map/all_to_all | solution.py:54
  28.2 18.0 %all-to-all-start.1 = ((bf16[128,4,8,128]{3,2,0,1:T(8,128)(2,1)}), bf16[128,4,8,128]{3,2,0,1:T(8,128)(2,1)S(1)}, u32[]{:S(2)}, u32[]{:S(2)}) async-start(bf16[128,4,8,128]{3,2,0,1:T(8,128)(2,1)} %copy.41), calls=%async_computation.1 | async-start | bytes 2097152 | tf_op jit(solution)/shard_map/all_to_all | solution.py:51
  31.7 64.8 %all-gather.3.cloned.1.call-start = ((), (), s32[]{:S(2)}) async-start(), calls=%async_computation.4 | async-start | bytes 2621440 | tf_op jit(solution)/shard_map/all_gather | solution.py:72
  46.1 1.2 copy-start.2
  50.8 5.6 %copy-start.6 = (u32[32]{0:T(128)S(1)}, u32[32]{0:T(128)}, u32[]{:S(2)}) copy-start(u32[32]{0:T(128)} %constant.40) | copy-start | bytes 388
  52.2 19.4 %all-to-all-start = ((bf16[128,4,8,128]{3,2,0,1:T(8,128)(2,1)}), bf16[128,4,8,128]{3,2,0,1:T(8,128)(2,1)S(1)}, u32[]{:S(2)}, u32[]{:S(2)}) async-start(bf16[128,4,8,128]{3,2,0,1:T(8,128)(2,1)} %copy.37), calls=%async_computation | async-start | bytes 2097152 | tf_op jit(solution)/shard_map/all_to_all | solution.py:48
  96.5 5.5 %copy-start = (f32[128,4,1,8,128]{4,3,0,1,2:T(8,128)S(1)}, f32[128,4,1,8,128]{4,3,0,1,2:T(8,128)}, u32[]{:S(2)}) copy-start(f32[128,4,1,8,128]{4,3,0,1,2:T(8,128)} %bitcast_convert_fusion.1) | copy-start | bytes 6291460
  102.0 2.7 %copy-start.3 = (bf16[4,128,1,8,128]{4,1,0,3,2:T(8,128)(2,1)S(1)}, bf16[4,128,1,8,128]{4,1,0,3,2:T(8,128)(2,1)}, u32[]{:S(2)}) copy-start(bf16[4,128,1,8,128]{4,1,0,3,2:T(8,128)(2,1)} %copy.46) | copy-start | bytes 3145732
  132.3 1.8 %copy-start.4 = (f32[4096]{0:T(1024)S(1)}, f32[4096]{0:T(1024)}, u32[]{:S(2)}) copy-start(f32[4096]{0:T(1024)} %param.9) | copy-start | bytes 49156
Sparse Core Ops, SparseCore 0:
  49.3 47.1 all-gather.2
where the time goes:
time: 143 us; the launch traced here: 142 us
  waiting for transfers between devices  46.4 us (32%)
  blocking collectives  30.2 us (21%)
  local copies, waits for them, and re-layouts  17.5 us (12%)
  matrix products  15.7 us (11%)
  between operations  14.8 us (10%)
  starting transfers between devices  11.3 us (8%)
  other arithmetic  6.28 us (4%)
    all_gather x1, waiting for transfers between devices, per_device(): piece = lax.all_gather(tail[None], 'ctx', axis=0, tiled=True)  23.4 us
    all_to_all x1, blocking collectives, per_device(): lax.all_to_all(attended[:, None], 'head', split_axis=0, concat_axis=1, ti...  17 us
    unnamed x1, blocking collectives  13.2 us
    all_to_all x1, waiting for transfers between devices, per_device(): lax.all_to_all(values.reshape(split_shape), 'head', split_axis=1, concat_...  12.1 us
    all_to_all x1, waiting for transfers between devices, per_device(): lax.all_to_all(keys_in.reshape(split_shape), 'head', split_axis=1, concat...  10.8 us
    unnamed x20, local copies, waits for them, and re-layouts  6.32 us
    dot_general x1, matrix products, local_part(): jnp.einsum('hqk,khd->qhd', weights, v_shard[:last_row], preferred_element...  5.81 us
    dot_general x1, matrix products, per_device(): jnp.einsum('n,nhde->hde', weight, piece, precision=lax.Precision.HIGHEST)  5.5 us
  transfers between devices with their start and end apart: 4, of which 3 were waited for; matrix products, arithmetic and copies ran while one was open for 8% of the time, Pallas kernels for 0%

commit v1 on v0

v1 whole, which is shorter than its diff:
```python
import functools
import jax
import jax.numpy as jnp
from jax import lax
from jax.experimental import pallas as pl
from jax.experimental.pallas import tpu as pltpu
from jax.sharding import PartitionSpec as P

DH = 128
F32, BF16 = jnp.float32, jnp.bfloat16
VMEM_LIMIT = 32 << 20


def silu(x):
    x = x.astype(F32)
    return x / (1.0 + jnp.exp(-x))


def doc_start(len_ref, position):
    start = jnp.zeros_like(position)
    end = jnp.int32(0)
    for doc in range(len_ref.shape[0]):
        end = end + len_ref[doc]
        start = jnp.where(position >= end, end, start)
    return start


def same_doc(len_ref, earlier, later):
    return doc_start(len_ref, later) <= earlier


def state_kernel(rows, len_ref, at_ref, k_ref, v_ref, t_ref):
    first = at_ref[0] * rows
    kept = doc_start(len_ref, first + rows - 1) - first
    keep = lax.broadcasted_iota(jnp.int32, (rows, DH), 0) >= kept
    for h in range(t_ref.shape[0]):
        cols = slice(h * DH, (h + 1) * DH)
        k = jnp.where(keep, silu(k_ref[:, cols]), 0.0).astype(BF16)
        t = lax.dot_general(k, v_ref[:, cols], (((0,), (0,)), ((), ())), preferred_element_type=F32)
        t_ref[h] = t.astype(t_ref.dtype)


def states(lens, at, k, v, first_head, heads, heads_total, dtype):
    rows = k.shape[0]
    step = min(8, heads)
    spec = pl.BlockSpec((rows, step * DH), lambda i, n, a: (0, first_head(a) // step + i))
    return pl.pallas_call(
        functools.partial(state_kernel, rows),
        out_shape=jax.ShapeDtypeStruct((heads, DH, DH), dtype),
        grid_spec=pltpu.PrefetchScalarGridSpec(
            num_scalar_prefetch=2,
            grid=(heads // step,),
            in_specs=[spec, spec],
            out_specs=pl.BlockSpec((step, DH, DH), lambda i, n, a: (i, 0, 0)),
        ),
        compiler_params=pltpu.CompilerParams(vmem_limit_bytes=VMEM_LIMIT),
        cost_estimate=pl.CostEstimate(
            flops=2 * heads * rows * DH * DH, bytes_accessed=heads * DH * (4 * rows + 2 * DH), transcendentals=heads * rows * DH
        ),
    )(lens, at, k, v)


def chip_kernel(rows, len_ref, at_ref, own_ref, got_ref, p1_ref, a_ref, b_ref):
    at = at_ref[0]
    core, x = at % 2, (at // 2) % 2
    low = at - core
    whole = same_doc(len_ref, low * rows + rows - 1, (low + 2) * rows - 1)
    w_own = jnp.where((core == 1) | whole, 1.0, 0.0)
    w_got = jnp.where((core == 0) | whole, 1.0, 0.0)
    half = a_ref.shape[0]
    for h in range(2 * half):
        s = (own_ref[h].astype(F32) * w_own + got_ref[h].astype(F32) * w_got).astype(BF16)
        if h < half:
            a_ref[h] = s

            @pl.when(x == 0)
            def _():
                p1_ref[h] = s
        else:
            b_ref[h - half] = s

            @pl.when(x == 1)
            def _():
                p1_ref[h - half] = s


def relay_kernel(rows, len_ref, at_ref, r2_ref, b_ref, p3_ref):
    x = (at_ref[0] // 2) % 2

    @pl.when(x == 0)
    def _():
        p3_ref[...] = b_ref[...]

    @pl.when(x == 1)
    def _():
        p3_ref[...] = r2_ref[...]


def carry_kernel(rows, len_ref, at_ref, r1_ref, b_ref, p4_ref):
    at = at_ref[0]
    x = (at // 2) % 2
    chip = at // 2 * 2 * rows
    goes_on = same_doc(len_ref, chip + 2 * rows - 1, chip + 4 * rows - 1)
    w_b = jnp.where((x == 1) | goes_on, 1.0, 0.0)
    w_r = jnp.where(x == 0, 1.0, 0.0)
    for h in range(p4_ref.shape[0]):
        p4_ref[h] = (b_ref[h].astype(F32) * w_b + r1_ref[h].astype(F32) * w_r).astype(BF16)


def join_kernel(rows, len_ref, at_ref, r1_ref, r2_ref, r3_ref, r4_ref, own_ref, got_ref, mine_ref, send_ref):
    at = at_ref[0]
    core, x = at % 2, (at // 2) % 2
    low = at - core
    chip = low * rows
    w = jnp.where(same_doc(len_ref, chip - 2 * rows - 1, chip - 1), 1.0, 0.0)
    on = jnp.where(same_doc(len_ref, chip - 1, chip + rows - 1), 1.0, 0.0)
    w4 = jnp.where(x == 0, 1.0, w)
    half = r1_ref.shape[0]
    for h in range(2 * half):
        if h < half:
            near = jnp.where(x == 0, r3_ref[h].astype(F32), r1_ref[h].astype(F32))
            p = near + w * r2_ref[h].astype(F32)
        else:
            near = jnp.where(x == 0, 0.0, r3_ref[h - half].astype(F32))
            p = near + w4 * r4_ref[h - half].astype(F32)
        low_t = jnp.where(core == 0, own_ref[h].astype(F32), got_ref[h].astype(F32))
        upper = (low_t + on * p).astype(BF16)
        p = p.astype(BF16)
        mine_ref[h] = jnp.where(core == 0, p, upper)
        send_ref[h] = jnp.where(core == 0, upper, p)


def small_call(kernel, rows, lens, at, ins, outs):
    vmem = pl.BlockSpec(memory_space=pltpu.VMEM)
    smem = pl.BlockSpec(memory_space=pltpu.SMEM)
    many = len(outs) > 1
    shapes = [jax.ShapeDtypeStruct(s, BF16) for s in outs]
    return pl.pallas_call(
        functools.partial(kernel, rows),
        out_shape=shapes if many else shapes[0],
        in_specs=[smem, smem] + [vmem] * len(ins),
        out_specs=[vmem] * len(outs) if many else vmem,
        compiler_params=pltpu.CompilerParams(vmem_limit_bytes=VMEM_LIMIT),
        cost_estimate=pl.CostEstimate(flops=1 << 20, bytes_accessed=2 << 20, transcendentals=0),
    )(lens, at, *ins)


def local_kernel(rows, len_ref, at_ref, q_ref, k_ref, v_ref, loc_ref, qm_ref):
    first = at_ref[0] * rows
    i = first + lax.broadcasted_iota(jnp.int32, (rows, rows), 0)
    j = first + lax.broadcasted_iota(jnp.int32, (rows, rows), 1)
    start = doc_start(len_ref, i)
    allowed = (j <= i) & (j >= start)
    i_q = first + lax.broadcasted_iota(jnp.int32, (rows, DH), 0)
    joined = doc_start(len_ref, i_q) < first
    for h in range(q_ref.shape[1] // DH):
        cols = slice(h * DH, (h + 1) * DH)
        q = silu(q_ref[:, cols])
        k = silu(k_ref[:, cols]).astype(BF16)
        qm_ref[:, cols] = jnp.where(joined, q, 0.0).astype(BF16)
        s = lax.dot_general(q.astype(BF16), k, (((1,), (1,)), ((), ())), preferred_element_type=F32)
        s = jnp.where(allowed, s, 0.0).astype(BF16)
        loc_ref[:, cols] = jnp.dot(s, v_ref[:, cols], preferred_element_type=F32)


def local_part(lens, at, q, k, v):
    rows, width = q.shape
    step = min(8 * DH, width)
    spec = pl.BlockSpec((rows, step), lambda i, n, a: (0, i))
    return pl.pallas_call(
        functools.partial(local_kernel, rows),
        out_shape=[jax.ShapeDtypeStruct((rows, width), F32), jax.ShapeDtypeStruct((rows, width), BF16)],
        grid_spec=pltpu.PrefetchScalarGridSpec(
            num_scalar_prefetch=2,
            grid=(width // step,),
            in_specs=[spec] * 3,
            out_specs=[spec, spec],
        ),
        compiler_params=pltpu.CompilerParams(vmem_limit_bytes=VMEM_LIMIT),
        cost_estimate=pl.CostEstimate(flops=4 * rows * rows * width, bytes_accessed=12 * rows * width, transcendentals=2 * rows * width),
    )(lens, at, q, k, v)


def final_kernel(off_ref, loc_ref, qm_ref, mine_ref, other_ref, gain_ref, out_ref, att_ref):
    rows, width = out_ref.shape
    half = mine_ref.shape[0]
    total = jnp.zeros((rows, 1), F32)
    for part, p_ref in ((0, mine_ref), (1, other_ref)):
        base = jnp.where(off_ref[0] == part, 0, half * DH)
        for h in range(half):
            cols = pl.ds(pl.multiple_of(base + h * DH, DH), DH)
            att = loc_ref[:, cols] + jnp.dot(qm_ref[:, cols], p_ref[h], preferred_element_type=F32)
            att = att.astype(BF16)
            att_ref[:, cols] = att
            wide = att.astype(F32)
            total = total + jnp.sum(wide * wide, axis=1, keepdims=True)
    scale = lax.rsqrt(total / width + 1e-5)
    for h in range(2 * half):
        cols = slice(h * DH, (h + 1) * DH)
        out_ref[:, cols] = (att_ref[:, cols].astype(F32) * scale * gain_ref[:, cols]).astype(BF16)


def final(off, loc, qm, mine, other, gain):
    rows, width = loc.shape
    vmem = pl.BlockSpec(memory_space=pltpu.VMEM)
    return pl.pallas_call(
        final_kernel,
        out_shape=jax.ShapeDtypeStruct((rows, width), BF16),
        in_specs=[pl.BlockSpec(memory_space=pltpu.SMEM)] + [vmem] * 5,
        out_specs=vmem,
        scratch_shapes=[pltpu.VMEM((rows, width), BF16)],
        compiler_params=pltpu.CompilerParams(vmem_limit_bytes=VMEM_LIMIT),
        cost_estimate=pl.CostEstimate(flops=2 * rows * DH * width, bytes_accessed=12 * rows * width, transcendentals=rows),
    )(off, loc, qm, mine, other, gain.reshape(1, width))


def general(lens, at, q, k, v, gain):
    rows, width = q.shape
    heads = width // DH
    blocks = lax.axis_size("ctx") * lax.axis_size("head")
    axes = ("ctx", "head")
    state = states(lens, at, k, v, lambda a: 0, heads, heads, F32)
    me = at[0]
    ends = jnp.cumsum(lens)

    def segment(position):
        return jnp.where(position < 0, -1, jnp.sum((position >= ends).astype(jnp.int32)))

    hop = 1
    while hop < blocks:
        came = lax.ppermute(state, axes, [(b, b + hop) for b in range(blocks - hop)])
        adds = segment((me + 1) * rows - 1) == segment((me + 1 - hop) * rows - 1)
        state = state + jnp.where(adds, came, 0.0)
        hop *= 2
    before = lax.ppermute(state, axes, [(b, b + 1) for b in range(blocks - 1)]).astype(BF16)
    loc, qm = local_part(lens, at, q, k, v)
    return final(jnp.zeros((1,), jnp.int32), loc, qm, before[: heads // 2], before[heads // 2 :], gain)


def neighbours(lens, at, q, k, v, gain):
    rows, width = q.shape
    heads = width // DH
    half, chunk = heads // 2, heads // 4
    ctx_parts = lax.axis_size("ctx")
    pair = [(0, 1), (1, 0), (2, 3), (3, 2)]
    across = [(0, 2), (2, 0), (1, 3), (3, 1)]
    onward = [(c, (c + 1) % ctx_parts) for c in range(ctx_parts)]
    theirs = states(lens, at, k, v, lambda a: (1 - a[0] % 2) * half, half, heads, BF16)
    got = lax.ppermute(theirs, "head", pair)
    own = states(lens, at, k, v, lambda a: a[0] % 2 * half, half, heads, BF16)
    part = (chunk, DH, DH)
    p1, a, b = small_call(chip_kernel, rows, lens, at, [own, got], [part] * 3)
    r1 = lax.ppermute(p1, "head", across)
    r2 = lax.ppermute(a, "ctx", onward)
    loc, qm = local_part(lens, at, q, k, v)
    p4 = small_call(carry_kernel, rows, lens, at, [r1, b], [part])
    r4 = lax.ppermute(p4, "ctx", onward)
    p3 = small_call(relay_kernel, rows, lens, at, [r2, b], [part])
    r3 = lax.ppermute(p3, "head", across)
    mine, send = small_call(join_kernel, rows, lens, at, [r1, r2, r3, r4, own, got], [(half, DH, DH)] * 2)
    other = lax.ppermute(send, "head", pair)
    return final(at % 2, loc, qm, mine, other, gain)


def per_device(queries, keys_in, values, doc_lengths, rms_gain):
    head_parts = lax.axis_size("head")
    at = jnp.reshape(lax.axis_index(("ctx", "head")).astype(jnp.int32), (1,))
    args = (doc_lengths, at, queries, keys_in, values, rms_gain)
    if head_parts != 4:
        return general(*args)
    shard_rows = queries.shape[0] * head_parts
    return lax.cond(jnp.max(doc_lengths) <= shard_rows, neighbours, general, *args)


def solution(mesh):
    return jax.shard_map(
        per_device,
        mesh=mesh,
        in_specs=(
            P(("groups", "ctx", "head"), None),
            P(("groups", "ctx", "head"), None),
            P(("groups", "ctx", "head"), None),
            P("groups"),
            P(),
        ),
        out_specs=P(("groups", "ctx", "head"), None),
        check_vma=False,
    )
```

time: 143 us -> 38.2 us (0.27)
  waiting for transfers between devices: 46.4 us -> 12.4 us
  blocking collectives: 30.2 us -> 0 us
  local copies, waits for them, and re-layouts: 17.5 us -> 1 us
  matrix products: 15.7 us -> 0 us
  Pallas kernels: 0 us -> 14.8 us
  between operations: 14.8 us -> 0.67 us
  other arithmetic: 6.28 us -> 1.29 us
  starting transfers between devices: 11.3 us -> 7.74 us
    all_gather x1 -> x0, waiting for transfers between devices: 23.4 us -> none  [per_device(): piece = lax.all_gather(tail[None], 'ctx', axis=0, tiled=True)]
    all_to_all x3 -> x0, waiting for transfers between devices: 23 us -> none  [the longest x1 12.1 us: per_device(): lax.all_to_all(values.reshape(split_shape), 'head', split_axis=1, concat_...]
    all_to_all x1 -> x0, blocking collectives: 17 us -> none  [per_device(): lax.all_to_all(attended[:, None], 'head', split_axis=0, concat_axis=1, ti...]
    dot_general x4 -> x0, matrix products: 15.7 us -> none  [the longest x1 5.81 us: local_part(): jnp.einsum('hqk,khd->qhd', weights, v_shard[:last_row], preferred_element...]
    pallas_call x0 -> x8, Pallas kernels: none -> 14.8 us  [the longest x1 6.45 us: local_part(): pl.pallas_call(functools.partial(local_kernel, rows), out_shape=[jax.Shap...]
    unnamed x1 -> x0, blocking collectives: 13.2 us -> none
    ppermute x0 -> x6, waiting for transfers between devices: none -> 12.4 us  [the longest x1 5.67 us: neighbours(): r4 = lax.ppermute(p4, 'ctx', onward)]
    all_to_all x3 -> x0, starting transfers between devices: 11.2 us -> none  [the longest x1 4.21 us: per_device(): lax.all_to_all(values.reshape(split_shape), 'head', split_axis=1, concat_...]
  transfers between devices with their start and end apart: 4 -> 6, of which waited for: 3 -> 4; matrix products, arithmetic and copies ran while one was open for 8% -> 0% of each run, Pallas kernels for 0% -> 24%
where the time goes in v1:
time: 38.2 us; the launch traced here: 38 us
  Pallas kernels  14.8 us (39%)
  waiting for transfers between devices  12.4 us (32%)
  starting transfers between devices  7.74 us (20%)
  other arithmetic  1.29 us (3%)
  local copies, waits for them, and re-layouts  1 us (3%)
  between operations  0.67 us (2%)
    pallas_call x1, Pallas kernels, local_part(): pl.pallas_call(functools.partial(local_kernel, rows), out_shape=[jax.Shap...  6.45 us
    ppermute x1, waiting for transfers between devices, neighbours(): r4 = lax.ppermute(p4, 'ctx', onward)  5.67 us
    ppermute x1, waiting for transfers between devices, neighbours(): r1 = lax.ppermute(p1, 'head', across)  5.03 us
    pallas_call x2, Pallas kernels, states(): pl.pallas_call(functools.partial(state_kernel, rows), out_shape=jax.Shape...  4.09 us
    pallas_call x4, Pallas kernels, small_call(): pl.pallas_call(functools.partial(kernel, rows), out_shape=shapes if many...  3.07 us
    ppermute x1, starting transfers between devices, neighbours(): r1 = lax.ppermute(p1, 'head', across)  2.93 us
    ppermute x1, starting transfers between devices, neighbours(): r4 = lax.ppermute(p4, 'ctx', onward)  1.88 us
    ppermute x1, starting transfers between devices, neighbours(): r2 = lax.ppermute(a, 'ctx', onward)  1.57 us
  transfers between devices with their start and end apart: 6, of which 4 were waited for; matrix products, arithmetic and copies ran while one was open for 0% of the time, Pallas kernels for 24%

profile of v1, /device:TPU:0, one launch (start us, length us, event | category | flops | bytes accessed | tf_op | source)
XLA Modules:
  0.0 38.0 jit_solution(15857731845728275899)
XLA Ops:
  0.0 1.3 %reduce_max.9 = s32[]{:T(128)} reduce(s32[5]{0:T(128)} %param.10, s32[]{:T(128)} %constant.60.clone.1), dimensions={0}, to_apply=%region_0.0 | reduce | flops 4 | bytes 28 | tf_op jit(solution)/shard_map/reduce_max | solution.py:272
  1.9 35.1 %conditional.1 = (bf16[128,4096]{1,0:T(8,128)(2,1)S(1)}) conditional(s32[]{:T(128)} %convert_element_type.29, (s32[5]{0:T(128)}, s32[1]{0:T(128)}, bf16[128,4096]{1,0:T(8,128)(2,1)}, bf16[128,4096]{1,0:T(8,128)(2,1)}, bf16[128,4096]{1,0:T(8,128)(2,1)}, /*index=5*/s32[]{:T(128)}, f32[4096]{0:T(1024)}) %tuple.11, (s32[1]{0:T(128)}, s32[5]{0:T(128)}, ...), branch_computations={%region_1.8_spmd, %region_8.9_spmd} | conditional | flops 541589632 | bytes 92341056 | solution.py:272
  2.0 0.0 copy-start.1
  2.0 0.0 copy-start.3
  2.0 0.0 copy-start.10
  2.0 2.6 %branch_1_fun.10 = bf16[16,128,128]{2,1,0:T(8,128)(2,1)S(1)} custom-call(s32[5]{0:T(128)} %get-tuple-element.44.len_ref, s32[1]{0:T(128)} %get-tuple-element.43.at_ref, bf16[128,4096]{1,0:T(8,128)(2,1)} %get-tuple-element.46.k_ref, bf16[128,4096]{1,0:T(8,128)(2,1)} %get-tuple-element.47.v_ref), custom_call_target="tpu_custom_call" | custom-call | flops 67108864 | bytes 1572864 | tf_op jit(solution)/shard_map/cond/branch_1_fun/pallas_call | solution.py:47
  4.6 0.5 %collective-permute-start = (bf16[16,128,128]{2,1,0:T(8,128)(2,1)S(1)}, bf16[16,128,128]{2,1,0:T(8,128)(2,1)S(1)}, u32[]{:S(2)}, u32[]{:S(2)}) collective-permute-start(bf16[16,128,128]{2,1,0:T(8,128)(2,1)S(1)} %branch_1_fun.10), channel_id=1, source_target_pairs={{0,1},{1,0},{2,3},{3,2},{4,5},{5,4},{6,7},{7,6},{8,9},{9,8},{10,11... | collective-permute-start | bytes 1572872 | tf_op jit(solution)/shard_map/cond/branch_1_fun/ppermute | solution.py:249
  5.1 0.0 copy-done.1
  5.1 0.0 copy-done.3
  5.1 0.0 copy-done.10
  5.1 1.5 %branch_1_fun.9.own_ref = bf16[16,128,128]{2,1,0:T(8,128)(2,1)S(1)} custom-call(s32[5]{0:T(128)S(1)} %copy-done.10, s32[1]{0:T(128)} %get-tuple-element.43.at_ref, bf16[128,4096]{1,0:T(8,128)(2,1)S(1)} %copy-done.1, bf16[128,4096]{1,0:T(8,128)(2,1)S(1)} %copy-done.3), custom_call_target="tpu_custom_call" | custom-call | flops 67108864 | bytes 1572864 | tf_op jit(solution)/shard_map/cond/branch_1_fun/pallas_call | solution.py:47
  6.6 0.0 collective-permute-done.got_ref
  6.7 0.8 %branch_1_fun.11 = (bf16[8,128,128]{2,1,0:T(8,128)(2,1)S(1)}, bf16[8,128,128]{2,1,0:T(8,128)(2,1)S(1)}, bf16[8,128,128]{2,1,0:T(8,128)(2,1)S(1)}) custom-call(s32[5]{0:T(128)S(1)} %copy-done.10, s32[1]{0:T(128)} %get-tuple-element.43.at_ref, bf16[16,128,128]{2,1,0:T(8,128)(2,1)S(1)} %branch_1_fun.9.own_ref, ...), custom_call_target="tpu_custom_call" | custom-call | flops 1048576 | bytes 2097152 | tf_op jit(solution)/shard_map/cond/branch_1_fun/pallas_call | solution.py:138
  7.5 0.0 copy-start.5
  7.5 2.9 %collective-permute-start.1 = (bf16[8,128,128]{2,1,0:T(8,128)(2,1)S(1)}, bf16[8,128,128]{2,1,0:T(8,128)(2,1)S(1)}, u32[]{:S(2)}, u32[]{:S(2)}) collective-permute-start(bf16[8,128,128]{2,1,0:T(8,128)(2,1)S(1)} %get-tuple-element.50), channel_id=1, source_target_pairs={{0,2},{2,0},{1,3},{3,1},{4,6},{6,4},{5,7},{7,5},{8,10},{10,8},{9,1... | collective-permute-start | bytes 786440 | tf_op jit(solution)/shard_map/cond/branch_1_fun/ppermute | solution.py:253
  10.4 1.6 %collective-permute-start.2 = (bf16[8,128,128]{2,1,0:T(8,128)(2,1)S(1)}, bf16[8,128,128]{2,1,0:T(8,128)(2,1)S(1)}, u32[]{:S(2)}, u32[]{:S(2)}) collective-permute-start(bf16[8,128,128]{2,1,0:T(8,128)(2,1)S(1)} %get-tuple-element.51), channel_id=1, source_target_pairs={{0,4},{4,8},{8,12},{12,0},{1,5},{5,9},{9,13},{13,1},{2,6},{6,10},{... | collective-permute-start | bytes 786440 | tf_op jit(solution)/shard_map/cond/branch_1_fun/ppermute | solution.py:254
  12.0 5.0 %collective-permute-done.1.r1_ref = bf16[8,128,128]{2,1,0:T(8,128)(2,1)S(1)} collective-permute-done((bf16[8,128,128]{2,1,0:T(8,128)(2,1)S(1)}, bf16[8,128,128]{2,1,0:T(8,128)(2,1)S(1)}, u32[]{:S(2)}, u32[]{:S(2)}) %collective-permute-start.1) | collective-permute-done | bytes 262176 | tf_op jit(solution)/shard_map/cond/branch_1_fun/ppermute | solution.py:253
  17.0 0.6 %branch_1_fun.13 = bf16[8,128,128]{2,1,0:T(8,128)(2,1)S(1)} custom-call(s32[5]{0:T(128)S(1)} %copy-done.10, s32[1]{0:T(128)} %get-tuple-element.43.at_ref, bf16[8,128,128]{2,1,0:T(8,128)(2,1)S(1)} %collective-permute-done.1.r1_ref, bf16[8,128,128]{2,1,0:T(8,128)(2,1)S(1)} %get-tuple-element.52.b_ref), custom_call_target="tpu_custom_call" | custom-call | flops 1048576 | bytes 2097152 | tf_op jit(solution)/shard_map/cond/branch_1_fun/pallas_call | solution.py:138
  17.7 1.9 %collective-permute-start.4 = (bf16[8,128,128]{2,1,0:T(8,128)(2,1)S(1)}, bf16[8,128,128]{2,1,0:T(8,128)(2,1)S(1)}, u32[]{:S(2)}, u32[]{:S(2)}) collective-permute-start(bf16[8,128,128]{2,1,0:T(8,128)(2,1)S(1)} %branch_1_fun.13), channel_id=1, source_target_pairs={{0,4},{4,8},{8,12},{12,0},{1,5},{5,9},{9,13},{13,1},{2,6},{6,10},{... | collective-permute-start | bytes 786440 | tf_op jit(solution)/shard_map/cond/branch_1_fun/ppermute | solution.py:257
  19.6 0.8 %collective-permute-done.2.r2_ref = bf16[8,128,128]{2,1,0:T(8,128)(2,1)S(1)} collective-permute-done((bf16[8,128,128]{2,1,0:T(8,128)(2,1)S(1)}, bf16[8,128,128]{2,1,0:T(8,128)(2,1)S(1)}, u32[]{:S(2)}, u32[]{:S(2)}) %collective-permute-start.2) | collective-permute-done | bytes 262176 | tf_op jit(solution)/shard_map/cond/branch_1_fun/ppermute | solution.py:254
  20.3 0.6 %branch_1_fun.12 = bf16[8,128,128]{2,1,0:T(8,128)(2,1)S(1)} custom-call(s32[5]{0:T(128)S(1)} %copy-done.10, s32[1]{0:T(128)} %get-tuple-element.43.at_ref, bf16[8,128,128]{2,1,0:T(8,128)(2,1)S(1)} %collective-permute-done.2.r2_ref, bf16[8,128,128]{2,1,0:T(8,128)(2,1)S(1)} %get-tuple-element.52.b_ref), custom_call_target="tpu_custom_call" | custom-call | flops 1048576 | bytes 2097152 | tf_op jit(solution)/shard_map/cond/branch_1_fun/pallas_call | solution.py:138
  20.9 0.8 %collective-permute-start.3 = (bf16[8,128,128]{2,1,0:T(8,128)(2,1)S(1)}, bf16[8,128,128]{2,1,0:T(8,128)(2,1)S(1)}, u32[]{:S(2)}, u32[]{:S(2)}) collective-permute-start(bf16[8,128,128]{2,1,0:T(8,128)(2,1)S(1)} %branch_1_fun.12), channel_id=1, source_target_pairs={{0,2},{2,0},{1,3},{3,1},{4,6},{6,4},{5,7},{7,5},{8,10},{10,8},{9,1... | collective-permute-start | bytes 786440 | tf_op jit(solution)/shard_map/cond/branch_1_fun/ppermute | solution.py:259
  21.7 5.7 %collective-permute-done.4.r4_ref = bf16[8,128,128]{2,1,0:T(8,128)(2,1)S(1)} collective-permute-done((bf16[8,128,128]{2,1,0:T(8,128)(2,1)S(1)}, bf16[8,128,128]{2,1,0:T(8,128)(2,1)S(1)}, u32[]{:S(2)}, u32[]{:S(2)}) %collective-permute-start.4) | collective-permute-done | bytes 262176 | tf_op jit(solution)/shard_map/cond/branch_1_fun/ppermute | solution.py:257
  27.4 0.9 %collective-permute-done.3.r3_ref = bf16[8,128,128]{2,1,0:T(8,128)(2,1)S(1)} collective-permute-done((bf16[8,128,128]{2,1,0:T(8,128)(2,1)S(1)}, bf16[8,128,128]{2,1,0:T(8,128)(2,1)S(1)}, u32[]{:S(2)}, u32[]{:S(2)}) %collective-permute-start.3) | collective-permute-done | bytes 262176 | tf_op jit(solution)/shard_map/cond/branch_1_fun/ppermute | solution.py:259
  28.2 1.1 %branch_1_fun.14 = (bf16[16,128,128]{2,1,0:T(8,128)(2,1)S(1)}, bf16[16,128,128]{2,1,0:T(8,128)(2,1)S(1)}) custom-call(s32[5]{0:T(128)S(1)} %copy-done.10, s32[1]{0:T(128)} %get-tuple-element.43.at_ref, bf16[8,128,128]{2,1,0:T(8,128)(2,1)S(1)} %collective-permute-done.1.r1_ref, bf16[8,128,128]{2,1,0:T(8,128)(2,1)S(1)} %collective-permute-done.2.r2_ref, ...), custom_call_target="tpu_custom_call" | custom-call | flops 1048576 | bytes 2097152 | tf_op jit(solution)/shard_map/cond/branch_1_fun/pallas_call | solution.py:138
  29.3 0.0 copy-start.8
  29.3 0.1 collective-permute-start.5
  29.4 0.0 copy-done.5
  29.4 6.4 %branch_1_fun.8 = (f32[128,4096]{1,0:T(8,128)S(1)}, bf16[128,4096]{1,0:T(8,128)(2,1)S(1)}) custom-call(s32[5]{0:T(128)S(1)} %copy-done.10, s32[1]{0:T(128)} %get-tuple-element.43.at_ref, bf16[128,4096]{1,0:T(8,128)(2,1)S(1)} %copy-done.5, bf16[128,4096]{1,0:T(8,128)(2,1)S(1)} %copy-done.1, bf16[128,4096]{1,0:T(8,128)(2,1)S(1)} %copy-done.3), custom_call_target="tpu_custom_call" | custom-call | flops 268435456 | bytes 6291456 | tf_op jit(solution)/shard_map/cond/branch_1_fun/pallas_call | solution.py:170
  35.9 0.0 collective-permute-done.5.other_ref
  35.9 0.0 copy-done.8
  35.9 1.2 %branch_1_fun.15 = bf16[128,4096]{1,0:T(8,128)(2,1)S(1)} custom-call(s32[1]{0:T(128)S(6)} %select_n.51.off_ref, f32[128,4096]{1,0:T(8,128)S(1)} %get-tuple-element.48.loc_ref, bf16[128,4096]{1,0:T(8,128)(2,1)S(1)} %get-tuple-element.49.qm_ref, bf16[16,128,128]{2,1,0:T(8,128)(2,1)S(1)} %get-tuple-element.53.mine_ref, ...), custom_call_target="tpu_custom_call" | custom-call | flops 134217728 | bytes 6291456 | tf_op jit(solution)/shard_map/cond/branch_1_fun/pallas_call | solution.py:206
  37.1 0.0 copy-start.6
  37.1 1.0 %copy-done.6 = bf16[128,4096]{1,0:T(8,128)(2,1)} copy-done((bf16[128,4096]{1,0:T(8,128)(2,1)}, bf16[128,4096]{1,0:T(8,128)(2,1)S(1)}, u32[]{:S(2)}) %copy-start.6) | copy-done | bytes 1048600
Async XLA Ops:
  2.0 3.2 %copy-start.1 = (bf16[128,4096]{1,0:T(8,128)(2,1)S(1)}, bf16[128,4096]{1,0:T(8,128)(2,1)}, u32[]{:S(2)}) copy-start(bf16[128,4096]{1,0:T(8,128)(2,1)} %get-tuple-element.46.k_ref) | copy-start | bytes 3145732 | tf_op jit(solution)/shard_map/cond
  2.0 3.2 %copy-start.3 = (bf16[128,4096]{1,0:T(8,128)(2,1)S(1)}, bf16[128,4096]{1,0:T(8,128)(2,1)}, u32[]{:S(2)}) copy-start(bf16[128,4096]{1,0:T(8,128)(2,1)} %get-tuple-element.47.v_ref) | copy-start | bytes 3145732 | tf_op jit(solution)/shard_map/cond
  2.0 3.2 %copy-start.10 = (s32[5]{0:T(128)S(1)}, s32[5]{0:T(128)}, u32[]{:S(2)}) copy-start(s32[5]{0:T(128)} %get-tuple-element.44.len_ref) | copy-start | bytes 64 | tf_op jit(solution)/shard_map/cond
  4.6 2.1 %collective-permute-start = (bf16[16,128,128]{2,1,0:T(8,128)(2,1)S(1)}, bf16[16,128,128]{2,1,0:T(8,128)(2,1)S(1)}, u32[]{:S(2)}, u32[]{:S(2)}) collective-permute-start(bf16[16,128,128]{2,1,0:T(8,128)(2,1)S(1)} %branch_1_fun.10), channel_id=1, source_target_pairs={{0,1},{1,0},{2,3},{3,2},{4,5},{5,4},{6,7},{7,6},{8,9},{9,8},{10,11... | collective-permute-start | bytes 1572872 | tf_op jit(solution)/shard_map/cond/branch_1_fun/ppermute | solution.py:249
  7.5 21.9 %copy-start.5 = (bf16[128,4096]{1,0:T(8,128)(2,1)S(1)}, bf16[128,4096]{1,0:T(8,128)(2,1)}, u32[]{:S(2)}) copy-start(bf16[128,4096]{1,0:T(8,128)(2,1)} %get-tuple-element.45.q_ref) | copy-start | bytes 3145732 | tf_op jit(solution)/shard_map/cond
  7.5 9.5 %collective-permute-start.1 = (bf16[8,128,128]{2,1,0:T(8,128)(2,1)S(1)}, bf16[8,128,128]{2,1,0:T(8,128)(2,1)S(1)}, u32[]{:S(2)}, u32[]{:S(2)}) collective-permute-start(bf16[8,128,128]{2,1,0:T(8,128)(2,1)S(1)} %get-tuple-element.50), channel_id=1, source_target_pairs={{0,2},{2,0},{1,3},{3,1},{4,6},{6,4},{5,7},{7,5},{8,10},{10,8},{9,1... | collective-permute-start | bytes 786440 | tf_op jit(solution)/shard_map/cond/branch_1_fun/ppermute | solution.py:253
  10.4 9.9 %collective-permute-start.2 = (bf16[8,128,128]{2,1,0:T(8,128)(2,1)S(1)}, bf16[8,128,128]{2,1,0:T(8,128)(2,1)S(1)}, u32[]{:S(2)}, u32[]{:S(2)}) collective-permute-start(bf16[8,128,128]{2,1,0:T(8,128)(2,1)S(1)} %get-tuple-element.51), channel_id=1, source_target_pairs={{0,4},{4,8},{8,12},{12,0},{1,5},{5,9},{9,13},{13,1},{2,6},{6,10},{... | collective-permute-start | bytes 786440 | tf_op jit(solution)/shard_map/cond/branch_1_fun/ppermute | solution.py:254
  17.7 9.7 %collective-permute-start.4 = (bf16[8,128,128]{2,1,0:T(8,128)(2,1)S(1)}, bf16[8,128,128]{2,1,0:T(8,128)(2,1)S(1)}, u32[]{:S(2)}, u32[]{:S(2)}) collective-permute-start(bf16[8,128,128]{2,1,0:T(8,128)(2,1)S(1)} %branch_1_fun.13), channel_id=1, source_target_pairs={{0,4},{4,8},{8,12},{12,0},{1,5},{5,9},{9,13},{13,1},{2,6},{6,10},{... | collective-permute-start | bytes 786440 | tf_op jit(solution)/shard_map/cond/branch_1_fun/ppermute | solution.py:257
  20.9 7.3 %collective-permute-start.3 = (bf16[8,128,128]{2,1,0:T(8,128)(2,1)S(1)}, bf16[8,128,128]{2,1,0:T(8,128)(2,1)S(1)}, u32[]{:S(2)}, u32[]{:S(2)}) collective-permute-start(bf16[8,128,128]{2,1,0:T(8,128)(2,1)S(1)} %branch_1_fun.12), channel_id=1, source_target_pairs={{0,2},{2,0},{1,3},{3,1},{4,6},{6,4},{5,7},{7,5},{8,10},{10,8},{9,1... | collective-permute-start | bytes 786440 | tf_op jit(solution)/shard_map/cond/branch_1_fun/ppermute | solution.py:259
  29.3 6.6 %copy-start.8 = (f32[4096]{0:T(1024)S(1)}, f32[4096]{0:T(1024)}, u32[]{:S(2)}) copy-start(f32[4096]{0:T(1024)} %get-tuple-element.55) | copy-start | bytes 49156 | tf_op jit(solution)/shard_map/cond
  29.3 6.6 %collective-permute-start.5 = (bf16[16,128,128]{2,1,0:T(8,128)(2,1)S(1)}, bf16[16,128,128]{2,1,0:T(8,128)(2,1)S(1)}, u32[]{:S(2)}, u32[]{:S(2)}) collective-permute-start(bf16[16,128,128]{2,1,0:T(8,128)(2,1)S(1)} %get-tuple-element.54), channel_id=1, source_target_pairs={{0,1},{1,0},{2,3},{3,2},{4,5},{5,4},{6,7},{7,6},{8,9},{9,8},{10,11... | collective-permute-start | bytes 1572872 | tf_op jit(solution)/shard_map/cond/branch_1_fun/ppermute | solution.py:261
  37.1 1.0 %copy-start.6 = (bf16[128,4096]{1,0:T(8,128)(2,1)}, bf16[128,4096]{1,0:T(8,128)(2,1)S(1)}, u32[]{:S(2)}) copy-start(bf16[128,4096]{1,0:T(8,128)(2,1)S(1)} %get-tuple-element.82) | copy-start | bytes 3145732

commit v2 on v0

v2 whole, which is shorter than its diff:
```python
import functools
import jax
import jax.numpy as jnp
from jax import lax
from jax.experimental import pallas as pl
from jax.experimental.pallas import tpu as pltpu
from jax.sharding import PartitionSpec as P

DH = 128
F32, BF16 = jnp.float32, jnp.bfloat16
VMEM = pl.BlockSpec(memory_space=pltpu.VMEM)
SMEM = pl.BlockSpec(memory_space=pltpu.SMEM)
HBM = pl.BlockSpec(memory_space=pltpu.HBM)
PARAMS = pltpu.CompilerParams(vmem_limit_bytes=12 << 20)
W_OWN, W_GOT, W_NEXT, W_FAR, W_ON, IS_X1, IS_CORE1 = range(7)


def silu(x):
    half = x.astype(F32) * 0.5
    return half + half * jnp.tanh(half)


def doc_start(len_ref, position):
    start = jnp.zeros_like(position)
    end = jnp.int32(0)
    for doc in range(len_ref.shape[0]):
        end = end + len_ref[doc]
        start = jnp.where(position >= end, end, start)
    return start


def same_doc(len_ref, earlier, later):
    return doc_start(len_ref, later) <= earlier


def columns(start, heads):
    return pl.ds(pl.multiple_of(start, DH), heads * DH)


def cost(flops, nbytes, trans=0):
    return pl.CostEstimate(flops=flops, bytes_accessed=nbytes, transcendentals=trans)


def block_states(len_ref, at, k_ref, v_ref, t_ref, base, heads, ready=None):
    rows = k_ref.shape[0]
    first = at * rows
    keep = lax.broadcasted_iota(jnp.int32, (rows, DH), 0) >= doc_start(len_ref, first + rows - 1) - first
    for h in range(heads):
        if ready is not None:
            ready(h)
        cols = columns(base + h * DH, 1)
        k = jnp.where(keep, silu(k_ref[:, cols]), 0.0).astype(BF16)
        t = lax.dot_general(k, v_ref[:, cols], (((0,), (0,)), ((), ())), preferred_element_type=F32)
        t_ref[h] = t.astype(t_ref.dtype)


def state_kernel(offset, len_ref, at_ref, k_ref, v_ref, t_ref):
    at = at_ref[0]
    block_states(len_ref, at, k_ref, v_ref, t_ref, offset(at), t_ref.shape[0])


def opening_kernel(pieces, len_ref, at_ref, k_hbm, v_hbm, t_ref, w_ref, k_ref, v_ref, sems):
    at = at_ref[0]
    core, x = at % 2, (at // 2) % 2
    half, rows = t_ref.shape[0], k_ref.shape[0]
    theirs, mine = (1 - core) * half * DH, core * half * DH
    step = half // pieces
    copies = []
    for piece in range(pieces + 1):
        cols = columns(theirs + piece * step * DH, step) if piece < pieces else columns(mine, half)
        pairs = ((k_hbm, k_ref), (v_hbm, v_ref))
        copies.append([pltpu.make_async_copy(src.at[:, cols], dst.at[:, cols], sems.at[piece, n]) for n, (src, dst) in enumerate(pairs)])
        for copy in copies[-1]:
            copy.start()
    chip = (at - core) * rows
    whole = same_doc(len_ref, chip + rows - 1, chip + 2 * rows - 1)
    values = {
        W_OWN: (core == 1) | whole,
        W_GOT: (core == 0) | whole,
        W_NEXT: same_doc(len_ref, chip + 2 * rows - 1, chip + 4 * rows - 1),
        W_FAR: same_doc(len_ref, chip - 2 * rows - 1, chip - 1),
        W_ON: same_doc(len_ref, chip - 1, chip + rows - 1),
        IS_X1: x == 1,
        IS_CORE1: core == 1,
    }
    for row, value in values.items():
        w_ref[row : row + 1, :] = jnp.full((1, DH), jnp.where(value, 1.0, 0.0), F32)

    def ready(h):
        if h % step == 0:
            for copy in copies[h // step]:
                copy.wait()

    block_states(len_ref, at, k_ref, v_ref, t_ref, theirs, half, ready)
    for copy in copies[pieces]:
        copy.wait()


def opening(lens, at, k, v, half):
    pieces = 4 if half % 4 == 0 else 1
    rows = k.shape[0]
    vmem = jax.ShapeDtypeStruct(k.shape, BF16)
    return pl.pallas_call(
        functools.partial(opening_kernel, pieces),
        out_shape=[jax.ShapeDtypeStruct((half, DH, DH), BF16), jax.ShapeDtypeStruct((8, DH), F32), vmem, vmem],
        in_specs=[SMEM, SMEM, HBM, HBM],
        out_specs=[VMEM] * 4,
        scratch_shapes=[pltpu.SemaphoreType.DMA((pieces + 1, 2))],
        compiler_params=PARAMS,
        cost_estimate=cost(2 * half * rows * DH * DH, 4 * k.size, half * rows * DH),
    )(lens, at, k, v)


def states(lens, at, k, v, offset, heads, dtype):
    rows = k.shape[0]
    return pl.pallas_call(
        functools.partial(state_kernel, offset),
        out_shape=jax.ShapeDtypeStruct((heads, DH, DH), dtype),
        in_specs=[SMEM, SMEM, VMEM, VMEM],
        out_specs=VMEM,
        compiler_params=PARAMS,
        cost_estimate=cost(2 * heads * rows * DH * DH, heads * DH * (4 * rows + 2 * DH), heads * rows * DH),
    )(lens, at, k, v)


def weight(w_ref, row):
    return jnp.broadcast_to(w_ref[row : row + 1, :], (DH, DH)).astype(BF16)


def chip_kernel(w_ref, own_ref, got_ref, a_ref, b_ref):
    w_own, w_got = weight(w_ref, W_OWN), weight(w_ref, W_GOT)
    cut = a_ref.shape[0]
    for h in range(own_ref.shape[0]):
        s = own_ref[h] * w_own + got_ref[h] * w_got
        if h < cut:
            a_ref[h] = s
        else:
            b_ref[h - cut] = s


def relay_kernel(w_ref, a_ref, r2_ref, p3_ref):
    is_x1 = weight(w_ref, IS_X1)
    is_x0 = 1.0 - is_x1
    for h in range(p3_ref.shape[0]):
        p3_ref[h] = r2_ref[h] * is_x1 + a_ref[h] * is_x0


def carry_kernel(w_ref, b_ref, r1_ref, p4_ref):
    is_x1, w_next = weight(w_ref, IS_X1), weight(w_ref, W_NEXT)
    w_r = 1.0 - is_x1
    w_b = is_x1 + w_r * w_next
    for h in range(p4_ref.shape[0]):
        p4_ref[h] = b_ref[h] * w_b + r1_ref[h] * w_r


def join_kernel(start, first_row, near_ref, far_ref, w_ref, own_ref, got_ref, mine_ref, send_ref):
    w, on, is_x1, core1 = (weight(w_ref, row) for row in (W_FAR, W_ON, IS_X1, IS_CORE1))
    core0 = 1.0 - core1
    if first_row:
        w_near = None
    else:
        w_near = is_x1
        w = is_x1 * w + (1.0 - is_x1)
    m1, m2 = core1 * on + core0, core0 * on + core1
    for h in range(mine_ref.shape[0]):
        near = near_ref[h] if w_near is None else near_ref[h] * w_near
        p = near + far_ref[h] * w
        mine_ref[h] = p * m1 + got_ref[start + h] * core1
        send_ref[h] = p * m2 + own_ref[start + h] * core0


def small_call(kernel, ins, outs):
    many = len(outs) > 1
    shapes = [jax.ShapeDtypeStruct(s, BF16) for s in outs]
    return pl.pallas_call(
        kernel,
        out_shape=shapes if many else shapes[0],
        in_specs=[VMEM] * len(ins),
        out_specs=[VMEM] * len(outs) if many else VMEM,
        compiler_params=PARAMS,
        cost_estimate=cost(1 << 20, 1 << 20),
    )(*ins)


def local_kernel(offset, len_ref, at_ref, q_ref, k_ref, v_ref, loc_ref, qm_ref):
    rows = q_ref.shape[0]
    at = at_ref[0]
    first = at * rows
    i = first + lax.broadcasted_iota(jnp.int32, (rows, rows), 0)
    j = first + lax.broadcasted_iota(jnp.int32, (rows, rows), 1)
    start = doc_start(len_ref, i)
    allowed = (j <= i) & (j >= start)
    i_q = first + lax.broadcasted_iota(jnp.int32, (rows, DH), 0)
    joined = doc_start(len_ref, i_q) < first
    base = offset(at)
    for h in range(loc_ref.shape[1] // DH):
        cols, here = columns(base + h * DH, 1), slice(h * DH, (h + 1) * DH)
        q = silu(q_ref[:, cols])
        k = silu(k_ref[:, cols]).astype(BF16)
        qm_ref[:, here] = jnp.where(joined, q, 0.0).astype(BF16)
        s = lax.dot_general(q.astype(BF16), k, (((1,), (1,)), ((), ())), preferred_element_type=F32)
        s = jnp.where(allowed, s, 0.0).astype(BF16)
        loc_ref[:, here] = jnp.dot(s, v_ref[:, cols], preferred_element_type=F32)


def local_part(lens, at, q, k, v, offset, heads):
    rows = q.shape[0]
    width = heads * DH
    return pl.pallas_call(
        functools.partial(local_kernel, offset),
        out_shape=[jax.ShapeDtypeStruct((rows, width), F32), jax.ShapeDtypeStruct((rows, width), BF16)],
        in_specs=[SMEM, SMEM, VMEM, VMEM, VMEM],
        out_specs=[VMEM, VMEM],
        compiler_params=PARAMS,
        cost_estimate=cost(4 * rows * rows * width, 12 * rows * width, 2 * rows * width),
    )(lens, at, q, k, v)


def attend(loc_ref, qm_ref, p_refs, att_ref):
    total = jnp.zeros((att_ref.shape[0], DH), F32)
    h = 0
    for p_ref in p_refs:
        for n in range(p_ref.shape[0]):
            cols = slice(h * DH, (h + 1) * DH)
            att = loc_ref[:, cols] + jnp.dot(qm_ref[:, cols], p_ref[n], preferred_element_type=F32)
            att = att.astype(BF16)
            att_ref[:, cols] = att
            wide = att.astype(F32)
            total = total + wide * wide
            h += 1
    return total


def attend_any(far_ref, scanned_ref, start, loc_ref, qm_ref, p_refs, att_ref, sum_ref, scan_ref, sem):
    @pl.when(far_ref[0] == 0)
    def _():
        sum_ref[...] = attend(loc_ref, qm_ref, p_refs, att_ref)

    @pl.when(far_ref[0] != 0)
    def _():
        copy = pltpu.make_async_copy(scanned_ref.at[pl.ds(start, scan_ref.shape[0])], scan_ref, sem)
        copy.start()
        copy.wait()
        sum_ref[...] = attend(loc_ref, qm_ref, [scan_ref], att_ref)


def first_kernel(at_ref, far_ref, loc_ref, qm_ref, pa_ref, pb_ref, scanned_ref, att_ref, sum_ref, scan_ref, sem):
    start = at_ref[0] % 2 * scan_ref.shape[0]
    attend_any(far_ref, scanned_ref, start, loc_ref, qm_ref, [pa_ref, pb_ref], att_ref, sum_ref, scan_ref, sem)


def last_kernel(
    pieces, at_ref, far_ref, loc_ref, qm_ref, pa_ref, pb_ref, scanned_ref, att0_ref, sum0_ref, gain_ref,
    out_ref, att_ref, sum_ref, done_ref, scan_ref, sem, sems,
):
    half = scan_ref.shape[0]
    core = at_ref[0] % 2
    attend_any(far_ref, scanned_ref, (1 - core) * half, loc_ref, qm_ref, [pa_ref, pb_ref], att_ref, sum_ref, scan_ref, sem)
    width = 2 * half * DH
    total = jnp.sum(sum_ref[...] + sum0_ref[...], axis=1, keepdims=True)
    scale = lax.rsqrt(total / width + 1e-5)
    step = half // pieces
    copies = []
    for part, src in enumerate((att0_ref, att_ref)):
        base = jnp.where(core == part, 0, half * DH)
        for piece in range(pieces):
            for h in range(piece * step, (piece + 1) * step):
                cols = slice(h * DH, (h + 1) * DH)
                gain = gain_ref[:, columns(base + h * DH, 1)]
                done_ref[part, :, cols] = (src[:, cols].astype(F32) * scale * gain).astype(BF16)
            cols = slice(piece * step * DH, (piece + 1) * step * DH)
            there = columns(base + piece * step * DH, step)
            copies.append(pltpu.make_async_copy(done_ref.at[part, :, cols], out_ref.at[:, there], sems.at[part, piece]))
            copies[-1].start()
    for copy in copies:
        copy.wait()


def empty_kernel(out_ref):
    pass


def scan(lens, at, k, v):
    rows, width = k.shape
    blocks = lax.axis_size("ctx") * lax.axis_size("head")
    axes = ("ctx", "head")
    state = states(lens, at, k, v, lambda a: 0, width // DH, F32)
    me = at[0]
    ends = jnp.cumsum(lens)

    def segment(position):
        return jnp.where(position < 0, -1, jnp.sum((position >= ends).astype(jnp.int32)))

    hop = 1
    while hop < blocks:
        came = lax.ppermute(state, axes, [(b, b + hop) for b in range(blocks - hop)])
        adds = segment((me + 1) * rows - 1) == segment((me + 1 - hop) * rows - 1)
        state = state + jnp.where(adds, came, 0.0)
        hop *= 2
    return lax.ppermute(state, axes, [(b, b + 1) for b in range(blocks - 1)]).astype(BF16)


def finish_first(at, far, loc, qm, pa, pb, scanned):
    rows, width = loc.shape
    return pl.pallas_call(
        first_kernel,
        out_shape=[jax.ShapeDtypeStruct((rows, width), BF16), jax.ShapeDtypeStruct((rows, DH), F32)],
        in_specs=[SMEM, SMEM] + [VMEM] * 4 + [HBM],
        out_specs=[VMEM, VMEM],
        scratch_shapes=[pltpu.VMEM((width // DH, DH, DH), BF16), pltpu.SemaphoreType.DMA],
        compiler_params=PARAMS,
        cost_estimate=cost(2 * rows * DH * width, 10 * rows * width),
    )(at, far, loc, qm, pa, pb, scanned)


def finish_last(at, far, loc, qm, pa, pb, scanned, att, total, gain):
    rows, half_width = loc.shape
    half = half_width // DH
    pieces = 2 if half % 2 == 0 else 1
    return pl.pallas_call(
        functools.partial(last_kernel, pieces),
        out_shape=jax.ShapeDtypeStruct((rows, 2 * half_width), BF16),
        in_specs=[SMEM, SMEM] + [VMEM] * 4 + [HBM] + [VMEM] * 3,
        out_specs=HBM,
        scratch_shapes=[
            pltpu.VMEM((rows, half_width), BF16),
            pltpu.VMEM((rows, DH), F32),
            pltpu.VMEM((2, rows, half_width), BF16),
            pltpu.VMEM((half, DH, DH), BF16),
            pltpu.SemaphoreType.DMA,
            pltpu.SemaphoreType.DMA((2, pieces)),
        ],
        compiler_params=PARAMS,
        cost_estimate=cost(2 * rows * DH * half_width, 12 * rows * half_width),
    )(at, far, loc, qm, pa, pb, scanned, att, total, gain.reshape(1, 2 * half_width))


def general(lens, at, q, k, v, gain):
    half = q.shape[1] // (2 * DH)
    cut = half // 2
    far = jnp.ones((1,), jnp.int32)
    even = at * 2
    scanned = scan(lens, at, k, v)
    loc0, qm0 = local_part(lens, at, q, k, v, lambda a: 0, half)
    loc1, qm1 = local_part(lens, at, q, k, v, lambda a: half * DH, half)
    att, total = finish_first(even, far, loc0, qm0, scanned[:cut], scanned[cut:half], scanned)
    return finish_last(even, far, loc1, qm1, scanned[half : half + cut], scanned[half + cut :], scanned, att, total, gain)


def neighbours(lens, at, q, k, v, gain):
    rows, width = q.shape
    heads = width // DH
    half = heads // 2
    cut = half // 2
    ctx_parts, head_parts = lax.axis_size("ctx"), lax.axis_size("head")
    pair = [(0, 1), (1, 0), (2, 3), (3, 2)]
    across = [(0, 2), (2, 0), (1, 3), (3, 1)]
    onward = [(c, (c + 1) % ctx_parts) for c in range(ctx_parts)]
    chunk_a, chunk_b = (cut, DH, DH), (half - cut, DH, DH)

    def own_half(a):
        return a % 2 * half * DH

    def other_half(a):
        return (1 - a % 2) * half * DH

    theirs, w, k_in, v_in = opening(lens, at, k, v, half)
    got = lax.ppermute(theirs, "head", pair)
    own = states(lens, at, k_in, v_in, own_half, half, BF16)
    a, b = small_call(chip_kernel, [w, own, got], [chunk_a, chunk_b])
    r2 = lax.ppermute(a, "ctx", onward)
    r1 = lax.ppermute(b, "head", across)
    loc0, qm0 = local_part(lens, at, q, k_in, v_in, own_half, half)
    far = (jnp.max(lens) > rows * head_parts).astype(jnp.int32)
    scanned = lax.cond(
        far > 0,
        lambda: scan(lens, at, k, v),
        lambda: pl.pallas_call(empty_kernel, out_shape=jax.ShapeDtypeStruct((heads, DH, DH), BF16), out_specs=HBM)(),
    )
    far = far.reshape(1)
    r2, loc0, scanned = lax.optimization_barrier((r2, loc0, scanned))
    p3 = small_call(relay_kernel, [w, a, r2], [chunk_a])
    r3 = lax.ppermute(p3, "head", across)
    p4 = small_call(carry_kernel, [w, b, r1], [chunk_b])
    r4 = lax.ppermute(p4, "ctx", onward)
    loc1, qm1 = local_part(lens, at, q, k_in, v_in, other_half, half)
    r3, loc1 = lax.optimization_barrier((r3, loc1))
    mine_a, send_a = small_call(functools.partial(join_kernel, 0, True), [r3, r2, w, own, got], [chunk_a] * 2)
    other_a = lax.ppermute(send_a, "head", pair)
    mine_b, send_b = small_call(functools.partial(join_kernel, cut, False), [r1, r4, w, own, got], [chunk_b] * 2)
    other_b = lax.ppermute(send_b, "head", pair)
    att, total = finish_first(at, far, loc0, qm0, mine_a, mine_b, scanned)
    return finish_last(at, far, loc1, qm1, other_a, other_b, scanned, att, total, gain)


def per_device(queries, keys_in, values, doc_lengths, rms_gain):
    at = jnp.reshape(lax.axis_index(("ctx", "head")).astype(jnp.int32), (1,))
    plan = neighbours if lax.axis_size("head") == 4 else general
    return plan(doc_lengths, at, queries, keys_in, values, rms_gain)


def solution(mesh):
    return jax.shard_map(
        per_device,
        mesh=mesh,
        in_specs=(
            P(("groups", "ctx", "head"), None),
            P(("groups", "ctx", "head"), None),
            P(("groups", "ctx", "head"), None),
            P("groups"),
            P(),
        ),
        out_specs=P(("groups", "ctx", "head"), None),
        check_vma=False,
    )
```

time: 143 us -> 31.4 us (0.22)
  waiting for transfers between devices: 46.4 us -> 3.83 us
  blocking collectives: 30.2 us -> 0 us
  Pallas kernels: 0 us -> 16.3 us
  local copies, waits for them, and re-layouts: 17.5 us -> 1.23 us
  matrix products: 15.7 us -> 0 us
  between operations: 14.8 us -> 0.68 us
  other arithmetic: 6.28 us -> 0.62 us
  starting transfers between devices: 11.3 us -> 8.51 us
    all_gather x1 -> x0, waiting for transfers between devices: 23.4 us -> none  [per_device(): piece = lax.all_gather(tail[None], 'ctx', axis=0, tiled=True)]
    all_to_all x3 -> x0, waiting for transfers between devices: 23 us -> none  [the longest x1 12.1 us: per_device(): lax.all_to_all(values.reshape(split_shape), 'head', split_axis=1, concat_...]
    all_to_all x1 -> x0, blocking collectives: 17 us -> none  [per_device(): lax.all_to_all(attended[:, None], 'head', split_axis=0, concat_axis=1, ti...]
    pallas_call x0 -> x12, Pallas kernels: none -> 16.3 us  [the longest x2 6.26 us: local_part(): pl.pallas_call(functools.partial(local_kernel, offset), out_shape=[jax.Sh...]
    dot_general x4 -> x0, matrix products: 15.7 us -> none  [the longest x1 5.81 us: local_part(): jnp.einsum('hqk,khd->qhd', weights, v_shard[:last_row], preferred_element...]
    unnamed x1 -> x0, blocking collectives: 13.2 us -> none
    all_to_all x3 -> x0, starting transfers between devices: 11.2 us -> none  [the longest x1 4.21 us: per_device(): lax.all_to_all(values.reshape(split_shape), 'head', split_axis=1, concat_...]
    ppermute x0 -> x7, starting transfers between devices: none -> 8.51 us  [the longest x1 2.86 us: neighbours(): r1 = lax.ppermute(b, 'head', across)]
  transfers between devices with their start and end apart: 4 -> 7, of which waited for: 3 -> 5; matrix products, arithmetic and copies ran while one was open for 8% -> 2% of each run, Pallas kernels for 0% -> 35%
where the time goes in v2:
time: 31.4 us; the launch traced here: 31.2 us
  Pallas kernels  16.3 us (52%)
  starting transfers between devices  8.51 us (27%)
  waiting for transfers between devices  3.83 us (12%)
  local copies, waits for them, and re-layouts  1.23 us (4%)
  between operations  0.68 us (2%)
  other arithmetic  0.62 us (2%)
    pallas_call x2, Pallas kernels, local_part(): pl.pallas_call(functools.partial(local_kernel, offset), out_shape=[jax.Sh...  6.26 us
    pallas_call x5, Pallas kernels, small_call(): pl.pallas_call(kernel, out_shape=shapes if many else shapes[0], in_specs=...  4.3 us
    ppermute x1, starting transfers between devices, neighbours(): r1 = lax.ppermute(b, 'head', across)  2.86 us
    pallas_call x1, Pallas kernels, opening(): pl.pallas_call(functools.partial(opening_kernel, pieces), out_shape=[jax....  2.82 us
    ppermute x1, waiting for transfers between devices, neighbours(): r4 = lax.ppermute(p4, 'ctx', onward)  2.28 us
    ppermute x1, starting transfers between devices, neighbours(): r4 = lax.ppermute(p4, 'ctx', onward)  1.63 us
    ppermute x1, starting transfers between devices, neighbours(): r2 = lax.ppermute(a, 'ctx', onward)  1.58 us
    pallas_call x1, Pallas kernels, finish_last(): pl.pallas_call(functools.partial(last_kernel, pieces), out_shape=jax.Shap...  1.52 us
  transfers between devices with their start and end apart: 7, of which 5 were waited for; matrix products, arithmetic and copies ran while one was open for 2% of the time, Pallas kernels for 35%

profile of v2, /device:TPU:0, one launch (start us, length us, event | category | flops | bytes accessed | tf_op | source)
XLA Modules:
  0.0 31.2 jit_solution(15572833659465587255)
XLA Ops:
  0.0 0.0 copy-start.3
  0.0 2.8 %shard_map.55 = (bf16[16,128,128]{2,1,0:T(8,128)(2,1)S(1)}, f32[8,128]{1,0:T(8,128)S(1)}, bf16[128,4096]{1,0:T(8,128)(2,1)S(1)}, bf16[128,4096]{1,0:T(8,128)(2,1)S(1)}) custom-call(s32[5]{0:T(128)} %len_ref.7, s32[1]{0:T(128)} %bitcast.1.at_ref, bf16[128,4096]{1,0:T(8,128)(2,1)} %k_hbm.1, bf16[128,4096]{1,0:T(8,128)(2,1)} %v_hbm.1), custom_call_target="tpu_custom_call" | custom-call | flops 67108864 | bytes 2097152 | tf_op jit(solution)/shard_map/pallas_call | solution.py:103
  2.8 0.5 %collective-permute-start.5 = (bf16[16,128,128]{2,1,0:T(8,128)(2,1)S(1)}, bf16[16,128,128]{2,1,0:T(8,128)(2,1)S(1)}, u32[]{:S(2)}, u32[]{:S(2)}) collective-permute-start(bf16[16,128,128]{2,1,0:T(8,128)(2,1)S(1)} %get-tuple-element.47), channel_id=1, source_target_pairs={{0,1},{1,0},{2,3},{3,2},{4,5},{5,4},{6,7},{7,6},{8,9},{9,8},{10,11... | collective-permute-start | bytes 1572872 | tf_op jit(solution)/shard_map/ppermute | solution.py:368
  3.4 0.0 copy-done.3
  3.4 1.0 %shard_map.56.own_ref = bf16[16,128,128]{2,1,0:T(8,128)(2,1)S(1)} custom-call(s32[5]{0:T(128)S(1)} %copy-done.3, s32[1]{0:T(128)} %bitcast.1.at_ref, bf16[128,4096]{1,0:T(8,128)(2,1)S(1)} %get-tuple-element.45.k_ref, bf16[128,4096]{1,0:T(8,128)(2,1)S(1)} %get-tuple-element.46.v_ref), custom_call_target="tpu_custom_call" | custom-call | flops 67108864 | bytes 1572864 | tf_op jit(solution)/shard_map/pallas_call | solution.py:116
  4.4 0.5 %collective-permute-done.5.got_ref = bf16[16,128,128]{2,1,0:T(8,128)(2,1)S(1)} collective-permute-done((bf16[16,128,128]{2,1,0:T(8,128)(2,1)S(1)}, bf16[16,128,128]{2,1,0:T(8,128)(2,1)S(1)}, u32[]{:S(2)}, u32[]{:S(2)}) %collective-permute-start.5) | collective-permute-done | bytes 524320 | tf_op jit(solution)/shard_map/ppermute | solution.py:368
  4.9 0.9 %shard_map.57 = (bf16[8,128,128]{2,1,0:T(8,128)(2,1)}, bf16[8,128,128]{2,1,0:T(8,128)(2,1)}) custom-call(f32[8,128]{1,0:T(8,128)S(1)} %get-tuple-element.44.w_ref, bf16[16,128,128]{2,1,0:T(8,128)(2,1)S(1)} %shard_map.56.own_ref, bf16[16,128,128]{2,1,0:T(8,128)(2,1)S(1)} %collective-permute-done.5.got_ref), custom_call_target="tpu_custom_call" | custom-call | flops 1048576 | bytes 1048576 | tf_op jit(solution)/shard_map/pallas_call | solution.py:175
  5.8 2.9 %collective-permute-start.9 = (bf16[8,128,128]{2,1,0:T(8,128)(2,1)}, bf16[8,128,128]{2,1,0:T(8,128)(2,1)}, u32[]{:S(2)}, u32[]{:S(2)}) collective-permute-start(bf16[8,128,128]{2,1,0:T(8,128)(2,1)} %get-tuple-element.56.b_ref), channel_id=1, source_target_pairs={{0,2},{2,0},{1,3},{3,1},{4,6},{6,4},{5,7},{7,5},{8,10},{10,8},{9,1... | collective-permute-start | bytes 786440 | tf_op jit(solution)/shard_map/ppermute | solution.py:372
  8.6 1.6 %collective-permute-start.6 = (bf16[8,128,128]{2,1,0:T(8,128)(2,1)}, bf16[8,128,128]{2,1,0:T(8,128)(2,1)S(1)}, u32[]{:S(2)}, u32[]{:S(2)}) collective-permute-start(bf16[8,128,128]{2,1,0:T(8,128)(2,1)} %get-tuple-element.48.a_ref), channel_id=1, source_target_pairs={{0,4},{4,8},{8,12},{12,0},{1,5},{5,9},{9,13},{13,1},{2,6},{6,10},{... | collective-permute-start | bytes 786440 | tf_op jit(solution)/shard_map/ppermute | solution.py:371
  10.2 0.6 %reduce_max.9 = s32[]{:T(128)} reduce(s32[5]{0:T(128)S(1)} %copy-done.3, s32[]{:T(128)} %constant.43.clone.1), dimensions={0}, to_apply=%region_0.0 | reduce | flops 4 | bytes 28 | tf_op jit(solution)/shard_map/reduce_max | solution.py:374
  11.4 0.0 copy-start
  11.4 1.2 %copy-done = bf16[128,4096]{1,0:T(8,128)(2,1)S(1)} copy-done((bf16[128,4096]{1,0:T(8,128)(2,1)S(1)}, bf16[128,4096]{1,0:T(8,128)(2,1)}, u32[]{:S(2)}) %copy-start) | copy-done | bytes 1048600
  12.7 0.0 copy-start.1
  12.7 3.1 %shard_map.58 = (f32[128,2048]{1,0:T(8,128)S(1)}, bf16[128,2048]{1,0:T(8,128)(2,1)S(1)}) custom-call(s32[5]{0:T(128)S(1)} %copy-done.3, s32[1]{0:T(128)} %bitcast.1.at_ref, bf16[128,4096]{1,0:T(8,128)(2,1)S(1)} %copy-done, bf16[128,4096]{1,0:T(8,128)(2,1)S(1)} %get-tuple-element.45.k_ref, bf16[128,4096]{1,0:T(8,128)(2,1)S(1)} %get-tuple-element.46.v_ref), custom_call_target="tpu_custom_call" | custom-call | flops 134217728 | bytes 3145728 | tf_op jit(solution)/shard_map/pallas_call | solution.py:209
  15.8 0.0 collective-permute-done.9.r1_ref.near_ref
  15.8 1.1 %shard_map.62 = bf16[8,128,128]{2,1,0:T(8,128)(2,1)S(1)} custom-call(f32[8,128]{1,0:T(8,128)S(1)} %get-tuple-element.44.w_ref, bf16[8,128,128]{2,1,0:T(8,128)(2,1)} %get-tuple-element.56.b_ref, bf16[8,128,128]{2,1,0:T(8,128)(2,1)} %collective-permute-done.9.r1_ref.near_ref), custom_call_target="tpu_custom_call" | custom-call | flops 1048576 | bytes 1048576 | tf_op jit(solution)/shard_map/pallas_call | solution.py:175
  16.9 1.6 %collective-permute-start.10 = (bf16[8,128,128]{2,1,0:T(8,128)(2,1)S(1)}, bf16[8,128,128]{2,1,0:T(8,128)(2,1)S(1)}, u32[]{:S(2)}, u32[]{:S(2)}) collective-permute-start(bf16[8,128,128]{2,1,0:T(8,128)(2,1)S(1)} %shard_map.62), channel_id=1, source_target_pairs={{0,4},{4,8},{8,12},{12,0},{1,5},{5,9},{9,13},{13,1},{2,6},{6,10},{... | collective-permute-start | bytes 786440 | tf_op jit(solution)/shard_map/ppermute | solution.py:385
  18.5 0.2 collective-permute-done.6.r2_ref.far_ref
  18.8 1.0 %shard_map.59 = bf16[8,128,128]{2,1,0:T(8,128)(2,1)S(1)} custom-call(f32[8,128]{1,0:T(8,128)S(1)} %get-tuple-element.44.w_ref, bf16[8,128,128]{2,1,0:T(8,128)(2,1)} %get-tuple-element.48.a_ref, bf16[8,128,128]{2,1,0:T(8,128)(2,1)S(1)} %collective-permute-done.6.r2_ref.far_ref), custom_call_target="tpu_custom_call" | custom-call | flops 1048576 | bytes 1048576 | tf_op jit(solution)/shard_map/pallas_call | solution.py:175
  19.8 1.3 %collective-permute-start.7 = (bf16[8,128,128]{2,1,0:T(8,128)(2,1)S(1)}, bf16[8,128,128]{2,1,0:T(8,128)(2,1)S(1)}, u32[]{:S(2)}, u32[]{:S(2)}) collective-permute-start(bf16[8,128,128]{2,1,0:T(8,128)(2,1)S(1)} %shard_map.59), channel_id=1, source_target_pairs={{0,2},{2,0},{1,3},{3,1},{4,6},{6,4},{5,7},{7,5},{8,10},{10,8},{9,1... | collective-permute-start | bytes 786440 | tf_op jit(solution)/shard_map/ppermute | solution.py:383
  21.1 0.0 copy-done.1
  21.1 3.1 %shard_map.60 = (f32[128,2048]{1,0:T(8,128)S(1)}, bf16[128,2048]{1,0:T(8,128)(2,1)S(1)}) custom-call(s32[5]{0:T(128)S(1)} %copy-done.3, s32[1]{0:T(128)} %bitcast.1.at_ref, bf16[128,4096]{1,0:T(8,128)(2,1)S(1)} %copy-done.1, bf16[128,4096]{1,0:T(8,128)(2,1)S(1)} %get-tuple-element.45.k_ref, bf16[128,4096]{1,0:T(8,128)(2,1)S(1)} %get-tuple-element.46.v_ref), custom_call_target="tpu_custom_call" | custom-call | flops 134217728 | bytes 3145728 | tf_op jit(solution)/shard_map/pallas_call | solution.py:209
  24.3 2.3 %collective-permute-done.10.far_ref = bf16[8,128,128]{2,1,0:T(8,128)(2,1)S(1)} collective-permute-done((bf16[8,128,128]{2,1,0:T(8,128)(2,1)S(1)}, bf16[8,128,128]{2,1,0:T(8,128)(2,1)S(1)}, u32[]{:S(2)}, u32[]{:S(2)}) %collective-permute-start.10) | collective-permute-done | bytes 262176 | tf_op jit(solution)/shard_map/ppermute | solution.py:385
  26.5 1.1 %shard_map.63 = (bf16[8,128,128]{2,1,0:T(8,128)(2,1)S(1)}, bf16[8,128,128]{2,1,0:T(8,128)(2,1)S(1)}) custom-call(bf16[8,128,128]{2,1,0:T(8,128)(2,1)} %collective-permute-done.9.r1_ref.near_ref, bf16[8,128,128]{2,1,0:T(8,128)(2,1)S(1)} %collective-permute-done.10.far_ref, f32[8,128]{1,0:T(8,128)S(1)} %get-tuple-element.44.w_ref, ...), custom_call_target="tpu_custom_call" | custom-call | flops 1048576 | bytes 1048576 | tf_op jit(solution)/shard_map/pallas_call | solution.py:175
  27.7 0.1 collective-permute-start.11
  27.8 0.0 collective-permute-done.7.near_ref
  27.8 0.0 copy-start.2
  27.8 0.2 shard_map.61
  27.9 0.5 %collective-permute-start.8 = (bf16[8,128,128]{2,1,0:T(8,128)(2,1)S(1)}, bf16[8,128,128]{2,1,0:T(8,128)(2,1)S(1)}, u32[]{:S(2)}, u32[]{:S(2)}) collective-permute-start(bf16[8,128,128]{2,1,0:T(8,128)(2,1)S(1)} %get-tuple-element.55), channel_id=1, source_target_pairs={{0,1},{1,0},{2,3},{3,2},{4,5},{5,4},{6,7},{7,6},{8,9},{9,8},{10,11... | collective-permute-start | bytes 786440 | tf_op jit(solution)/shard_map/ppermute | solution.py:389
  28.5 0.3 %shard_map.64 = (bf16[128,2048]{1,0:T(8,128)(2,1)S(1)}, f32[128,128]{1,0:T(8,128)S(1)}) custom-call(s32[1]{0:T(128)} %bitcast.1.at_ref, s32[1]{0:T(128)} %bitcast.2.far_ref, f32[128,2048]{1,0:T(8,128)S(1)} %get-tuple-element.59.loc_ref, bf16[128,2048]{1,0:T(8,128)(2,1)S(1)} %get-tuple-element.60.qm_ref, bf16[8,128,128]{2,1,0:T(8,128)(2,1)S(1)} %get-tuple-element.61.pa_ref, ...), custom_call_target="tpu_custom_call" | custom-call | flops 67108864 | bytes 2621440 | tf_op jit(solution)/shard_map/pallas_call | solution.py:305
  28.8 0.5 %collective-permute-done.11.pb_ref = bf16[8,128,128]{2,1,0:T(8,128)(2,1)S(1)} collective-permute-done((bf16[8,128,128]{2,1,0:T(8,128)(2,1)S(1)}, bf16[8,128,128]{2,1,0:T(8,128)(2,1)S(1)}, u32[]{:S(2)}, u32[]{:S(2)}) %collective-permute-start.11) | collective-permute-done | bytes 262176 | tf_op jit(solution)/shard_map/ppermute | solution.py:391
  29.3 0.4 %collective-permute-done.8.pa_ref = bf16[8,128,128]{2,1,0:T(8,128)(2,1)S(1)} collective-permute-done((bf16[8,128,128]{2,1,0:T(8,128)(2,1)S(1)}, bf16[8,128,128]{2,1,0:T(8,128)(2,1)S(1)}, u32[]{:S(2)}, u32[]{:S(2)}) %collective-permute-start.8) | collective-permute-done | bytes 262176 | tf_op jit(solution)/shard_map/ppermute | solution.py:389
  29.7 0.0 copy-done.2
  29.7 1.5 %shard_map.65 = bf16[128,4096]{1,0:T(8,128)(2,1)} custom-call(s32[1]{0:T(128)} %bitcast.1.at_ref, s32[1]{0:T(128)} %bitcast.2.far_ref, f32[128,2048]{1,0:T(8,128)S(1)} %get-tuple-element.52.loc_ref, bf16[128,2048]{1,0:T(8,128)(2,1)S(1)} %get-tuple-element.53.qm_ref, bf16[8,128,128]{2,1,0:T(8,128)(2,1)S(1)} %collective-permute-done.8.pa_ref, ...), custom_call_target="tpu_custom_call" | custom-call | flops 67108864 | bytes 3145728 | tf_op jit(solution)/shard_map/pallas_call | solution.py:320
  (2 shorter events, 0.0 us)
Async XLA Ops:
  0.0 3.4 %copy-start.3 = (s32[5]{0:T(128)S(1)}, s32[5]{0:T(128)}, u32[]{:S(2)}) copy-start(s32[5]{0:T(128)} %len_ref.7) | copy-start | bytes 64
  2.8 2.1 %collective-permute-start.5 = (bf16[16,128,128]{2,1,0:T(8,128)(2,1)S(1)}, bf16[16,128,128]{2,1,0:T(8,128)(2,1)S(1)}, u32[]{:S(2)}, u32[]{:S(2)}) collective-permute-start(bf16[16,128,128]{2,1,0:T(8,128)(2,1)S(1)} %get-tuple-element.47), channel_id=1, source_target_pairs={{0,1},{1,0},{2,3},{3,2},{4,5},{5,4},{6,7},{7,6},{8,9},{9,8},{10,11... | collective-permute-start | bytes 1572872 | tf_op jit(solution)/shard_map/ppermute | solution.py:368
  5.8 10.0 %collective-permute-start.9 = (bf16[8,128,128]{2,1,0:T(8,128)(2,1)}, bf16[8,128,128]{2,1,0:T(8,128)(2,1)}, u32[]{:S(2)}, u32[]{:S(2)}) collective-permute-start(bf16[8,128,128]{2,1,0:T(8,128)(2,1)} %get-tuple-element.56.b_ref), channel_id=1, source_target_pairs={{0,2},{2,0},{1,3},{3,1},{4,6},{6,4},{5,7},{7,5},{8,10},{10,8},{9,1... | collective-permute-start | bytes 786440 | tf_op jit(solution)/shard_map/ppermute | solution.py:372
  8.6 10.1 %collective-permute-start.6 = (bf16[8,128,128]{2,1,0:T(8,128)(2,1)}, bf16[8,128,128]{2,1,0:T(8,128)(2,1)S(1)}, u32[]{:S(2)}, u32[]{:S(2)}) collective-permute-start(bf16[8,128,128]{2,1,0:T(8,128)(2,1)} %get-tuple-element.48.a_ref), channel_id=1, source_target_pairs={{0,4},{4,8},{8,12},{12,0},{1,5},{5,9},{9,13},{13,1},{2,6},{6,10},{... | collective-permute-start | bytes 786440 | tf_op jit(solution)/shard_map/ppermute | solution.py:371
  11.4 1.2 %copy-start = (bf16[128,4096]{1,0:T(8,128)(2,1)S(1)}, bf16[128,4096]{1,0:T(8,128)(2,1)}, u32[]{:S(2)}) copy-start(bf16[128,4096]{1,0:T(8,128)(2,1)} %q_ref.3) | copy-start | bytes 3145732
  12.7 8.5 %copy-start.1 = (bf16[128,4096]{1,0:T(8,128)(2,1)S(1)}, bf16[128,4096]{1,0:T(8,128)(2,1)}, u32[]{:S(2)}) copy-start(bf16[128,4096]{1,0:T(8,128)(2,1)} %q_ref.3) | copy-start | bytes 3145732
  16.9 9.6 %collective-permute-start.10 = (bf16[8,128,128]{2,1,0:T(8,128)(2,1)S(1)}, bf16[8,128,128]{2,1,0:T(8,128)(2,1)S(1)}, u32[]{:S(2)}, u32[]{:S(2)}) collective-permute-start(bf16[8,128,128]{2,1,0:T(8,128)(2,1)S(1)} %shard_map.62), channel_id=1, source_target_pairs={{0,4},{4,8},{8,12},{12,0},{1,5},{5,9},{9,13},{13,1},{2,6},{6,10},{... | collective-permute-start | bytes 786440 | tf_op jit(solution)/shard_map/ppermute | solution.py:385
  19.8 8.0 %collective-permute-start.7 = (bf16[8,128,128]{2,1,0:T(8,128)(2,1)S(1)}, bf16[8,128,128]{2,1,0:T(8,128)(2,1)S(1)}, u32[]{:S(2)}, u32[]{:S(2)}) collective-permute-start(bf16[8,128,128]{2,1,0:T(8,128)(2,1)S(1)} %shard_map.59), channel_id=1, source_target_pairs={{0,2},{2,0},{1,3},{3,1},{4,6},{6,4},{5,7},{7,5},{8,10},{10,8},{9,1... | collective-permute-start | bytes 786440 | tf_op jit(solution)/shard_map/ppermute | solution.py:383
  27.7 1.6 %collective-permute-start.11 = (bf16[8,128,128]{2,1,0:T(8,128)(2,1)S(1)}, bf16[8,128,128]{2,1,0:T(8,128)(2,1)S(1)}, u32[]{:S(2)}, u32[]{:S(2)}) collective-permute-start(bf16[8,128,128]{2,1,0:T(8,128)(2,1)S(1)} %get-tuple-element.57), channel_id=1, source_target_pairs={{0,1},{1,0},{2,3},{3,2},{4,5},{5,4},{6,7},{7,6},{8,9},{9,8},{10,11... | collective-permute-start | bytes 786440 | tf_op jit(solution)/shard_map/ppermute | solution.py:391
  27.8 1.9 %copy-start.2 = (f32[4096]{0:T(1024)S(1)}, f32[4096]{0:T(1024)}, u32[]{:S(2)}) copy-start(f32[4096]{0:T(1024)} %param.11) | copy-start | bytes 49156
  27.9 1.7 %collective-permute-start.8 = (bf16[8,128,128]{2,1,0:T(8,128)(2,1)S(1)}, bf16[8,128,128]{2,1,0:T(8,128)(2,1)S(1)}, u32[]{:S(2)}, u32[]{:S(2)}) collective-permute-start(bf16[8,128,128]{2,1,0:T(8,128)(2,1)S(1)} %get-tuple-element.55), channel_id=1, source_target_pairs={{0,1},{1,0},{2,3},{3,2},{4,5},{5,4},{6,7},{7,6},{8,9},{9,8},{10,11... | collective-permute-start | bytes 786440 | tf_op jit(solution)/shard_map/ppermute | solution.py:389

commit v3 on v2

v3 whole, which is shorter than its diff:
```python
import functools
import jax
import jax.numpy as jnp
from jax import lax
from jax.experimental import pallas as pl
from jax.experimental.pallas import tpu as pltpu
from jax.sharding import PartitionSpec as P

DH = 128
F32, BF16 = jnp.float32, jnp.bfloat16
VMEM = pl.BlockSpec(memory_space=pltpu.VMEM)
SMEM = pl.BlockSpec(memory_space=pltpu.SMEM)
HBM = pl.BlockSpec(memory_space=pltpu.HBM)
PARAMS = pltpu.CompilerParams(vmem_limit_bytes=12 << 20)
W_OWN, W_GOT, W_NEXT, W_FAR, W_ON, IS_X1, IS_CORE1 = range(7)
KEEP, ALLOWED, JOINED = range(3)
GROUP = 4


def in_hbm(x):
    return pltpu.with_memory_space_constraint(x, pltpu.HBM)


def silu(x):
    half = x.astype(F32) * 0.5
    return half + half * jnp.tanh(half)


def doc_start(len_ref, position):
    start = jnp.zeros_like(position)
    end = jnp.int32(0)
    for doc in range(len_ref.shape[0]):
        end = end + len_ref[doc]
        start = jnp.where(position >= end, end, start)
    return start


def same_doc(len_ref, earlier, later):
    return doc_start(len_ref, later) <= earlier


def columns(start, heads):
    return pl.ds(pl.multiple_of(start, DH), heads * DH)


def cost(flops, nbytes, trans=0):
    return pl.CostEstimate(flops=flops, bytes_accessed=nbytes, transcendentals=trans)


def make_masks(len_ref, at, rows):
    first = at * rows
    i = lax.broadcasted_iota(jnp.int32, (rows, DH), 0)
    keep = i >= doc_start(len_ref, first + rows - 1) - first
    start = doc_start(len_ref, first + i)
    joined = start < first
    i = lax.broadcasted_iota(jnp.int32, (rows, rows), 0)
    j = lax.broadcasted_iota(jnp.int32, (rows, rows), 1)
    allowed = (j <= i) & (j >= doc_start(len_ref, first + i) - first)
    return [jnp.where(mask, 1.0, 0.0).astype(BF16) for mask in (keep, allowed, joined)]


def block_states(keep, k_ref, v_ref, t_ref, base, heads, ready=None):
    for h0 in range(0, heads, GROUP):
        group = range(h0, min(h0 + GROUP, heads))
        sums = []
        for h in group:
            if ready is not None:
                ready(h)
            cols = columns(base + h * DH, 1)
            k = silu(k_ref[:, cols]).astype(BF16) * keep
            sums.append(lax.dot_general(k, v_ref[:, cols], (((0,), (0,)), ((), ())), preferred_element_type=F32))
        for h, t in zip(group, sums):
            t_ref[h] = t.astype(t_ref.dtype)


def own_kernel(offset, at_ref, m_ref, k_ref, v_ref, t_ref):
    block_states(m_ref[KEEP], k_ref, v_ref, t_ref, offset(at_ref[0]), t_ref.shape[0])


def opening_kernel(pieces, len_hbm, at_ref, k_hbm, v_hbm, t_ref, w_ref, m_ref, k_ref, v_ref, len_ref, sems, len_sem):
    at = at_ref[0]
    core, x = at % 2, (at // 2) % 2
    half, rows = t_ref.shape[0], k_ref.shape[0]
    len_copy = pltpu.make_async_copy(len_hbm, len_ref, len_sem)
    len_copy.start()
    theirs, mine = (1 - core) * half * DH, core * half * DH
    step = half // pieces
    copies = []
    for piece in range(pieces + 1):
        cols = columns(theirs + piece * step * DH, step) if piece < pieces else columns(mine, half)
        pairs = ((k_hbm, k_ref), (v_hbm, v_ref))
        copies.append([pltpu.make_async_copy(src.at[:, cols], dst.at[:, cols], sems.at[piece, n]) for n, (src, dst) in enumerate(pairs)])
        for copy in copies[-1]:
            copy.start()
    len_copy.wait()
    chip = (at - core) * rows
    whole = same_doc(len_ref, chip + rows - 1, chip + 2 * rows - 1)
    values = {
        W_OWN: (core == 1) | whole,
        W_GOT: (core == 0) | whole,
        W_NEXT: same_doc(len_ref, chip + 2 * rows - 1, chip + 4 * rows - 1),
        W_FAR: same_doc(len_ref, chip - 2 * rows - 1, chip - 1),
        W_ON: same_doc(len_ref, chip - 1, chip + rows - 1),
        IS_X1: x == 1,
        IS_CORE1: core == 1,
    }
    for row, value in values.items():
        w_ref[row : row + 1, :] = jnp.full((1, DH), jnp.where(value, 1.0, 0.0), F32)

    masks = make_masks(len_ref, at, rows)
    for n, mask in enumerate(masks):
        m_ref[n] = mask

    def ready(h):
        if h % step == 0:
            for copy in copies[h // step]:
                copy.wait()

    block_states(masks[KEEP], k_ref, v_ref, t_ref, theirs, half, ready)
    for copy in copies[pieces]:
        copy.wait()


def masks_kernel(rows, len_ref, at_ref, m_ref):
    for n, mask in enumerate(make_masks(len_ref, at_ref[0], rows)):
        m_ref[n] = mask


def masks_only(lens, at, rows):
    return pl.pallas_call(
        functools.partial(masks_kernel, rows),
        out_shape=jax.ShapeDtypeStruct((3, rows, DH), BF16),
        in_specs=[SMEM, SMEM],
        out_specs=VMEM,
        compiler_params=PARAMS,
        cost_estimate=cost(1 << 20, 6 * rows * DH),
    )(lens, at)


def opening(lens, at, k, v, half):
    pieces = 4 if half % 4 == 0 else 1
    rows = k.shape[0]
    vmem = jax.ShapeDtypeStruct(k.shape, BF16)
    return pl.pallas_call(
        functools.partial(opening_kernel, pieces),
        out_shape=[
            jax.ShapeDtypeStruct((half, DH, DH), BF16),
            jax.ShapeDtypeStruct((8, DH), F32),
            jax.ShapeDtypeStruct((3, rows, DH), BF16),
            vmem,
            vmem,
        ],
        in_specs=[HBM, SMEM, HBM, HBM],
        out_specs=[VMEM] * 5,
        scratch_shapes=[pltpu.SMEM(lens.shape, jnp.int32), pltpu.SemaphoreType.DMA((pieces + 1, 2)), pltpu.SemaphoreType.DMA],
        compiler_params=PARAMS,
        cost_estimate=cost(2 * half * rows * DH * DH, 4 * k.size, half * rows * DH),
    )(in_hbm(lens), at, in_hbm(k), in_hbm(v))


def states(at, masks, k, v, offset, heads, dtype):
    rows = k.shape[0]
    return pl.pallas_call(
        functools.partial(own_kernel, offset),
        out_shape=jax.ShapeDtypeStruct((heads, DH, DH), dtype),
        in_specs=[SMEM, VMEM, VMEM, VMEM],
        out_specs=VMEM,
        compiler_params=PARAMS,
        cost_estimate=cost(2 * heads * rows * DH * DH, heads * DH * (4 * rows + 2 * DH), heads * rows * DH),
    )(at, masks, k, v)


def weight(w_ref, row):
    return jnp.broadcast_to(w_ref[row : row + 1, :], (DH, DH)).astype(BF16)


def chip_kernel(w_ref, own_ref, got_ref, a_ref, b_ref):
    w_own, w_got = weight(w_ref, W_OWN), weight(w_ref, W_GOT)
    cut = a_ref.shape[0]
    for h in range(own_ref.shape[0]):
        s = own_ref[h] * w_own + got_ref[h] * w_got
        if h < cut:
            a_ref[h] = s
        else:
            b_ref[h - cut] = s


def relay_kernel(w_ref, a_ref, r2_ref, p3_ref):
    is_x1 = weight(w_ref, IS_X1)
    is_x0 = 1.0 - is_x1
    for h in range(p3_ref.shape[0]):
        p3_ref[h] = r2_ref[h] * is_x1 + a_ref[h] * is_x0


def carry_kernel(w_ref, b_ref, r1_ref, p4_ref):
    is_x1, w_next = weight(w_ref, IS_X1), weight(w_ref, W_NEXT)
    w_r = 1.0 - is_x1
    w_b = is_x1 + w_r * w_next
    for h in range(p4_ref.shape[0]):
        p4_ref[h] = b_ref[h] * w_b + r1_ref[h] * w_r


def join_kernel(start, first_row, near_ref, far_ref, w_ref, own_ref, got_ref, mine_ref, send_ref):
    w, on, is_x1, core1 = (weight(w_ref, row) for row in (W_FAR, W_ON, IS_X1, IS_CORE1))
    core0 = 1.0 - core1
    if first_row:
        w_near = None
    else:
        w_near = is_x1
        w = is_x1 * w + (1.0 - is_x1)
    m1, m2 = core1 * on + core0, core0 * on + core1
    for h in range(mine_ref.shape[0]):
        near = near_ref[h] if w_near is None else near_ref[h] * w_near
        p = near + far_ref[h] * w
        mine_ref[h] = p * m1 + got_ref[start + h] * core1
        send_ref[h] = p * m2 + own_ref[start + h] * core0


def small_call(kernel, ins, outs):
    many = len(outs) > 1
    shapes = [jax.ShapeDtypeStruct(s, BF16) for s in outs]
    return pl.pallas_call(
        kernel,
        out_shape=shapes if many else shapes[0],
        in_specs=[VMEM] * len(ins),
        out_specs=[VMEM] * len(outs) if many else VMEM,
        compiler_params=PARAMS,
        cost_estimate=cost(1 << 20, 1 << 20),
    )(*ins)


def local_kernel(offset, pieces, at_ref, m_ref, q_hbm, k_ref, v_ref, loc_ref, qm_ref, q_ref, sems):
    heads = loc_ref.shape[1] // DH
    base = offset(at_ref[0])
    step = heads // pieces
    copies = []
    for piece in range(pieces):
        here = slice(piece * step * DH, (piece + 1) * step * DH)
        copies.append(pltpu.make_async_copy(q_hbm.at[:, columns(base + piece * step * DH, step)], q_ref.at[:, here], sems.at[piece]))
        copies[-1].start()
    allowed, joined = m_ref[ALLOWED], m_ref[JOINED]
    for piece in range(pieces):
        copies[piece].wait()
        for h0 in range(piece * step, (piece + 1) * step, GROUP):
            group = range(h0, min(h0 + GROUP, (piece + 1) * step))
            queries, weights, sums = [], [], []
            for h in group:
                q = silu(q_ref[:, h * DH : (h + 1) * DH]).astype(BF16)
                k = silu(k_ref[:, columns(base + h * DH, 1)]).astype(BF16)
                s = lax.dot_general(q, k, (((1,), (1,)), ((), ())), preferred_element_type=F32)
                queries.append(q * joined)
                weights.append(s.astype(BF16) * allowed)
            for h, s in zip(group, weights):
                sums.append(jnp.dot(s, v_ref[:, columns(base + h * DH, 1)], preferred_element_type=F32))
            for n, h in enumerate(group):
                here = slice(h * DH, (h + 1) * DH)
                qm_ref[:, here] = queries[n]
                loc_ref[:, here] = sums[n]


def local_part(at, masks, q, k, v, offset, heads):
    rows = q.shape[0]
    width = heads * DH
    pieces = 4 if heads % 4 == 0 else 1
    return pl.pallas_call(
        functools.partial(local_kernel, offset, pieces),
        out_shape=[jax.ShapeDtypeStruct((rows, width), F32), jax.ShapeDtypeStruct((rows, width), BF16)],
        in_specs=[SMEM, VMEM, HBM, VMEM, VMEM],
        out_specs=[VMEM, VMEM],
        scratch_shapes=[pltpu.VMEM((rows, width), BF16), pltpu.SemaphoreType.DMA((pieces,))],
        compiler_params=PARAMS,
        cost_estimate=cost(4 * rows * rows * width, 12 * rows * width, 2 * rows * width),
    )(at, masks, in_hbm(q), k, v)


def attend(loc_ref, qm_ref, p_refs, att_ref):
    total = jnp.zeros((att_ref.shape[0], DH), F32)
    h = 0
    for p_ref in p_refs:
        for n in range(p_ref.shape[0]):
            cols = slice(h * DH, (h + 1) * DH)
            att = loc_ref[:, cols] + jnp.dot(qm_ref[:, cols], p_ref[n], preferred_element_type=F32)
            att = att.astype(BF16)
            att_ref[:, cols] = att
            wide = att.astype(F32)
            total = total + wide * wide
            h += 1
    return total


def first_kernel(loc_ref, qm_ref, pa_ref, pb_ref, att_ref, sum_ref):
    sum_ref[...] = attend(loc_ref, qm_ref, [pa_ref, pb_ref], att_ref)


def last_kernel(pieces, at_ref, loc_ref, qm_ref, pa_ref, pb_ref, att0_ref, sum0_ref, gain_ref, out_ref, att_ref, done_ref, sems):
    half = att_ref.shape[1] // DH
    core = at_ref[0] % 2
    total = attend(loc_ref, qm_ref, [pa_ref, pb_ref], att_ref) + sum0_ref[...]
    width = 2 * half * DH
    scale = lax.rsqrt(jnp.sum(total, axis=1, keepdims=True) / width + 1e-5)
    step = half // pieces
    copies = []
    for part, src in enumerate((att0_ref, att_ref)):
        base = jnp.where(core == part, 0, half * DH)
        for piece in range(pieces):
            for h in range(piece * step, (piece + 1) * step):
                cols = slice(h * DH, (h + 1) * DH)
                gain = gain_ref[:, columns(base + h * DH, 1)]
                done_ref[part, :, cols] = (src[:, cols].astype(F32) * scale * gain).astype(BF16)
            cols = slice(piece * step * DH, (piece + 1) * step * DH)
            there = columns(base + piece * step * DH, step)
            copies.append(pltpu.make_async_copy(done_ref.at[part, :, cols], out_ref.at[:, there], sems.at[part, piece]))
            copies[-1].start()
    for copy in copies:
        copy.wait()


def scan_kernel(rows, hop, len_ref, at_ref, state_ref, came_ref, out_ref):
    last = (at_ref[0] + 1) * rows - 1
    adds = (at_ref[0] >= hop) & same_doc(len_ref, last - hop * rows, last)
    out_ref[...] = state_ref[...] + jnp.where(adds, came_ref[...], 0.0)


def round_kernel(state_ref, out_ref):
    out_ref[...] = state_ref[...].astype(BF16)


def scan(lens, at, masks, k, v):
    rows, width = k.shape
    heads = width // DH
    blocks = lax.axis_size("ctx") * lax.axis_size("head")
    axes = ("ctx", "head")
    state = states(at, masks, k, v, lambda a: 0, heads, F32)
    spec = pl.BlockSpec((1, DH, DH), lambda h: (h, 0, 0))
    common = dict(grid=(heads,), out_specs=spec, compiler_params=PARAMS)
    hop = 1
    while hop < blocks:
        came = lax.ppermute(state, axes, [(b, b + hop) for b in range(blocks - hop)])
        state = pl.pallas_call(
            functools.partial(scan_kernel, rows, hop),
            out_shape=jax.ShapeDtypeStruct(state.shape, F32),
            in_specs=[SMEM, SMEM, spec, spec],
            **common,
        )(lens, at, state, came)
        hop *= 2
    state = pl.pallas_call(round_kernel, out_shape=jax.ShapeDtypeStruct(state.shape, BF16), in_specs=[spec], **common)(state)
    return lax.ppermute(state, axes, [(b, b + 1) for b in range(blocks - 1)])


def finish_first(loc, qm, pa, pb):
    rows, width = loc.shape
    return pl.pallas_call(
        first_kernel,
        out_shape=[jax.ShapeDtypeStruct((rows, width), BF16), jax.ShapeDtypeStruct((rows, DH), F32)],
        in_specs=[VMEM] * 4,
        out_specs=[VMEM, VMEM],
        compiler_params=PARAMS,
        cost_estimate=cost(2 * rows * DH * width, 10 * rows * width),
    )(loc, qm, pa, pb)


def finish_last(at, loc, qm, pa, pb, att, total, gain):
    rows, half_width = loc.shape
    pieces = 4 if half_width % (4 * DH) == 0 else 1
    return pl.pallas_call(
        functools.partial(last_kernel, pieces),
        out_shape=jax.ShapeDtypeStruct((rows, 2 * half_width), BF16),
        in_specs=[SMEM] + [VMEM] * 7,
        out_specs=HBM,
        scratch_shapes=[
            pltpu.VMEM((rows, half_width), BF16),
            pltpu.VMEM((2, rows, half_width), BF16),
            pltpu.SemaphoreType.DMA((2, pieces)),
        ],
        compiler_params=PARAMS,
        cost_estimate=cost(2 * rows * DH * half_width, 12 * rows * half_width),
    )(at, loc, qm, pa, pb, att, total, gain.reshape(1, 2 * half_width))


def general(lens, at, q, k, v, gain):
    half = q.shape[1] // (2 * DH)
    cut = half // 2
    masks = masks_only(lens, at, q.shape[0])
    before = scan(lens, at, masks, k, v)
    loc0, qm0 = local_part(at, masks, q, k, v, lambda a: 0, half)
    loc1, qm1 = local_part(at, masks, q, k, v, lambda a: half * DH, half)
    att, total = finish_first(loc0, qm0, before[:cut], before[cut:half])
    return finish_last(at * 2, loc1, qm1, before[half : half + cut], before[half + cut :], att, total, gain)


def neighbours(lens, at, q, k, v, gain):
    rows, width = q.shape
    heads = width // DH
    half = heads // 2
    cut = half // 2
    ctx_parts = lax.axis_size("ctx")
    pair = [(0, 1), (1, 0), (2, 3), (3, 2)]
    across = [(0, 2), (2, 0), (1, 3), (3, 1)]
    onward = [(c, c + 1) for c in range(ctx_parts - 1)]
    chunk_a, chunk_b = (cut, DH, DH), (half - cut, DH, DH)

    def own_half(a):
        return a % 2 * half * DH

    def other_half(a):
        return (1 - a % 2) * half * DH

    theirs, w, masks, k_in, v_in = opening(lens, at, k, v, half)
    got = lax.ppermute(theirs, "head", pair)
    own = states(at, masks, k_in, v_in, own_half, half, BF16)
    a, b = small_call(chip_kernel, [w, own, got], [chunk_a, chunk_b])
    r1 = lax.ppermute(b, "head", across)
    r2 = lax.ppermute(a, "ctx", onward)
    loc0, qm0 = local_part(at, masks, q, k_in, v_in, own_half, half)
    r1, loc0 = lax.optimization_barrier((r1, loc0))
    p4 = small_call(carry_kernel, [w, b, r1], [chunk_b])
    r4 = lax.ppermute(p4, "ctx", onward)
    p4, r2 = lax.optimization_barrier((p4, r2))
    p3 = small_call(relay_kernel, [w, a, r2], [chunk_a])
    r3 = lax.ppermute(p3, "head", across)
    loc1, qm1 = local_part(at, masks, q, k_in, v_in, other_half, half)
    r4, loc1 = lax.optimization_barrier((r4, loc1))
    mine_b, send_b = small_call(functools.partial(join_kernel, cut, False), [r1, r4, w, own, got], [chunk_b] * 2)
    other_b = lax.ppermute(send_b, "head", pair)
    r3, mine_b = lax.optimization_barrier((r3, mine_b))
    mine_a, send_a = small_call(functools.partial(join_kernel, 0, True), [r3, r2, w, own, got], [chunk_a] * 2)
    other_a = lax.ppermute(send_a, "head", pair)
    att, total = finish_first(loc0, qm0, mine_a, mine_b)
    return finish_last(at, loc1, qm1, other_a, other_b, att, total, gain)


def per_device(queries, keys_in, values, doc_lengths, rms_gain):
    at = jnp.reshape(lax.axis_index(("ctx", "head")).astype(jnp.int32), (1,))
    plan = neighbours if lax.axis_size("head") == 4 else general
    return plan(doc_lengths, at, queries, keys_in, values, rms_gain)


def solution(mesh):
    return jax.shard_map(
        per_device,
        mesh=mesh,
        in_specs=(
            P(("groups", "ctx", "head"), None),
            P(("groups", "ctx", "head"), None),
            P(("groups", "ctx", "head"), None),
            P("groups"),
            P(),
        ),
        out_specs=P(("groups", "ctx", "head"), None),
        check_vma=False,
    )
```

time: 31.4 us -> 29 us (0.924)
  Pallas kernels: 16.3 us -> 9.86 us
  starting transfers between devices: 8.51 us -> 12.8 us
  waiting for transfers between devices: 3.83 us -> 6.03 us
  local copies, waits for them, and re-layouts: 1.23 us -> 0.01 us
  other arithmetic: 0.62 us -> 0 us
  between operations: 0.68 us -> 0.1 us
    pallas_call x5, Pallas kernels: 4.3 us -> 0.59 us  [small_call(): pl.pallas_call(kernel, out_shape=shapes if many else shapes[0], in_specs=...]
    ppermute x1, waiting for transfers between devices: 0.01 us -> 2.21 us  [neighbours(): r3 = lax.ppermute(p3, 'head', across)]
    ppermute x1, starting transfers between devices: 1.63 us -> 3.74 us  [neighbours(): r4 = lax.ppermute(p4, 'ctx', onward)]
    pallas_call x4 -> x3, Pallas kernels: 7.31 us -> 5.23 us  [the longest x2 4.74 us: local_part(): pl.pallas_call(functools.partial(local_kernel, offset, pieces), out_shape...]
    ppermute x1, starting transfers between devices: 1.58 us -> 3.48 us  [neighbours(): r2 = lax.ppermute(a, 'ctx', onward)]
    ppermute x1, waiting for transfers between devices: 2.28 us -> 0.99 us  [neighbours(): r4 = lax.ppermute(p4, 'ctx', onward)]
    unnamed x8 -> x2, local copies, waits for them, and re-layouts: 1.23 us -> 0.01 us
    pallas_call x1, Pallas kernels: 2.82 us -> 2.03 us  [opening(): pl.pallas_call(functools.partial(opening_kernel, pieces), out_shape=[jax....]
  transfers between devices with their start and end apart: 7 -> 7, of which waited for: 5 -> 6; matrix products, arithmetic and copies ran while one was open for 2% -> 0% of each run, Pallas kernels for 35% -> 20%
where the time goes in v3:
time: 29 us; the launch traced here: 28.8 us
  starting transfers between devices  12.8 us (44%)
  Pallas kernels  9.86 us (34%)
  waiting for transfers between devices  6.03 us (21%)
    pallas_call x2, Pallas kernels, local_part(): pl.pallas_call(functools.partial(local_kernel, offset, pieces), out_shape...  4.74 us
    ppermute x1, starting transfers between devices, neighbours(): r4 = lax.ppermute(p4, 'ctx', onward)  3.74 us
    ppermute x1, starting transfers between devices, neighbours(): r2 = lax.ppermute(a, 'ctx', onward)  3.48 us
    ppermute x1, starting transfers between devices, neighbours(): r1 = lax.ppermute(b, 'head', across)  2.92 us
    ppermute x1, waiting for transfers between devices, neighbours(): r3 = lax.ppermute(p3, 'head', across)  2.21 us
    pallas_call x1, Pallas kernels, opening(): pl.pallas_call(functools.partial(opening_kernel, pieces), out_shape=[jax....  2.03 us
    pallas_call x1, Pallas kernels, finish_last(): pl.pallas_call(functools.partial(last_kernel, pieces), out_shape=jax.Shap...  1.69 us
    ppermute x1, starting transfers between devices, neighbours(): r3 = lax.ppermute(p3, 'head', across)  1.56 us
  transfers between devices with their start and end apart: 7, of which 6 were waited for; matrix products, arithmetic and copies ran while one was open for 0% of the time, Pallas kernels for 20%

profile of v3, /device:TPU:0, one launch (start us, length us, event | category | flops | bytes accessed | tf_op | source)
XLA Modules:
  0.0 28.8 jit_solution(17385337528510864424)
XLA Ops:
  0.0 2.0 %shard_map.55 = (bf16[16,128,128]{2,1,0:T(8,128)(2,1)S(1)}, f32[8,128]{1,0:T(8,128)S(1)}, bf16[3,128,128]{2,1,0:T(8,128)(2,1)S(1)}, bf16[128,4096]{1,0:T(8,128)(2,1)S(1)}, bf16[128,4096]{1,0:T(8,128)(2,1)S(1)}) custom-call(s32[5]{0:T(128)} %len_hbm.1, s32[1]{0:T(128)} %bitcast.at_ref, bf16[128,4096]{1,0:T(8,128)(2,1)} %k_hbm.1, bf16[128,4096]{1,0:T(8,128)(2,1)} %v_hbm.1), custom_call_target="tpu_custom_call" | custom-call | flops 67108864 | bytes 2097152 | tf_op jit(solution)/shard_map/pallas_call | solution.py:144
  2.0 0.5 %collective-permute-start = (bf16[16,128,128]{2,1,0:T(8,128)(2,1)S(1)}, bf16[16,128,128]{2,1,0:T(8,128)(2,1)S(1)}, u32[]{:S(2)}, u32[]{:S(2)}) collective-permute-start(bf16[16,128,128]{2,1,0:T(8,128)(2,1)S(1)} %get-tuple-element.33), channel_id=1, source_target_pairs={{0,1},{1,0},{2,3},{3,2},{4,5},{5,4},{6,7},{7,6},{8,9},{9,8},{10,11... | collective-permute-start | bytes 1572872 | tf_op jit(solution)/shard_map/ppermute | solution.py:409
  2.6 0.5 %shard_map.56.own_ref = bf16[16,128,128]{2,1,0:T(8,128)(2,1)S(1)} custom-call(s32[1]{0:T(128)} %bitcast.at_ref, bf16[3,128,128]{2,1,0:T(8,128)(2,1)S(1)} %get-tuple-element.30.m_ref, bf16[128,4096]{1,0:T(8,128)(2,1)S(1)} %get-tuple-element.31.k_ref, bf16[128,4096]{1,0:T(8,128)(2,1)S(1)} %get-tuple-element.32.v_ref), custom_call_target="tpu_custom_call" | custom-call | flops 67108864 | bytes 1572864 | tf_op jit(solution)/shard_map/pallas_call | solution.py:163
  3.1 1.0 %collective-permute-done.got_ref = bf16[16,128,128]{2,1,0:T(8,128)(2,1)S(1)} collective-permute-done((bf16[16,128,128]{2,1,0:T(8,128)(2,1)S(1)}, bf16[16,128,128]{2,1,0:T(8,128)(2,1)S(1)}, u32[]{:S(2)}, u32[]{:S(2)}) %collective-permute-start) | collective-permute-done | bytes 524320 | tf_op jit(solution)/shard_map/ppermute | solution.py:409
  4.1 0.1 shard_map.57
  4.2 2.9 %collective-permute-start.1 = (bf16[8,128,128]{2,1,0:T(8,128)(2,1)S(1)}, bf16[8,128,128]{2,1,0:T(8,128)(2,1)S(1)}, u32[]{:S(2)}, u32[]{:S(2)}) collective-permute-start(bf16[8,128,128]{2,1,0:T(8,128)(2,1)S(1)} %get-tuple-element.34.b_ref), channel_id=1, source_target_pairs={{0,2},{2,0},{1,3},{3,1},{4,6},{6,4},{5,7},{7,5},{8,10},{10,8},{9,1... | collective-permute-start | bytes 786440 | tf_op jit(solution)/shard_map/ppermute | solution.py:412
  7.1 3.5 %collective-permute-start.3 = (bf16[8,128,128]{2,1,0:T(8,128)(2,1)S(1)}, bf16[8,128,128]{2,1,0:T(8,128)(2,1)S(1)}, u32[]{:S(2)}, u32[]{:S(2)}) collective-permute-start(bf16[8,128,128]{2,1,0:T(8,128)(2,1)S(1)} %get-tuple-element.40.a_ref), channel_id=1, source_target_pairs={{0,4},{4,8},{8,12},{1,5},{5,9},{9,13},{2,6},{6,10},{10,14},{3,7},{... | collective-permute-start | bytes 786440 | tf_op jit(solution)/shard_map/ppermute | solution.py:413
  10.6 2.4 %shard_map.58 = (f32[128,2048]{1,0:T(8,128)S(1)}, bf16[128,2048]{1,0:T(8,128)(2,1)S(1)}) custom-call(s32[1]{0:T(128)} %bitcast.at_ref, bf16[3,128,128]{2,1,0:T(8,128)(2,1)S(1)} %get-tuple-element.30.m_ref, bf16[128,4096]{1,0:T(8,128)(2,1)} %q_hbm.3, bf16[128,4096]{1,0:T(8,128)(2,1)S(1)} %get-tuple-element.31.k_ref, bf16[128,4096]{1,0:T(8,128)(2,1)S(1)} %get-tuple-element.32.v_ref), custom_call_target="tpu_custom_call" | custom-call | flops 134217728 | bytes 3145728 | tf_op jit(solution)/shard_map/pallas_call | solution.py:265
  13.0 0.7 %collective-permute-done.1.r1_ref.near_ref = bf16[8,128,128]{2,1,0:T(8,128)(2,1)S(1)} collective-permute-done((bf16[8,128,128]{2,1,0:T(8,128)(2,1)S(1)}, bf16[8,128,128]{2,1,0:T(8,128)(2,1)S(1)}, u32[]{:S(2)}, u32[]{:S(2)}) %collective-permute-start.1) | collective-permute-done | bytes 262176 | tf_op jit(solution)/shard_map/ppermute | solution.py:412
  13.8 0.1 shard_map.59
  13.8 3.7 %collective-permute-start.2 = (bf16[8,128,128]{2,1,0:T(8,128)(2,1)S(1)}, bf16[8,128,128]{2,1,0:T(8,128)(2,1)S(1)}, u32[]{:S(2)}, u32[]{:S(2)}) collective-permute-start(bf16[8,128,128]{2,1,0:T(8,128)(2,1)S(1)} %shard_map.59), channel_id=1, source_target_pairs={{0,4},{4,8},{8,12},{1,5},{5,9},{9,13},{2,6},{6,10},{10,14},{3,7},{... | collective-permute-start | bytes 786440 | tf_op jit(solution)/shard_map/ppermute | solution.py:417
  17.6 0.0 collective-permute-done.3.r2_ref.far_ref
  17.6 0.1 shard_map.61
  17.7 1.6 %collective-permute-start.4 = (bf16[8,128,128]{2,1,0:T(8,128)(2,1)S(1)}, bf16[8,128,128]{2,1,0:T(8,128)(2,1)S(1)}, u32[]{:S(2)}, u32[]{:S(2)}) collective-permute-start(bf16[8,128,128]{2,1,0:T(8,128)(2,1)S(1)} %shard_map.61), channel_id=1, source_target_pairs={{0,2},{2,0},{1,3},{3,1},{4,6},{6,4},{5,7},{7,5},{8,10},{10,8},{9,1... | collective-permute-start | bytes 786440 | tf_op jit(solution)/shard_map/ppermute | solution.py:420
  19.2 2.4 %shard_map.60 = (f32[128,2048]{1,0:T(8,128)S(1)}, bf16[128,2048]{1,0:T(8,128)(2,1)S(1)}) custom-call(s32[1]{0:T(128)} %bitcast.at_ref, bf16[3,128,128]{2,1,0:T(8,128)(2,1)S(1)} %get-tuple-element.30.m_ref, bf16[128,4096]{1,0:T(8,128)(2,1)} %q_hbm.3, bf16[128,4096]{1,0:T(8,128)(2,1)S(1)} %get-tuple-element.31.k_ref, bf16[128,4096]{1,0:T(8,128)(2,1)S(1)} %get-tuple-element.32.v_ref), custom_call_target="tpu_custom_call" | custom-call | flops 134217728 | bytes 3145728 | tf_op jit(solution)/shard_map/pallas_call | solution.py:265
  21.6 1.0 %collective-permute-done.2.far_ref = bf16[8,128,128]{2,1,0:T(8,128)(2,1)S(1)} collective-permute-done((bf16[8,128,128]{2,1,0:T(8,128)(2,1)S(1)}, bf16[8,128,128]{2,1,0:T(8,128)(2,1)S(1)}, u32[]{:S(2)}, u32[]{:S(2)}) %collective-permute-start.2) | collective-permute-done | bytes 262176 | tf_op jit(solution)/shard_map/ppermute | solution.py:417
  22.6 0.2 shard_map.62
  22.8 2.2 %collective-permute-done.4.near_ref = bf16[8,128,128]{2,1,0:T(8,128)(2,1)S(1)} collective-permute-done((bf16[8,128,128]{2,1,0:T(8,128)(2,1)S(1)}, bf16[8,128,128]{2,1,0:T(8,128)(2,1)S(1)}, u32[]{:S(2)}, u32[]{:S(2)}) %collective-permute-start.4) | collective-permute-done | bytes 262176 | tf_op jit(solution)/shard_map/ppermute | solution.py:420
  25.0 0.2 shard_map.63
  25.1 0.1 collective-permute-start.5
  25.2 0.5 %collective-permute-start.6 = (bf16[8,128,128]{2,1,0:T(8,128)(2,1)S(1)}, bf16[8,128,128]{2,1,0:T(8,128)(2,1)S(1)}, u32[]{:S(2)}, u32[]{:S(2)}) collective-permute-start(bf16[8,128,128]{2,1,0:T(8,128)(2,1)S(1)} %get-tuple-element.46), channel_id=1, source_target_pairs={{0,1},{1,0},{2,3},{3,2},{4,5},{5,4},{6,7},{7,6},{8,9},{9,8},{10,11... | collective-permute-start | bytes 786440 | tf_op jit(solution)/shard_map/ppermute | solution.py:424
  25.7 0.0 copy-start
  25.7 0.3 %shard_map.64 = (bf16[128,2048]{1,0:T(8,128)(2,1)S(1)}, f32[128,128]{1,0:T(8,128)S(1)}) custom-call(f32[128,2048]{1,0:T(8,128)S(1)} %get-tuple-element.47.loc_ref, bf16[128,2048]{1,0:T(8,128)(2,1)S(1)} %get-tuple-element.48.qm_ref, bf16[8,128,128]{2,1,0:T(8,128)(2,1)S(1)} %get-tuple-element.49.pa_ref, bf16[8,128,128]{2,1,0:T(8,128)(2,1)S(1)} %get-tuple-element.50.pb_ref), custom_call_target="tpu_custom_call" | custom-call | flops 67108864 | bytes 2621440 | tf_op jit(solution)/shard_map/pallas_call | solution.py:352
  26.0 0.7 %collective-permute-done.5.pa_ref = bf16[8,128,128]{2,1,0:T(8,128)(2,1)S(1)} collective-permute-done((bf16[8,128,128]{2,1,0:T(8,128)(2,1)S(1)}, bf16[8,128,128]{2,1,0:T(8,128)(2,1)S(1)}, u32[]{:S(2)}, u32[]{:S(2)}) %collective-permute-start.5) | collective-permute-done | bytes 262176 | tf_op jit(solution)/shard_map/ppermute | solution.py:427
  26.7 0.4 %collective-permute-done.6.pb_ref = bf16[8,128,128]{2,1,0:T(8,128)(2,1)S(1)} collective-permute-done((bf16[8,128,128]{2,1,0:T(8,128)(2,1)S(1)}, bf16[8,128,128]{2,1,0:T(8,128)(2,1)S(1)}, u32[]{:S(2)}, u32[]{:S(2)}) %collective-permute-start.6) | collective-permute-done | bytes 262176 | tf_op jit(solution)/shard_map/ppermute | solution.py:424
  27.1 0.0 copy-done
  27.1 1.7 %shard_map.65 = bf16[128,4096]{1,0:T(8,128)(2,1)} custom-call(s32[1]{0:T(128)} %bitcast.at_ref, f32[128,2048]{1,0:T(8,128)S(1)} %get-tuple-element.38.loc_ref, bf16[128,2048]{1,0:T(8,128)(2,1)S(1)} %get-tuple-element.39.qm_ref, bf16[8,128,128]{2,1,0:T(8,128)(2,1)S(1)} %collective-permute-done.5.pa_ref, ...), custom_call_target="tpu_custom_call" | custom-call | flops 67108864 | bytes 3145728 | tf_op jit(solution)/shard_map/pallas_call | solution.py:365
Async XLA Ops:
  2.0 2.1 %collective-permute-start = (bf16[16,128,128]{2,1,0:T(8,128)(2,1)S(1)}, bf16[16,128,128]{2,1,0:T(8,128)(2,1)S(1)}, u32[]{:S(2)}, u32[]{:S(2)}) collective-permute-start(bf16[16,128,128]{2,1,0:T(8,128)(2,1)S(1)} %get-tuple-element.33), channel_id=1, source_target_pairs={{0,1},{1,0},{2,3},{3,2},{4,5},{5,4},{6,7},{7,6},{8,9},{9,8},{10,11... | collective-permute-start | bytes 1572872 | tf_op jit(solution)/shard_map/ppermute | solution.py:409
  4.2 9.5 %collective-permute-start.1 = (bf16[8,128,128]{2,1,0:T(8,128)(2,1)S(1)}, bf16[8,128,128]{2,1,0:T(8,128)(2,1)S(1)}, u32[]{:S(2)}, u32[]{:S(2)}) collective-permute-start(bf16[8,128,128]{2,1,0:T(8,128)(2,1)S(1)} %get-tuple-element.34.b_ref), channel_id=1, source_target_pairs={{0,2},{2,0},{1,3},{3,1},{4,6},{6,4},{5,7},{7,5},{8,10},{10,8},{9,1... | collective-permute-start | bytes 786440 | tf_op jit(solution)/shard_map/ppermute | solution.py:412
  7.1 10.4 %collective-permute-start.3 = (bf16[8,128,128]{2,1,0:T(8,128)(2,1)S(1)}, bf16[8,128,128]{2,1,0:T(8,128)(2,1)S(1)}, u32[]{:S(2)}, u32[]{:S(2)}) collective-permute-start(bf16[8,128,128]{2,1,0:T(8,128)(2,1)S(1)} %get-tuple-element.40.a_ref), channel_id=1, source_target_pairs={{0,4},{4,8},{8,12},{1,5},{5,9},{9,13},{2,6},{6,10},{10,14},{3,7},{... | collective-permute-start | bytes 786440 | tf_op jit(solution)/shard_map/ppermute | solution.py:413
  13.8 8.8 %collective-permute-start.2 = (bf16[8,128,128]{2,1,0:T(8,128)(2,1)S(1)}, bf16[8,128,128]{2,1,0:T(8,128)(2,1)S(1)}, u32[]{:S(2)}, u32[]{:S(2)}) collective-permute-start(bf16[8,128,128]{2,1,0:T(8,128)(2,1)S(1)} %shard_map.59), channel_id=1, source_target_pairs={{0,4},{4,8},{8,12},{1,5},{5,9},{9,13},{2,6},{6,10},{10,14},{3,7},{... | collective-permute-start | bytes 786440 | tf_op jit(solution)/shard_map/ppermute | solution.py:417
  17.7 7.3 %collective-permute-start.4 = (bf16[8,128,128]{2,1,0:T(8,128)(2,1)S(1)}, bf16[8,128,128]{2,1,0:T(8,128)(2,1)S(1)}, u32[]{:S(2)}, u32[]{:S(2)}) collective-permute-start(bf16[8,128,128]{2,1,0:T(8,128)(2,1)S(1)} %shard_map.61), channel_id=1, source_target_pairs={{0,2},{2,0},{1,3},{3,1},{4,6},{6,4},{5,7},{7,5},{8,10},{10,8},{9,1... | collective-permute-start | bytes 786440 | tf_op jit(solution)/shard_map/ppermute | solution.py:420
  25.1 1.6 %collective-permute-start.5 = (bf16[8,128,128]{2,1,0:T(8,128)(2,1)S(1)}, bf16[8,128,128]{2,1,0:T(8,128)(2,1)S(1)}, u32[]{:S(2)}, u32[]{:S(2)}) collective-permute-start(bf16[8,128,128]{2,1,0:T(8,128)(2,1)S(1)} %get-tuple-element.45), channel_id=1, source_target_pairs={{0,1},{1,0},{2,3},{3,2},{4,5},{5,4},{6,7},{7,6},{8,9},{9,8},{10,11... | collective-permute-start | bytes 786440 | tf_op jit(solution)/shard_map/ppermute | solution.py:427
  25.2 1.9 %collective-permute-start.6 = (bf16[8,128,128]{2,1,0:T(8,128)(2,1)S(1)}, bf16[8,128,128]{2,1,0:T(8,128)(2,1)S(1)}, u32[]{:S(2)}, u32[]{:S(2)}) collective-permute-start(bf16[8,128,128]{2,1,0:T(8,128)(2,1)S(1)} %get-tuple-element.46), channel_id=1, source_target_pairs={{0,1},{1,0},{2,3},{3,2},{4,5},{5,4},{6,7},{7,6},{8,9},{9,8},{10,11... | collective-permute-start | bytes 786440 | tf_op jit(solution)/shard_map/ppermute | solution.py:424
  25.7 1.4 %copy-start = (f32[4096]{0:T(1024)S(1)}, f32[4096]{0:T(1024)}, u32[]{:S(2)}) copy-start(f32[4096]{0:T(1024)} %param.9) | copy-start | bytes 49156

commit v4 on v3

--- a/solution.py
+++ b/solution.py
@@ -59,7 +59,9 @@
     return [jnp.where(mask, 1.0, 0.0).astype(BF16) for mask in (keep, allowed, joined)]
 
 
-def block_states(keep, k_ref, v_ref, t_ref, base, heads, ready=None):
+def block_states(keep, k_ref, v_ref, t_refs, base, ready=None):
+    slots = [t_ref.at[h] for t_ref in t_refs for h in range(t_ref.shape[0])]
+    heads = len(slots)
     for h0 in range(0, heads, GROUP):
         group = range(h0, min(h0 + GROUP, heads))
         sums = []
@@ -70,17 +72,17 @@
             k = silu(k_ref[:, cols]).astype(BF16) * keep
             sums.append(lax.dot_general(k, v_ref[:, cols], (((0,), (0,)), ((), ())), preferred_element_type=F32))
         for h, t in zip(group, sums):
-            t_ref[h] = t.astype(t_ref.dtype)
+            slots[h][...] = t.astype(slots[h].dtype)
 
 
 def own_kernel(offset, at_ref, m_ref, k_ref, v_ref, t_ref):
-    block_states(m_ref[KEEP], k_ref, v_ref, t_ref, offset(at_ref[0]), t_ref.shape[0])
-
-
-def opening_kernel(pieces, len_hbm, at_ref, k_hbm, v_hbm, t_ref, w_ref, m_ref, k_ref, v_ref, len_ref, sems, len_sem):
+    block_states(m_ref[KEEP], k_ref, v_ref, [t_ref], offset(at_ref[0]))
+
+
+def opening_kernel(pieces, len_hbm, at_ref, k_hbm, v_hbm, ta_ref, tb_ref, w_ref, m_ref, k_ref, v_ref, len_ref, sems, len_sem):
     at = at_ref[0]
     core, x = at % 2, (at // 2) % 2
-    half, rows = t_ref.shape[0], k_ref.shape[0]
+    half, rows = ta_ref.shape[0] + tb_ref.shape[0], k_ref.shape[0]
     len_copy = pltpu.make_async_copy(len_hbm, len_ref, len_sem)
     len_copy.start()
     theirs, mine = (1 - core) * half * DH, core * half * DH
@@ -116,7 +118,7 @@
             for copy in copies[h // step]:
                 copy.wait()
 
-    block_states(masks[KEEP], k_ref, v_ref, t_ref, theirs, half, ready)
+    block_states(masks[KEEP], k_ref, v_ref, [ta_ref, tb_ref], theirs, ready)
     for copy in copies[pieces]:
         copy.wait()
 
@@ -137,21 +139,22 @@
     )(lens, at)
 
 
-def opening(lens, at, k, v, half):
+def opening(lens, at, k, v, half, cut):
     pieces = 4 if half % 4 == 0 else 1
     rows = k.shape[0]
     vmem = jax.ShapeDtypeStruct(k.shape, BF16)
     return pl.pallas_call(
         functools.partial(opening_kernel, pieces),
         out_shape=[
-            jax.ShapeDtypeStruct((half, DH, DH), BF16),
+            jax.ShapeDtypeStruct((cut, DH, DH), BF16),
+            jax.ShapeDtypeStruct((half - cut, DH, DH), BF16),
             jax.ShapeDtypeStruct((8, DH), F32),
             jax.ShapeDtypeStruct((3, rows, DH), BF16),
             vmem,
             vmem,
         ],
         in_specs=[HBM, SMEM, HBM, HBM],
-        out_specs=[VMEM] * 5,
+        out_specs=[VMEM] * 6,
         scratch_shapes=[pltpu.SMEM(lens.shape, jnp.int32), pltpu.SemaphoreType.DMA((pieces + 1, 2)), pltpu.SemaphoreType.DMA],
         compiler_params=PARAMS,
         cost_estimate=cost(2 * half * rows * DH * DH, 4 * k.size, half * rows * DH),
@@ -174,15 +177,10 @@
     return jnp.broadcast_to(w_ref[row : row + 1, :], (DH, DH)).astype(BF16)
 
 
-def chip_kernel(w_ref, own_ref, got_ref, a_ref, b_ref):
+def chip_kernel(start, w_ref, own_ref, got_ref, chip_ref):
     w_own, w_got = weight(w_ref, W_OWN), weight(w_ref, W_GOT)
-    cut = a_ref.shape[0]
-    for h in range(own_ref.shape[0]):
-        s = own_ref[h] * w_own + got_ref[h] * w_got
-        if h < cut:
-            a_ref[h] = s
-        else:
-            b_ref[h - cut] = s
+    for h in range(chip_ref.shape[0]):
+        chip_ref[h] = own_ref[start + h] * w_own + got_ref[h] * w_got
 
 
 def relay_kernel(w_ref, a_ref, r2_ref, p3_ref):
@@ -212,7 +210,7 @@
     for h in range(mine_ref.shape[0]):
         near = near_ref[h] if w_near is None else near_ref[h] * w_near
         p = near + far_ref[h] * w
-        mine_ref[h] = p * m1 + got_ref[start + h] * core1
+        mine_ref[h] = p * m1 + got_ref[h] * core1
         send_ref[h] = p * m2 + own_ref[start + h] * core0
 
 
@@ -269,48 +267,55 @@
         out_specs=[VMEM, VMEM],
         scratch_shapes=[pltpu.VMEM((rows, width), BF16), pltpu.SemaphoreType.DMA((pieces,))],
         compiler_params=PARAMS,
-        cost_estimate=cost(4 * rows * rows * width, 12 * rows * width, 2 * rows * width),
+        cost_estimate=cost(0, 0),
     )(at, masks, in_hbm(q), k, v)
 
 
-def attend(loc_ref, qm_ref, p_refs, att_ref):
+def attend(loc_ref, qm_ref, p_ref, start, att_ref):
     total = jnp.zeros((att_ref.shape[0], DH), F32)
-    h = 0
-    for p_ref in p_refs:
-        for n in range(p_ref.shape[0]):
-            cols = slice(h * DH, (h + 1) * DH)
-            att = loc_ref[:, cols] + jnp.dot(qm_ref[:, cols], p_ref[n], preferred_element_type=F32)
-            att = att.astype(BF16)
-            att_ref[:, cols] = att
+    heads = p_ref.shape[0]
+    for h0 in range(0, heads, GROUP):
+        sums = []
+        group = range(h0, min(h0 + GROUP, heads))
+        for h in group:
+            cols = slice((start + h) * DH, (start + h + 1) * DH)
+            att = loc_ref[:, cols] + jnp.dot(qm_ref[:, cols], p_ref[h], preferred_element_type=F32)
+            sums.append(att.astype(BF16))
+        for h, att in zip(group, sums):
+            att_ref[:, h * DH : (h + 1) * DH] = att
             wide = att.astype(F32)
             total = total + wide * wide
-            h += 1
     return total
 
 
-def first_kernel(loc_ref, qm_ref, pa_ref, pb_ref, att_ref, sum_ref):
-    sum_ref[...] = attend(loc_ref, qm_ref, [pa_ref, pb_ref], att_ref)
-
-
-def last_kernel(pieces, at_ref, loc_ref, qm_ref, pa_ref, pb_ref, att0_ref, sum0_ref, gain_ref, out_ref, att_ref, done_ref, sems):
-    half = att_ref.shape[1] // DH
+def first_kernel(starts, *refs):
+    n = len(starts)
+    ins, outs = refs[: 3 * n], refs[3 * n :]
+    total = 0.0
+    for c, start in enumerate(starts):
+        total = total + attend(*ins[3 * c : 3 * c + 3], start, outs[c])
+    outs[n][...] = total
+
+
+def last_kernel(start, loc_ref, qm_ref, p_ref, at_ref, gain_ref, sum_ref, own_a_ref, own_b_ref, other_b_ref, out_ref, att_ref, done_ref, sems):
+    half = loc_ref.shape[1] // DH
+    cut = p_ref.shape[0]
     core = at_ref[0] % 2
-    total = attend(loc_ref, qm_ref, [pa_ref, pb_ref], att_ref) + sum0_ref[...]
+    total = attend(loc_ref, qm_ref, p_ref, start, att_ref) + sum_ref[...]
     width = 2 * half * DH
     scale = lax.rsqrt(jnp.sum(total, axis=1, keepdims=True) / width + 1e-5)
-    step = half // pieces
+    scale = jnp.broadcast_to(scale, (att_ref.shape[0], DH))
+    own, other = core * half * DH, (1 - core) * half * DH
     copies = []
-    for part, src in enumerate((att0_ref, att_ref)):
-        base = jnp.where(core == part, 0, half * DH)
-        for piece in range(pieces):
-            for h in range(piece * step, (piece + 1) * step):
-                cols = slice(h * DH, (h + 1) * DH)
-                gain = gain_ref[:, columns(base + h * DH, 1)]
-                done_ref[part, :, cols] = (src[:, cols].astype(F32) * scale * gain).astype(BF16)
-            cols = slice(piece * step * DH, (piece + 1) * step * DH)
-            there = columns(base + piece * step * DH, step)
-            copies.append(pltpu.make_async_copy(done_ref.at[part, :, cols], out_ref.at[:, there], sems.at[part, piece]))
-            copies[-1].start()
+    parts = ((own_a_ref, own), (own_b_ref, own + cut * DH), (other_b_ref, other + cut * DH), (att_ref, other))
+    for n, (src, base) in enumerate(parts):
+        heads = src.shape[1] // DH
+        for h in range(heads):
+            cols = slice(h * DH, (h + 1) * DH)
+            gain = gain_ref[:, columns(base + h * DH, 1)]
+            done_ref[n, :, cols] = (src[:, cols].astype(F32) * scale * gain).astype(BF16)
+        copies.append(pltpu.make_async_copy(done_ref.at[n, :, : heads * DH], out_ref.at[:, columns(base, heads)], sems.at[n]))
+        copies[-1].start()
     for copy in copies:
         copy.wait()
 
@@ -347,34 +352,37 @@
     return lax.ppermute(state, axes, [(b, b + 1) for b in range(blocks - 1)])
 
 
-def finish_first(loc, qm, pa, pb):
-    rows, width = loc.shape
-    return pl.pallas_call(
-        first_kernel,
-        out_shape=[jax.ShapeDtypeStruct((rows, width), BF16), jax.ShapeDtypeStruct((rows, DH), F32)],
-        in_specs=[VMEM] * 4,
-        out_specs=[VMEM, VMEM],
-        compiler_params=PARAMS,
-        cost_estimate=cost(2 * rows * DH * width, 10 * rows * width),
-    )(loc, qm, pa, pb)
-
-
-def finish_last(at, loc, qm, pa, pb, att, total, gain):
+def finish_first(chunks):
+    rows = chunks[0][0].shape[0]
+    ins = [x for chunk in chunks for x in chunk[:3]]
+    shapes = [jax.ShapeDtypeStruct((rows, chunk[2].shape[0] * DH), BF16) for chunk in chunks]
+    return pl.pallas_call(
+        functools.partial(first_kernel, tuple(chunk[3] for chunk in chunks)),
+        out_shape=shapes + [jax.ShapeDtypeStruct((rows, DH), F32)],
+        in_specs=[VMEM] * len(ins),
+        out_specs=[VMEM] * (len(shapes) + 1),
+        compiler_params=PARAMS,
+        cost_estimate=cost(2 * rows * DH * DH * 16, 1 << 21),
+    )(*ins)
+
+
+def finish_last(at, chunk, gain, own_a, own_b, other_b, total):
+    loc, qm, p, start = chunk
     rows, half_width = loc.shape
-    pieces = 4 if half_width % (4 * DH) == 0 else 1
-    return pl.pallas_call(
-        functools.partial(last_kernel, pieces),
+    widest = max(own_a.shape[1], own_b.shape[1])
+    return pl.pallas_call(
+        functools.partial(last_kernel, start),
         out_shape=jax.ShapeDtypeStruct((rows, 2 * half_width), BF16),
-        in_specs=[SMEM] + [VMEM] * 7,
+        in_specs=[VMEM] * 3 + [SMEM] + [VMEM] * 5,
         out_specs=HBM,
         scratch_shapes=[
-            pltpu.VMEM((rows, half_width), BF16),
-            pltpu.VMEM((2, rows, half_width), BF16),
-            pltpu.SemaphoreType.DMA((2, pieces)),
+            pltpu.VMEM((rows, p.shape[0] * DH), BF16),
+            pltpu.VMEM((4, rows, widest), BF16),
+            pltpu.SemaphoreType.DMA((4,)),
         ],
         compiler_params=PARAMS,
         cost_estimate=cost(2 * rows * DH * half_width, 12 * rows * half_width),
-    )(at, loc, qm, pa, pb, att, total, gain.reshape(1, 2 * half_width))
+    )(loc, qm, p, at, gain.reshape(1, 2 * half_width), total, own_a, own_b, other_b)
 
 
 def general(lens, at, q, k, v, gain):
@@ -384,8 +392,8 @@
     before = scan(lens, at, masks, k, v)
     loc0, qm0 = local_part(at, masks, q, k, v, lambda a: 0, half)
     loc1, qm1 = local_part(at, masks, q, k, v, lambda a: half * DH, half)
-    att, total = finish_first(loc0, qm0, before[:cut], before[cut:half])
-    return finish_last(at * 2, loc1, qm1, before[half : half + cut], before[half + cut :], att, total, gain)
+    first = finish_first([(loc0, qm0, before[:cut], 0), (loc0, qm0, before[cut:half], cut), (loc1, qm1, before[half + cut :], cut)])
+    return finish_last(at * 2, (loc1, qm1, before[half : half + cut], 0), gain, *first)
 
 
 def neighbours(lens, at, q, k, v, gain):
@@ -405,12 +413,15 @@
     def other_half(a):
         return (1 - a % 2) * half * DH
 
-    theirs, w, masks, k_in, v_in = opening(lens, at, k, v, half)
-    got = lax.ppermute(theirs, "head", pair)
+    theirs_a, theirs_b, w, masks, k_in, v_in = opening(lens, at, k, v, half, cut)
+    got_b = lax.ppermute(theirs_b, "head", pair)
+    got_a = lax.ppermute(theirs_a, "head", pair)
     own = states(at, masks, k_in, v_in, own_half, half, BF16)
-    a, b = small_call(chip_kernel, [w, own, got], [chunk_a, chunk_b])
+    b = small_call(functools.partial(chip_kernel, cut), [w, own, got_b], [chunk_b])
     r1 = lax.ppermute(b, "head", across)
+    a = small_call(functools.partial(chip_kernel, 0), [w, own, got_a], [chunk_a])
     r2 = lax.ppermute(a, "ctx", onward)
+    a, masks = lax.optimization_barrier((a, masks))
     loc0, qm0 = local_part(at, masks, q, k_in, v_in, own_half, half)
     r1, loc0 = lax.optimization_barrier((r1, loc0))
     p4 = small_call(carry_kernel, [w, b, r1], [chunk_b])
@@ -418,15 +429,16 @@
     p4, r2 = lax.optimization_barrier((p4, r2))
     p3 = small_call(relay_kernel, [w, a, r2], [chunk_a])
     r3 = lax.ppermute(p3, "head", across)
+    p3, masks = lax.optimization_barrier((p3, masks))
     loc1, qm1 = local_part(at, masks, q, k_in, v_in, other_half, half)
     r4, loc1 = lax.optimization_barrier((r4, loc1))
-    mine_b, send_b = small_call(functools.partial(join_kernel, cut, False), [r1, r4, w, own, got], [chunk_b] * 2)
+    mine_b, send_b = small_call(functools.partial(join_kernel, cut, False), [r1, r4, w, own, got_b], [chunk_b] * 2)
     other_b = lax.ppermute(send_b, "head", pair)
-    r3, mine_b = lax.optimization_barrier((r3, mine_b))
-    mine_a, send_a = small_call(functools.partial(join_kernel, 0, True), [r3, r2, w, own, got], [chunk_a] * 2)
+    r3, other_b = lax.optimization_barrier((r3, other_b))
+    mine_a, send_a = small_call(functools.partial(join_kernel, 0, True), [r3, r2, w, own, got_a], [chunk_a] * 2)
     other_a = lax.ppermute(send_a, "head", pair)
-    att, total = finish_first(loc0, qm0, mine_a, mine_b)
-    return finish_last(at, loc1, qm1, other_a, other_b, att, total, gain)
+    first = finish_first([(loc0, qm0, mine_a, 0), (loc0, qm0, mine_b, cut), (loc1, qm1, other_b, cut)])
+    return finish_last(at, (loc1, qm1, other_a, 0), gain, *first)
 
 
 def per_device(queries, keys_in, values, doc_lengths, rms_gain):

time: 29 us -> 28 us (0.966)
  waiting for transfers between devices: 6.03 us -> 5.43 us
  starting transfers between devices: 12.8 us -> 12.5 us
    ppermute x1 -> x2, waiting for transfers between devices: 1.03 us -> 0.58 us  [the longest x1 0.58 us: neighbours(): got_b = lax.ppermute(theirs_b, 'head', pair)]
    ppermute x1, starting transfers between devices: 0.5 us -> 0.07 us  [neighbours(): other_b = lax.ppermute(send_b, 'head', pair)]
    ppermute x1, waiting for transfers between devices: 0.69 us -> 1.07 us  [neighbours(): other_a = lax.ppermute(send_a, 'head', pair)]
    ppermute x1, waiting for transfers between devices: 0.37 us -> 0.01 us  [neighbours(): other_b = lax.ppermute(send_b, 'head', pair)]
    ppermute x1 -> x2, starting transfers between devices: 0.52 us -> 0.6 us  [the longest x1 0.52 us: neighbours(): got_b = lax.ppermute(theirs_b, 'head', pair)]
    pallas_call x5 -> x6, Pallas kernels: 0.59 us -> 0.59 us  [small_call(): pl.pallas_call(kernel, out_shape=shapes if many else shapes[0], in_specs=...]
  transfers between devices with their start and end apart: 7 -> 8, of which waited for: 6 -> 5; matrix products, arithmetic and copies ran while one was open for 0% -> 0% of each run, Pallas kernels for 20% -> 22%
where the time goes in v4:
time: 28 us; the launch traced here: 27.8 us
  starting transfers between devices  12.5 us (45%)
  Pallas kernels  9.79 us (35%)
  waiting for transfers between devices  5.43 us (19%)
    pallas_call x2, Pallas kernels, local_part(): pl.pallas_call(functools.partial(local_kernel, offset, pieces), out_shape...  4.74 us
    ppermute x1, starting transfers between devices, neighbours(): r4 = lax.ppermute(p4, 'ctx', onward)  3.74 us
    ppermute x1, starting transfers between devices, neighbours(): r2 = lax.ppermute(a, 'ctx', onward)  3.5 us
    ppermute x1, starting transfers between devices, neighbours(): r1 = lax.ppermute(b, 'head', across)  2.92 us
    ppermute x1, waiting for transfers between devices, neighbours(): r3 = lax.ppermute(p3, 'head', across)  2.13 us
    pallas_call x1, Pallas kernels, opening(): pl.pallas_call(functools.partial(opening_kernel, pieces), out_shape=[jax....  2.03 us
    ppermute x1, starting transfers between devices, neighbours(): r3 = lax.ppermute(p3, 'head', across)  1.56 us
    pallas_call x1, Pallas kernels, finish_last(): pl.pallas_call(functools.partial(last_kernel, start), out_shape=jax.Shape...  1.51 us
  transfers between devices with their start and end apart: 8, of which 5 were waited for; matrix products, arithmetic and copies ran while one was open for 0% of the time, Pallas kernels for 22%

profile of v4, /device:TPU:0, one launch (start us, length us, event | category | flops | bytes accessed | tf_op | source)
XLA Modules:
  0.0 27.8 jit_solution(8796409098865370553)
XLA Ops:
  0.0 2.0 %shard_map.55 = (bf16[8,128,128]{2,1,0:T(8,128)(2,1)S(1)}, bf16[8,128,128]{2,1,0:T(8,128)(2,1)S(1)}, f32[8,128]{1,0:T(8,128)S(1)}, bf16[3,128,128]{2,1,0:T(8,128...) custom-call(s32[5]{0:T(128)} %len_hbm.1, s32[1]{0:T(128)} %bitcast.at_ref, ...), custom_call_target="tpu_custom_call" | custom-call | flops 67108864 | bytes 2097152 | tf_op jit(solution)/shard_map/pallas_call | solution.py:146
  2.0 0.5 %collective-permute-start = (bf16[8,128,128]{2,1,0:T(8,128)(2,1)S(1)}, bf16[8,128,128]{2,1,0:T(8,128)(2,1)S(1)}, u32[]{:S(2)}, u32[]{:S(2)}) collective-permute-start(bf16[8,128,128]{2,1,0:T(8,128)(2,1)S(1)} %get-tuple-element.37), channel_id=1, source_target_pairs={{0,1},{1,0},{2,3},{3,2},{4,5},{5,4},{6,7},{7,6},{8,9},{9,8},{10,11... | collective-permute-start | bytes 786440 | tf_op jit(solution)/shard_map/ppermute | solution.py:417
  2.6 0.1 collective-permute-start.2
  2.6 0.5 %shard_map.56.own_ref = bf16[16,128,128]{2,1,0:T(8,128)(2,1)S(1)} custom-call(s32[1]{0:T(128)} %bitcast.at_ref, bf16[3,128,128]{2,1,0:T(8,128)(2,1)S(1)} %get-tuple-element.44.m_ref, bf16[128,4096]{1,0:T(8,128)(2,1)S(1)} %get-tuple-element.35.k_ref, bf16[128,4096]{1,0:T(8,128)(2,1)S(1)} %get-tuple-element.36.v_ref), custom_call_target="tpu_custom_call" | custom-call | flops 67108864 | bytes 1572864 | tf_op jit(solution)/shard_map/pallas_call | solution.py:166
  3.1 0.6 %collective-permute-done.got_ref = bf16[8,128,128]{2,1,0:T(8,128)(2,1)S(1)} collective-permute-done((bf16[8,128,128]{2,1,0:T(8,128)(2,1)S(1)}, bf16[8,128,128]{2,1,0:T(8,128)(2,1)S(1)}, u32[]{:S(2)}, u32[]{:S(2)}) %collective-permute-start) | collective-permute-done | bytes 262176 | tf_op jit(solution)/shard_map/ppermute | solution.py:417
  3.7 0.1 shard_map.57.b_ref
  3.8 2.9 %collective-permute-start.1 = (bf16[8,128,128]{2,1,0:T(8,128)(2,1)S(1)}, bf16[8,128,128]{2,1,0:T(8,128)(2,1)S(1)}, u32[]{:S(2)}, u32[]{:S(2)}) collective-permute-start(bf16[8,128,128]{2,1,0:T(8,128)(2,1)S(1)} %shard_map.57.b_ref), channel_id=1, source_target_pairs={{0,2},{2,0},{1,3},{3,1},{4,6},{6,4},{5,7},{7,5},{8,10},{10,8},{9,1... | collective-permute-start | bytes 786440 | tf_op jit(solution)/shard_map/ppermute | solution.py:421
  6.7 0.0 collective-permute-done.2.got_ref
  6.7 0.1 shard_map.58.a_ref
  6.8 3.5 %collective-permute-start.4 = (bf16[8,128,128]{2,1,0:T(8,128)(2,1)S(1)}, bf16[8,128,128]{2,1,0:T(8,128)(2,1)S(1)}, u32[]{:S(2)}, u32[]{:S(2)}) collective-permute-start(bf16[8,128,128]{2,1,0:T(8,128)(2,1)S(1)} %shard_map.58.a_ref), channel_id=1, source_target_pairs={{0,4},{4,8},{8,12},{1,5},{5,9},{9,13},{2,6},{6,10},{10,14},{3,7},{... | collective-permute-start | bytes 786440 | tf_op jit(solution)/shard_map/ppermute | solution.py:423
  10.3 2.4 %shard_map.59 = (f32[128,2048]{1,0:T(8,128)S(1)}, bf16[128,2048]{1,0:T(8,128)(2,1)S(1)}) custom-call(s32[1]{0:T(128)} %bitcast.at_ref, bf16[3,128,128]{2,1,0:T(8,128)(2,1)S(1)} %get-tuple-element.44.m_ref, bf16[128,4096]{1,0:T(8,128)(2,1)} %q_hbm.3, bf16[128,4096]{1,0:T(8,128)(2,1)S(1)} %get-tuple-element.35.k_ref, bf16[128,4096]{1,0:T(8,128)(2,1)S(1)} %get-tuple-element.36.v_ref), custom_call_target="tpu_custom_call" | custom-call | tf_op jit(solution)/shard_map/pallas_call | solution.py:263
  12.7 0.7 %collective-permute-done.1.r1_ref.near_ref = bf16[8,128,128]{2,1,0:T(8,128)(2,1)S(1)} collective-permute-done((bf16[8,128,128]{2,1,0:T(8,128)(2,1)S(1)}, bf16[8,128,128]{2,1,0:T(8,128)(2,1)S(1)}, u32[]{:S(2)}, u32[]{:S(2)}) %collective-permute-start.1) | collective-permute-done | bytes 262176 | tf_op jit(solution)/shard_map/ppermute | solution.py:421
  13.3 0.1 shard_map.60
  13.4 3.7 %collective-permute-start.3 = (bf16[8,128,128]{2,1,0:T(8,128)(2,1)S(1)}, bf16[8,128,128]{2,1,0:T(8,128)(2,1)S(1)}, u32[]{:S(2)}, u32[]{:S(2)}) collective-permute-start(bf16[8,128,128]{2,1,0:T(8,128)(2,1)S(1)} %shard_map.60), channel_id=1, source_target_pairs={{0,4},{4,8},{8,12},{1,5},{5,9},{9,13},{2,6},{6,10},{10,14},{3,7},{... | collective-permute-start | bytes 786440 | tf_op jit(solution)/shard_map/ppermute | solution.py:428
  17.1 0.0 collective-permute-done.4.r2_ref.far_ref
  17.2 0.1 shard_map.61
  17.2 1.6 %collective-permute-start.5 = (bf16[8,128,128]{2,1,0:T(8,128)(2,1)S(1)}, bf16[8,128,128]{2,1,0:T(8,128)(2,1)S(1)}, u32[]{:S(2)}, u32[]{:S(2)}) collective-permute-start(bf16[8,128,128]{2,1,0:T(8,128)(2,1)S(1)} %shard_map.61), channel_id=1, source_target_pairs={{0,2},{2,0},{1,3},{3,1},{4,6},{6,4},{5,7},{7,5},{8,10},{10,8},{9,1... | collective-permute-start | bytes 786440 | tf_op jit(solution)/shard_map/ppermute | solution.py:431
  18.8 2.4 %shard_map.62 = (f32[128,2048]{1,0:T(8,128)S(1)}, bf16[128,2048]{1,0:T(8,128)(2,1)S(1)}) custom-call(s32[1]{0:T(128)} %bitcast.at_ref, bf16[3,128,128]{2,1,0:T(8,128)(2,1)S(1)} %get-tuple-element.44.m_ref, bf16[128,4096]{1,0:T(8,128)(2,1)} %q_hbm.3, bf16[128,4096]{1,0:T(8,128)(2,1)S(1)} %get-tuple-element.35.k_ref, bf16[128,4096]{1,0:T(8,128)(2,1)S(1)} %get-tuple-element.36.v_ref), custom_call_target="tpu_custom_call" | custom-call | tf_op jit(solution)/shard_map/pallas_call | solution.py:263
  21.2 1.0 %collective-permute-done.3.far_ref = bf16[8,128,128]{2,1,0:T(8,128)(2,1)S(1)} collective-permute-done((bf16[8,128,128]{2,1,0:T(8,128)(2,1)S(1)}, bf16[8,128,128]{2,1,0:T(8,128)(2,1)S(1)}, u32[]{:S(2)}, u32[]{:S(2)}) %collective-permute-start.3) | collective-permute-done | bytes 262176 | tf_op jit(solution)/shard_map/ppermute | solution.py:428
  22.1 0.2 shard_map.63
  22.3 0.1 collective-permute-start.6
  22.4 2.1 %collective-permute-done.5.near_ref = bf16[8,128,128]{2,1,0:T(8,128)(2,1)S(1)} collective-permute-done((bf16[8,128,128]{2,1,0:T(8,128)(2,1)S(1)}, bf16[8,128,128]{2,1,0:T(8,128)(2,1)S(1)}, u32[]{:S(2)}, u32[]{:S(2)}) %collective-permute-start.5) | collective-permute-done | bytes 262176 | tf_op jit(solution)/shard_map/ppermute | solution.py:431
  24.5 0.0 collective-permute-done.6.refs_8_
  24.5 0.2 shard_map.64
  24.7 0.1 collective-permute-start.7
  24.8 0.0 copy-start
  24.8 0.4 %shard_map.65 = (bf16[128,1024]{1,0:T(8,128)(2,1)S(1)}, bf16[128,1024]{1,0:T(8,128)(2,1)S(1)}, bf16[128,1024]{1,0:T(8,128)(2,1)S(1)}, f32[128,128]{1,0:T(8,128)S(1)}) custom-call(f32[128,2048]{1,0:T(8,128)S(1)} %get-tuple-element.52.refs_0_.refs_3_, bf16[128,2048]{1,0:T(8,128)(2,1)S(1)} %get-tuple-element.53.refs_1_.refs_4_, ...), custom_call_target="tpu_custom_call" | custom-call | flops 67108864 | bytes 2097152 | tf_op jit(solution)/shard_map/pallas_call | solution.py:359
  25.2 1.1 %collective-permute-done.7.p_ref = bf16[8,128,128]{2,1,0:T(8,128)(2,1)S(1)} collective-permute-done((bf16[8,128,128]{2,1,0:T(8,128)(2,1)S(1)}, bf16[8,128,128]{2,1,0:T(8,128)(2,1)S(1)}, u32[]{:S(2)}, u32[]{:S(2)}) %collective-permute-start.7) | collective-permute-done | bytes 262176 | tf_op jit(solution)/shard_map/ppermute | solution.py:439
  26.3 0.0 copy-done
  26.3 1.5 %shard_map.66 = bf16[128,4096]{1,0:T(8,128)(2,1)} custom-call(f32[128,2048]{1,0:T(8,128)S(1)} %get-tuple-element.46.refs_6_.loc_ref, bf16[128,2048]{1,0:T(8,128)(2,1)S(1)} %get-tuple-element.47.refs_7_.qm_ref, bf16[8,128,128]{2,1,0:T(8,128)(2,1)S(1)} %collective-permute-done.7.p_ref, s32[1]{0:T(128)} %bitcast.at_ref, f32[1,4096]{1,0:T(1,128)S(1)} %bitcast.2, ...), custom_call_target="tpu_custom_call" | custom-call | flops 67108864 | bytes 3145728 | tf_op jit(solution)/shard_map/pallas_call | solution.py:373
Async XLA Ops:
  2.0 1.7 %collective-permute-start = (bf16[8,128,128]{2,1,0:T(8,128)(2,1)S(1)}, bf16[8,128,128]{2,1,0:T(8,128)(2,1)S(1)}, u32[]{:S(2)}, u32[]{:S(2)}) collective-permute-start(bf16[8,128,128]{2,1,0:T(8,128)(2,1)S(1)} %get-tuple-element.37), channel_id=1, source_target_pairs={{0,1},{1,0},{2,3},{3,2},{4,5},{5,4},{6,7},{7,6},{8,9},{9,8},{10,11... | collective-permute-start | bytes 786440 | tf_op jit(solution)/shard_map/ppermute | solution.py:417
  2.6 4.2 %collective-permute-start.2 = (bf16[8,128,128]{2,1,0:T(8,128)(2,1)S(1)}, bf16[8,128,128]{2,1,0:T(8,128)(2,1)S(1)}, u32[]{:S(2)}, u32[]{:S(2)}) collective-permute-start(bf16[8,128,128]{2,1,0:T(8,128)(2,1)S(1)} %get-tuple-element.38), channel_id=1, source_target_pairs={{0,1},{1,0},{2,3},{3,2},{4,5},{5,4},{6,7},{7,6},{8,9},{9,8},{10,11... | collective-permute-start | bytes 786440 | tf_op jit(solution)/shard_map/ppermute | solution.py:418
  3.8 9.5 %collective-permute-start.1 = (bf16[8,128,128]{2,1,0:T(8,128)(2,1)S(1)}, bf16[8,128,128]{2,1,0:T(8,128)(2,1)S(1)}, u32[]{:S(2)}, u32[]{:S(2)}) collective-permute-start(bf16[8,128,128]{2,1,0:T(8,128)(2,1)S(1)} %shard_map.57.b_ref), channel_id=1, source_target_pairs={{0,2},{2,0},{1,3},{3,1},{4,6},{6,4},{5,7},{7,5},{8,10},{10,8},{9,1... | collective-permute-start | bytes 786440 | tf_op jit(solution)/shard_map/ppermute | solution.py:421
  6.8 10.4 %collective-permute-start.4 = (bf16[8,128,128]{2,1,0:T(8,128)(2,1)S(1)}, bf16[8,128,128]{2,1,0:T(8,128)(2,1)S(1)}, u32[]{:S(2)}, u32[]{:S(2)}) collective-permute-start(bf16[8,128,128]{2,1,0:T(8,128)(2,1)S(1)} %shard_map.58.a_ref), channel_id=1, source_target_pairs={{0,4},{4,8},{8,12},{1,5},{5,9},{9,13},{2,6},{6,10},{10,14},{3,7},{... | collective-permute-start | bytes 786440 | tf_op jit(solution)/shard_map/ppermute | solution.py:423
  13.4 8.8 %collective-permute-start.3 = (bf16[8,128,128]{2,1,0:T(8,128)(2,1)S(1)}, bf16[8,128,128]{2,1,0:T(8,128)(2,1)S(1)}, u32[]{:S(2)}, u32[]{:S(2)}) collective-permute-start(bf16[8,128,128]{2,1,0:T(8,128)(2,1)S(1)} %shard_map.60), channel_id=1, source_target_pairs={{0,4},{4,8},{8,12},{1,5},{5,9},{9,13},{2,6},{6,10},{10,14},{3,7},{... | collective-permute-start | bytes 786440 | tf_op jit(solution)/shard_map/ppermute | solution.py:428
  17.2 7.3 %collective-permute-start.5 = (bf16[8,128,128]{2,1,0:T(8,128)(2,1)S(1)}, bf16[8,128,128]{2,1,0:T(8,128)(2,1)S(1)}, u32[]{:S(2)}, u32[]{:S(2)}) collective-permute-start(bf16[8,128,128]{2,1,0:T(8,128)(2,1)S(1)} %shard_map.61), channel_id=1, source_target_pairs={{0,2},{2,0},{1,3},{3,1},{4,6},{6,4},{5,7},{7,5},{8,10},{10,8},{9,1... | collective-permute-start | bytes 786440 | tf_op jit(solution)/shard_map/ppermute | solution.py:431
  22.3 2.2 %collective-permute-start.6 = (bf16[8,128,128]{2,1,0:T(8,128)(2,1)S(1)}, bf16[8,128,128]{2,1,0:T(8,128)(2,1)S(1)}, u32[]{:S(2)}, u32[]{:S(2)}) collective-permute-start(bf16[8,128,128]{2,1,0:T(8,128)(2,1)S(1)} %get-tuple-element.49), channel_id=1, source_target_pairs={{0,1},{1,0},{2,3},{3,2},{4,5},{5,4},{6,7},{7,6},{8,9},{9,8},{10,11... | collective-permute-start | bytes 786440 | tf_op jit(solution)/shard_map/ppermute | solution.py:436
  24.7 1.6 %collective-permute-start.7 = (bf16[8,128,128]{2,1,0:T(8,128)(2,1)S(1)}, bf16[8,128,128]{2,1,0:T(8,128)(2,1)S(1)}, u32[]{:S(2)}, u32[]{:S(2)}) collective-permute-start(bf16[8,128,128]{2,1,0:T(8,128)(2,1)S(1)} %get-tuple-element.51), channel_id=1, source_target_pairs={{0,1},{1,0},{2,3},{3,2},{4,5},{5,4},{6,7},{7,6},{8,9},{9,8},{10,11... | collective-permute-start | bytes 786440 | tf_op jit(solution)/shard_map/ppermute | solution.py:439
  24.8 1.5 %copy-start = (f32[4096]{0:T(1024)S(1)}, f32[4096]{0:T(1024)}, u32[]{:S(2)}) copy-start(f32[4096]{0:T(1024)} %param.9) | copy-start | bytes 49156

commit v5 on v4

--- a/solution.py
+++ b/solution.py
@@ -12,7 +12,7 @@
 SMEM = pl.BlockSpec(memory_space=pltpu.SMEM)
 HBM = pl.BlockSpec(memory_space=pltpu.HBM)
 PARAMS = pltpu.CompilerParams(vmem_limit_bytes=12 << 20)
-W_OWN, W_GOT, W_NEXT, W_FAR, W_ON, IS_X1, IS_CORE1 = range(7)
+W_OWN, W_GOT, W_NEXT, W_FAR, W_ON, IS_X1, IS_CORE1, IS_ODD = range(8)
 KEEP, ALLOWED, JOINED = range(3)
 GROUP = 4
 
@@ -79,19 +79,19 @@
     block_states(m_ref[KEEP], k_ref, v_ref, [t_ref], offset(at_ref[0]))
 
 
-def opening_kernel(pieces, len_hbm, at_ref, k_hbm, v_hbm, ta_ref, tb_ref, w_ref, m_ref, k_ref, v_ref, len_ref, sems, len_sem):
+def opening_kernel(start, pieces, len_hbm, at_ref, k_hbm, v_hbm, t_ref, w_ref, m_ref, k_ref, v_ref, len_ref, sems, len_sem):
     at = at_ref[0]
     core, x = at % 2, (at // 2) % 2
-    half, rows = ta_ref.shape[0] + tb_ref.shape[0], k_ref.shape[0]
+    heads, rows = t_ref.shape[0], k_ref.shape[0]
     len_copy = pltpu.make_async_copy(len_hbm, len_ref, len_sem)
     len_copy.start()
-    theirs, mine = (1 - core) * half * DH, core * half * DH
-    step = half // pieces
+    base = start(at)
+    step = heads // pieces
     copies = []
-    for piece in range(pieces + 1):
-        cols = columns(theirs + piece * step * DH, step) if piece < pieces else columns(mine, half)
+    for piece in range(pieces):
+        there, here = columns(base + piece * step * DH, step), slice(piece * step * DH, (piece + 1) * step * DH)
         pairs = ((k_hbm, k_ref), (v_hbm, v_ref))
-        copies.append([pltpu.make_async_copy(src.at[:, cols], dst.at[:, cols], sems.at[piece, n]) for n, (src, dst) in enumerate(pairs)])
+        copies.append([pltpu.make_async_copy(src.at[:, there], dst.at[:, here], sems.at[piece, n]) for n, (src, dst) in enumerate(pairs)])
         for copy in copies[-1]:
             copy.start()
     len_copy.wait()
@@ -105,10 +105,10 @@
         W_ON: same_doc(len_ref, chip - 1, chip + rows - 1),
         IS_X1: x == 1,
         IS_CORE1: core == 1,
+        IS_ODD: (at // 4) % 2 == 1,
     }
     for row, value in values.items():
         w_ref[row : row + 1, :] = jnp.full((1, DH), jnp.where(value, 1.0, 0.0), F32)
-
     masks = make_masks(len_ref, at, rows)
     for n, mask in enumerate(masks):
         m_ref[n] = mask
@@ -118,9 +118,7 @@
             for copy in copies[h // step]:
                 copy.wait()
 
-    block_states(masks[KEEP], k_ref, v_ref, [ta_ref, tb_ref], theirs, ready)
-    for copy in copies[pieces]:
-        copy.wait()
+    block_states(masks[KEEP], k_ref, v_ref, [t_ref], 0, ready)
 
 
 def masks_kernel(rows, len_ref, at_ref, m_ref):
@@ -139,26 +137,45 @@
     )(lens, at)
 
 
-def opening(lens, at, k, v, half, cut):
-    pieces = 4 if half % 4 == 0 else 1
+def opening(lens, at, k, v, start, heads):
+    pieces = 1
     rows = k.shape[0]
-    vmem = jax.ShapeDtypeStruct(k.shape, BF16)
-    return pl.pallas_call(
-        functools.partial(opening_kernel, pieces),
+    return pl.pallas_call(
+        functools.partial(opening_kernel, start, pieces),
         out_shape=[
-            jax.ShapeDtypeStruct((cut, DH, DH), BF16),
-            jax.ShapeDtypeStruct((half - cut, DH, DH), BF16),
+            jax.ShapeDtypeStruct((heads, DH, DH), BF16),
             jax.ShapeDtypeStruct((8, DH), F32),
             jax.ShapeDtypeStruct((3, rows, DH), BF16),
-            vmem,
-            vmem,
         ],
         in_specs=[HBM, SMEM, HBM, HBM],
-        out_specs=[VMEM] * 6,
-        scratch_shapes=[pltpu.SMEM(lens.shape, jnp.int32), pltpu.SemaphoreType.DMA((pieces + 1, 2)), pltpu.SemaphoreType.DMA],
-        compiler_params=PARAMS,
-        cost_estimate=cost(2 * half * rows * DH * DH, 4 * k.size, half * rows * DH),
+        out_specs=[VMEM] * 3,
+        scratch_shapes=[
+            pltpu.VMEM((rows, heads * DH), BF16),
+            pltpu.VMEM((rows, heads * DH), BF16),
+            pltpu.SMEM(lens.shape, jnp.int32),
+            pltpu.SemaphoreType.DMA((pieces, 2)),
+            pltpu.SemaphoreType.DMA,
+        ],
+        compiler_params=PARAMS,
+        cost_estimate=cost(2 * heads * rows * DH * DH, 4 * rows * heads * DH, heads * rows * DH),
     )(in_hbm(lens), at, in_hbm(k), in_hbm(v))
+
+
+def rest_kernel(half, at_ref, m_ref, k_ref, v_ref, ta_ref, own_ref):
+    core = at_ref[0] % 2
+    block_states(m_ref[KEEP], k_ref, v_ref, [own_ref], core * half * DH)
+    block_states(m_ref[KEEP], k_ref, v_ref, [ta_ref], (1 - core) * half * DH)
+
+
+def rest_states(at, masks, k, v, half, cut):
+    return pl.pallas_call(
+        functools.partial(rest_kernel, half),
+        out_shape=[jax.ShapeDtypeStruct((cut, DH, DH), BF16), jax.ShapeDtypeStruct((half, DH, DH), BF16)],
+        in_specs=[SMEM, VMEM, VMEM, VMEM],
+        out_specs=[VMEM, VMEM],
+        compiler_params=PARAMS,
+        cost_estimate=cost(0, 0),
+    )(at, masks, k, v)
 
 
 def states(at, masks, k, v, offset, heads, dtype):
@@ -183,11 +200,18 @@
         chip_ref[h] = own_ref[start + h] * w_own + got_ref[h] * w_got
 
 
-def relay_kernel(w_ref, a_ref, r2_ref, p3_ref):
+def came(w_ref, odd_ref, even_ref, h):
+    odd = weight(w_ref, IS_ODD)
+    return odd_ref[h] * odd + even_ref[h] * (1.0 - odd)
+
+
+def relay_kernel(w_ref, a_ref, odd_ref, even_ref, p3_ref, r2_ref):
     is_x1 = weight(w_ref, IS_X1)
     is_x0 = 1.0 - is_x1
     for h in range(p3_ref.shape[0]):
-        p3_ref[h] = r2_ref[h] * is_x1 + a_ref[h] * is_x0
+        r2 = came(w_ref, odd_ref, even_ref, h)
+        r2_ref[h] = r2
+        p3_ref[h] = r2 * is_x1 + a_ref[h] * is_x0
 
 
 def carry_kernel(w_ref, b_ref, r1_ref, p4_ref):
@@ -198,20 +222,25 @@
         p4_ref[h] = b_ref[h] * w_b + r1_ref[h] * w_r
 
 
-def join_kernel(start, first_row, near_ref, far_ref, w_ref, own_ref, got_ref, mine_ref, send_ref):
-    w, on, is_x1, core1 = (weight(w_ref, row) for row in (W_FAR, W_ON, IS_X1, IS_CORE1))
+def join(w_ref, p, own, got, mine_ref, send_ref, h):
+    on, core1 = weight(w_ref, W_ON), weight(w_ref, IS_CORE1)
     core0 = 1.0 - core1
-    if first_row:
-        w_near = None
-    else:
-        w_near = is_x1
-        w = is_x1 * w + (1.0 - is_x1)
-    m1, m2 = core1 * on + core0, core0 * on + core1
+    mine_ref[h] = p * (core1 * on + core0) + got * core1
+    send_ref[h] = p * (core0 * on + core1) + own * core0
+
+
+def join_a_kernel(w_ref, r3_ref, r2_ref, own_ref, got_ref, mine_ref, send_ref):
+    far = weight(w_ref, W_FAR)
     for h in range(mine_ref.shape[0]):
-        near = near_ref[h] if w_near is None else near_ref[h] * w_near
-        p = near + far_ref[h] * w
-        mine_ref[h] = p * m1 + got_ref[h] * core1
-        send_ref[h] = p * m2 + own_ref[start + h] * core0
+        join(w_ref, r3_ref[h] + r2_ref[h] * far, own_ref[h], got_ref[h], mine_ref, send_ref, h)
+
+
+def join_b_kernel(start, w_ref, r1_ref, odd_ref, even_ref, own_ref, got_ref, mine_ref, send_ref):
+    is_x1 = weight(w_ref, IS_X1)
+    far = is_x1 * weight(w_ref, W_FAR) + (1.0 - is_x1)
+    for h in range(mine_ref.shape[0]):
+        p = r1_ref[h] * is_x1 + came(w_ref, odd_ref, even_ref, h) * far
+        join(w_ref, p, own_ref[start + h], got_ref[h], mine_ref, send_ref, h)
 
 
 def small_call(kernel, ins, outs):
@@ -271,8 +300,8 @@
     )(at, masks, in_hbm(q), k, v)
 
 
-def attend(loc_ref, qm_ref, p_ref, start, att_ref):
-    total = jnp.zeros((att_ref.shape[0], DH), F32)
+def attend(loc_ref, qm_ref, p_ref, start, gain_ref, base, out_ref):
+    total = jnp.zeros((out_ref.shape[0], DH), F32)
     heads = p_ref.shape[0]
     for h0 in range(0, heads, GROUP):
         sums = []
@@ -280,41 +309,41 @@
         for h in group:
             cols = slice((start + h) * DH, (start + h + 1) * DH)
             att = loc_ref[:, cols] + jnp.dot(qm_ref[:, cols], p_ref[h], preferred_element_type=F32)
-            sums.append(att.astype(BF16))
+            sums.append(att.astype(BF16).astype(F32))
         for h, att in zip(group, sums):
-            att_ref[:, h * DH : (h + 1) * DH] = att
-            wide = att.astype(F32)
-            total = total + wide * wide
+            out_ref[:, h * DH : (h + 1) * DH] = att * gain_ref[:, columns(base + h * DH, 1)]
+            total = total + att * att
     return total
 
 
-def first_kernel(starts, *refs):
+def bases(at, starts, half):
+    own, other = at % 2 * half * DH, (1 - at % 2) * half * DH
+    return [(own if n < 2 else other) + start * DH for n, start in enumerate(starts)]
+
+
+def first_kernel(starts, at_ref, gain_ref, *refs):
     n = len(starts)
     ins, outs = refs[: 3 * n], refs[3 * n :]
     total = 0.0
-    for c, start in enumerate(starts):
-        total = total + attend(*ins[3 * c : 3 * c + 3], start, outs[c])
+    for c, base in enumerate(bases(at_ref[0], starts, ins[0].shape[1] // DH)):
+        total = total + attend(*ins[3 * c : 3 * c + 3], starts[c], gain_ref, base, outs[c])
     outs[n][...] = total
 
 
-def last_kernel(start, loc_ref, qm_ref, p_ref, at_ref, gain_ref, sum_ref, own_a_ref, own_b_ref, other_b_ref, out_ref, att_ref, done_ref, sems):
+def last_kernel(starts, at_ref, gain_ref, loc_ref, qm_ref, p_ref, sum_ref, c0_ref, c1_ref, c2_ref, out_ref, c3_ref, done_ref, sems):
     half = loc_ref.shape[1] // DH
-    cut = p_ref.shape[0]
-    core = at_ref[0] % 2
-    total = attend(loc_ref, qm_ref, p_ref, start, att_ref) + sum_ref[...]
+    there = bases(at_ref[0], starts, half)
+    total = attend(loc_ref, qm_ref, p_ref, starts[3], gain_ref, there[3], c3_ref) + sum_ref[...]
     width = 2 * half * DH
     scale = lax.rsqrt(jnp.sum(total, axis=1, keepdims=True) / width + 1e-5)
-    scale = jnp.broadcast_to(scale, (att_ref.shape[0], DH))
-    own, other = core * half * DH, (1 - core) * half * DH
+    scale = jnp.broadcast_to(scale, (c3_ref.shape[0], DH))
     copies = []
-    parts = ((own_a_ref, own), (own_b_ref, own + cut * DH), (other_b_ref, other + cut * DH), (att_ref, other))
-    for n, (src, base) in enumerate(parts):
+    for n, src in enumerate((c0_ref, c1_ref, c2_ref, c3_ref)):
         heads = src.shape[1] // DH
         for h in range(heads):
             cols = slice(h * DH, (h + 1) * DH)
-            gain = gain_ref[:, columns(base + h * DH, 1)]
-            done_ref[n, :, cols] = (src[:, cols].astype(F32) * scale * gain).astype(BF16)
-        copies.append(pltpu.make_async_copy(done_ref.at[n, :, : heads * DH], out_ref.at[:, columns(base, heads)], sems.at[n]))
+            done_ref[n, :, cols] = (src[:, cols] * scale).astype(BF16)
+        copies.append(pltpu.make_async_copy(done_ref.at[n, :, : heads * DH], out_ref.at[:, columns(there[n], heads)], sems.at[n]))
         copies[-1].start()
     for copy in copies:
         copy.wait()
@@ -352,37 +381,34 @@
     return lax.ppermute(state, axes, [(b, b + 1) for b in range(blocks - 1)])
 
 
-def finish_first(chunks):
-    rows = chunks[0][0].shape[0]
-    ins = [x for chunk in chunks for x in chunk[:3]]
-    shapes = [jax.ShapeDtypeStruct((rows, chunk[2].shape[0] * DH), BF16) for chunk in chunks]
-    return pl.pallas_call(
-        functools.partial(first_kernel, tuple(chunk[3] for chunk in chunks)),
+def finish(at, gain, chunks):
+    rows, half_width = chunks[0][0].shape
+    gain = gain.reshape(1, 2 * half_width)
+    starts = tuple(chunk[3] for chunk in chunks)
+    ins = [x for chunk in chunks[:-1] for x in chunk[:3]]
+    shapes = [jax.ShapeDtypeStruct((rows, chunk[2].shape[0] * DH), F32) for chunk in chunks[:-1]]
+    *parts, total = pl.pallas_call(
+        functools.partial(first_kernel, starts[:-1]),
         out_shape=shapes + [jax.ShapeDtypeStruct((rows, DH), F32)],
-        in_specs=[VMEM] * len(ins),
+        in_specs=[SMEM] + [VMEM] * (1 + len(ins)),
         out_specs=[VMEM] * (len(shapes) + 1),
         compiler_params=PARAMS,
-        cost_estimate=cost(2 * rows * DH * DH * 16, 1 << 21),
-    )(*ins)
-
-
-def finish_last(at, chunk, gain, own_a, own_b, other_b, total):
-    loc, qm, p, start = chunk
-    rows, half_width = loc.shape
-    widest = max(own_a.shape[1], own_b.shape[1])
-    return pl.pallas_call(
-        functools.partial(last_kernel, start),
+        cost_estimate=cost(3 * rows * DH * half_width, 1 << 21),
+    )(at, gain, *ins)
+    last = chunks[-1]
+    return pl.pallas_call(
+        functools.partial(last_kernel, starts),
         out_shape=jax.ShapeDtypeStruct((rows, 2 * half_width), BF16),
-        in_specs=[VMEM] * 3 + [SMEM] + [VMEM] * 5,
+        in_specs=[SMEM] + [VMEM] * (5 + len(parts)),
         out_specs=HBM,
         scratch_shapes=[
-            pltpu.VMEM((rows, p.shape[0] * DH), BF16),
-            pltpu.VMEM((4, rows, widest), BF16),
+            pltpu.VMEM((rows, last[2].shape[0] * DH), F32),
+            pltpu.VMEM((4, rows, max(chunk[2].shape[0] for chunk in chunks) * DH), BF16),
             pltpu.SemaphoreType.DMA((4,)),
         ],
         compiler_params=PARAMS,
         cost_estimate=cost(2 * rows * DH * half_width, 12 * rows * half_width),
-    )(loc, qm, p, at, gain.reshape(1, 2 * half_width), total, own_a, own_b, other_b)
+    )(at, gain, *last[:3], total, *parts)
 
 
 def general(lens, at, q, k, v, gain):
@@ -392,8 +418,9 @@
     before = scan(lens, at, masks, k, v)
     loc0, qm0 = local_part(at, masks, q, k, v, lambda a: 0, half)
     loc1, qm1 = local_part(at, masks, q, k, v, lambda a: half * DH, half)
-    first = finish_first([(loc0, qm0, before[:cut], 0), (loc0, qm0, before[cut:half], cut), (loc1, qm1, before[half + cut :], cut)])
-    return finish_last(at * 2, (loc1, qm1, before[half : half + cut], 0), gain, *first)
+    chunks = [(loc0, qm0, before[:cut], 0), (loc0, qm0, before[cut:half], cut)]
+    chunks += [(loc1, qm1, before[half + cut :], cut), (loc1, qm1, before[half : half + cut], 0)]
+    return finish(at * 2, gain, chunks)
 
 
 def neighbours(lens, at, q, k, v, gain):
@@ -404,7 +431,14 @@
     ctx_parts = lax.axis_size("ctx")
     pair = [(0, 1), (1, 0), (2, 3), (3, 2)]
     across = [(0, 2), (2, 0), (1, 3), (3, 1)]
-    onward = [(c, c + 1) for c in range(ctx_parts - 1)]
+    windows = lax.axis_size("groups")
+    first_round, second_round = [], []
+    for g in range(windows):
+        for c in range(ctx_parts):
+            for swaps, there in ((first_round, c ^ 1), (second_round, ((c + 1) ^ 1) - 1)):
+                inside = 0 <= there < ctx_parts
+                other = g ^ 1 if (g ^ 1) < windows else g
+                swaps.append((g * ctx_parts + c, g * ctx_parts + there if inside else other * ctx_parts + c))
     chunk_a, chunk_b = (cut, DH, DH), (half - cut, DH, DH)
 
     def own_half(a):
@@ -413,32 +447,35 @@
     def other_half(a):
         return (1 - a % 2) * half * DH
 
-    theirs_a, theirs_b, w, masks, k_in, v_in = opening(lens, at, k, v, half, cut)
+    theirs_b, w, masks = opening(lens, at, k, v, lambda a: other_half(a) + cut * DH, half - cut)
     got_b = lax.ppermute(theirs_b, "head", pair)
+    theirs_a, own = rest_states(at, masks, k, v, half, cut)
     got_a = lax.ppermute(theirs_a, "head", pair)
-    own = states(at, masks, k_in, v_in, own_half, half, BF16)
     b = small_call(functools.partial(chip_kernel, cut), [w, own, got_b], [chunk_b])
     r1 = lax.ppermute(b, "head", across)
     a = small_call(functools.partial(chip_kernel, 0), [w, own, got_a], [chunk_a])
-    r2 = lax.ppermute(a, "ctx", onward)
+    r2_odd = lax.ppermute(a, ("groups", "ctx"), first_round)
+    r2_even = lax.ppermute(a, ("groups", "ctx"), second_round)
     a, masks = lax.optimization_barrier((a, masks))
-    loc0, qm0 = local_part(at, masks, q, k_in, v_in, own_half, half)
+    loc0, qm0 = local_part(at, masks, q, k, v, own_half, half)
     r1, loc0 = lax.optimization_barrier((r1, loc0))
     p4 = small_call(carry_kernel, [w, b, r1], [chunk_b])
-    r4 = lax.ppermute(p4, "ctx", onward)
-    p4, r2 = lax.optimization_barrier((p4, r2))
-    p3 = small_call(relay_kernel, [w, a, r2], [chunk_a])
+    r4_odd = lax.ppermute(p4, ("groups", "ctx"), first_round)
+    r4_even = lax.ppermute(p4, ("groups", "ctx"), second_round)
+    p4, r2_odd, r2_even = lax.optimization_barrier((p4, r2_odd, r2_even))
+    p3, r2 = small_call(relay_kernel, [w, a, r2_odd, r2_even], [chunk_a] * 2)
     r3 = lax.ppermute(p3, "head", across)
     p3, masks = lax.optimization_barrier((p3, masks))
-    loc1, qm1 = local_part(at, masks, q, k_in, v_in, other_half, half)
-    r4, loc1 = lax.optimization_barrier((r4, loc1))
-    mine_b, send_b = small_call(functools.partial(join_kernel, cut, False), [r1, r4, w, own, got_b], [chunk_b] * 2)
+    loc1, qm1 = local_part(at, masks, q, k, v, other_half, half)
+    r4_odd, loc1 = lax.optimization_barrier((r4_odd, loc1))
+    ins = [w, r1, r4_odd, r4_even, own, got_b]
+    mine_b, send_b = small_call(functools.partial(join_b_kernel, cut), ins, [chunk_b] * 2)
     other_b = lax.ppermute(send_b, "head", pair)
-    r3, other_b = lax.optimization_barrier((r3, other_b))
-    mine_a, send_a = small_call(functools.partial(join_kernel, 0, True), [r3, r2, w, own, got_a], [chunk_a] * 2)
+    r3, mine_b = lax.optimization_barrier((r3, mine_b))
+    mine_a, send_a = small_call(join_a_kernel, [w, r3, r2, own, got_a], [chunk_a] * 2)
     other_a = lax.ppermute(send_a, "head", pair)
-    first = finish_first([(loc0, qm0, mine_a, 0), (loc0, qm0, mine_b, cut), (loc1, qm1, other_b, cut)])
-    return finish_last(at, (loc1, qm1, other_a, 0), gain, *first)
+    chunks = [(loc0, qm0, mine_a, 0), (loc0, qm0, mine_b, cut), (loc1, qm1, other_b, cut), (loc1, qm1, other_a, 0)]
+    return finish(at, gain, chunks)
 
 
 def per_device(queries, keys_in, values, doc_lengths, rms_gain):

time: 28 us -> 26.8 us (0.957)
  waiting for transfers between devices: 5.43 us -> 4.74 us
  starting transfers between devices: 12.5 us -> 11.9 us
  local copies, waits for them, and re-layouts: 0.01 us -> 0.33 us
  Pallas kernels: 9.79 us -> 9.5 us
    ppermute x1, waiting for transfers between devices: 2.13 us -> 1.13 us  [neighbours(): r3 = lax.ppermute(p3, 'head', across)]
    ppermute x2 -> x4, waiting for transfers between devices: 0.99 us -> 1.66 us  [the longest x1 0.91 us: neighbours(): r4_odd = lax.ppermute(p4, ('groups', 'ctx'), first_round)]
    ppermute x2 -> x4, starting transfers between devices: 7.24 us -> 6.63 us  [the longest x1 1.89 us: neighbours(): r4_odd = lax.ppermute(p4, ('groups', 'ctx'), first_round)]
    ppermute x1, waiting for transfers between devices: 1.07 us -> 0.59 us  [neighbours(): other_a = lax.ppermute(send_a, 'head', pair)]
    pallas_call x4, Pallas kernels: 4.46 us -> 4.06 us  [the longest x1 1.5 us: opening(): pl.pallas_call(functools.partial(opening_kernel, start, pieces), out_shap...]
    unnamed x2 -> x6, local copies, waits for them, and re-layouts: 0.01 us -> 0.33 us
    ppermute x1, waiting for transfers between devices: 0.58 us -> 0.27 us  [neighbours(): got_b = lax.ppermute(theirs_b, 'head', pair)]
    ppermute x1, waiting for transfers between devices: 0.65 us -> 0.94 us  [neighbours(): r1 = lax.ppermute(b, 'head', across)]
  transfers between devices with their start and end apart: 8 -> 10, of which waited for: 5 -> 7; matrix products, arithmetic and copies ran while one was open for 0% -> 0% of each run, Pallas kernels for 22% -> 25%
where the time goes in v5:
time: 26.8 us; the launch traced here: 26.6 us
  starting transfers between devices  11.9 us (44%)
  Pallas kernels  9.5 us (35%)
  waiting for transfers between devices  4.74 us (18%)
  local copies, waits for them, and re-layouts  0.33 us (1%)
    pallas_call x2, Pallas kernels, local_part(): pl.pallas_call(functools.partial(local_kernel, offset, pieces), out_shape...  4.73 us
    ppermute x1, starting transfers between devices, neighbours(): r1 = lax.ppermute(b, 'head', across)  2.92 us
    ppermute x1, starting transfers between devices, neighbours(): r4_odd = lax.ppermute(p4, ('groups', 'ctx'), first_round)  1.89 us
    ppermute x1, starting transfers between devices, neighbours(): r2_odd = lax.ppermute(a, ('groups', 'ctx'), first_round)  1.63 us
    ppermute x1, starting transfers between devices, neighbours(): r2_even = lax.ppermute(a, ('groups', 'ctx'), second_round)  1.58 us
    ppermute x1, starting transfers between devices, neighbours(): r3 = lax.ppermute(p3, 'head', across)  1.56 us
    ppermute x1, starting transfers between devices, neighbours(): r4_even = lax.ppermute(p4, ('groups', 'ctx'), second_round)  1.52 us
    pallas_call x1, Pallas kernels, opening(): pl.pallas_call(functools.partial(opening_kernel, start, pieces), out_shap...  1.5 us
  transfers between devices with their start and end apart: 10, of which 7 were waited for; matrix products, arithmetic and copies ran while one was open for 0% of the time, Pallas kernels for 25%

profile of v5, /device:TPU:0, one launch (start us, length us, event | category | flops | bytes accessed | tf_op | source)
XLA Modules:
  0.0 26.6 jit_solution(2326861334501136913)
XLA Ops:
  0.0 0.0 copy-start
  0.0 0.0 copy-start.1
  0.0 1.5 %shard_map.55 = (bf16[8,128,128]{2,1,0:T(8,128)(2,1)S(1)}, f32[8,128]{1,0:T(8,128)S(1)}, bf16[3,128,128]{2,1,0:T(8,128)(2,1)S(1)}) custom-call(s32[5]{0:T(128)} %len_hbm.1, s32[1]{0:T(128)} %bitcast.at_ref, bf16[128,4096]{1,0:T(8,128)(2,1)} %k_ref.5, bf16[128,4096]{1,0:T(8,128)(2,1)} %v_ref.5), custom_call_target="tpu_custom_call" | custom-call | flops 33554432 | bytes 524288 | tf_op jit(solution)/shard_map/pallas_call | solution.py:143
  1.5 0.5 %collective-permute-start = (bf16[8,128,128]{2,1,0:T(8,128)(2,1)S(1)}, bf16[8,128,128]{2,1,0:T(8,128)(2,1)S(1)}, u32[]{:S(2)}, u32[]{:S(2)}) collective-permute-start(bf16[8,128,128]{2,1,0:T(8,128)(2,1)S(1)} %get-tuple-element.38), channel_id=1, source_target_pairs={{0,1},{1,0},{2,3},{3,2},{4,5},{5,4},{6,7},{7,6},{8,9},{9,8},{10,11... | collective-permute-start | bytes 786440 | tf_op jit(solution)/shard_map/ppermute | solution.py:451
  2.0 0.0 copy-done
  2.0 0.0 copy-done.1
  2.0 0.7 %shard_map.56 = (bf16[8,128,128]{2,1,0:T(8,128)(2,1)S(1)}, bf16[16,128,128]{2,1,0:T(8,128)(2,1)S(1)}) custom-call(s32[1]{0:T(128)} %bitcast.at_ref, bf16[3,128,128]{2,1,0:T(8,128)(2,1)S(1)} %get-tuple-element.47.m_ref, bf16[128,4096]{1,0:T(8,128)(2,1)S(1)} %copy-done, bf16[128,4096]{1,0:T(8,128)(2,1)S(1)} %copy-done.1), custom_call_target="tpu_custom_call" | custom-call | tf_op jit(solution)/shard_map/pallas_call | solution.py:171
  2.7 0.2 collective-permute-start.2
  2.9 0.3 %collective-permute-done.got_ref = bf16[8,128,128]{2,1,0:T(8,128)(2,1)S(1)} collective-permute-done((bf16[8,128,128]{2,1,0:T(8,128)(2,1)S(1)}, bf16[8,128,128]{2,1,0:T(8,128)(2,1)S(1)}, u32[]{:S(2)}, u32[]{:S(2)}) %collective-permute-start) | collective-permute-done | bytes 262176 | tf_op jit(solution)/shard_map/ppermute | solution.py:451
  3.2 0.1 shard_map.57.b_ref
  3.3 2.9 %collective-permute-start.1 = (bf16[8,128,128]{2,1,0:T(8,128)(2,1)S(1)}, bf16[8,128,128]{2,1,0:T(8,128)(2,1)S(1)}, u32[]{:S(2)}, u32[]{:S(2)}) collective-permute-start(bf16[8,128,128]{2,1,0:T(8,128)(2,1)S(1)} %shard_map.57.b_ref), channel_id=1, source_target_pairs={{0,2},{2,0},{1,3},{3,1},{4,6},{6,4},{5,7},{7,5},{8,10},{10,8},{9,1... | collective-permute-start | bytes 786440 | tf_op jit(solution)/shard_map/ppermute | solution.py:455
  6.2 0.0 collective-permute-done.2.got_ref
  6.2 0.1 shard_map.58.a_ref
  6.3 1.6 %collective-permute-start.5 = (bf16[8,128,128]{2,1,0:T(8,128)(2,1)S(1)}, bf16[8,128,128]{2,1,0:T(8,128)(2,1)S(1)}, u32[]{:S(2)}, u32[]{:S(2)}) collective-permute-start(bf16[8,128,128]{2,1,0:T(8,128)(2,1)S(1)} %shard_map.58.a_ref), channel_id=1, source_target_pairs={{0,16},{4,8},{8,4},{12,28},{16,0},{20,24},{24,20},{28,12},{1,17},{... | collective-permute-start | bytes 786440 | tf_op jit(solution)/shard_map/ppermute | solution.py:458
  7.8 1.6 %collective-permute-start.4 = (bf16[8,128,128]{2,1,0:T(8,128)(2,1)S(1)}, bf16[8,128,128]{2,1,0:T(8,128)(2,1)S(1)}, u32[]{:S(2)}, u32[]{:S(2)}) collective-permute-start(bf16[8,128,128]{2,1,0:T(8,128)(2,1)S(1)} %shard_map.58.a_ref), channel_id=1, source_target_pairs={{0,4},{4,0},{8,12},{12,8},{16,20},{20,16},{24,28},{28,24},{1,5},{5... | collective-permute-start | bytes 786440 | tf_op jit(solution)/shard_map/ppermute | solution.py:457
  9.5 2.4 %shard_map.59 = (f32[128,2048]{1,0:T(8,128)S(1)}, bf16[128,2048]{1,0:T(8,128)(2,1)S(1)}) custom-call(s32[1]{0:T(128)} %bitcast.at_ref, bf16[3,128,128]{2,1,0:T(8,128)(2,1)S(1)} %get-tuple-element.47.m_ref, bf16[128,4096]{1,0:T(8,128)(2,1)} %q_hbm.3, bf16[128,4096]{1,0:T(8,128)(2,1)S(1)} %copy-done, bf16[128,4096]{1,0:T(8,128)(2,1)S(1)} %copy-done.1), custom_call_target="tpu_custom_call" | custom-call | tf_op jit(solution)/shard_map/pallas_call | solution.py:292
  11.9 0.9 %collective-permute-done.1.r1_ref = bf16[8,128,128]{2,1,0:T(8,128)(2,1)S(1)} collective-permute-done((bf16[8,128,128]{2,1,0:T(8,128)(2,1)S(1)}, bf16[8,128,128]{2,1,0:T(8,128)(2,1)S(1)}, u32[]{:S(2)}, u32[]{:S(2)}) %collective-permute-start.1) | collective-permute-done | bytes 262176 | tf_op jit(solution)/shard_map/ppermute | solution.py:455
  12.8 0.1 shard_map.60
  12.9 1.9 %collective-permute-start.3 = (bf16[8,128,128]{2,1,0:T(8,128)(2,1)S(1)}, bf16[8,128,128]{2,1,0:T(8,128)(2,1)S(1)}, u32[]{:S(2)}, u32[]{:S(2)}) collective-permute-start(bf16[8,128,128]{2,1,0:T(8,128)(2,1)S(1)} %shard_map.60), channel_id=1, source_target_pairs={{0,4},{4,0},{8,12},{12,8},{16,20},{20,16},{24,28},{28,24},{1,5},{5... | collective-permute-start | bytes 786440 | tf_op jit(solution)/shard_map/ppermute | solution.py:463
  14.8 1.5 %collective-permute-start.7 = (bf16[8,128,128]{2,1,0:T(8,128)(2,1)S(1)}, bf16[8,128,128]{2,1,0:T(8,128)(2,1)S(1)}, u32[]{:S(2)}, u32[]{:S(2)}) collective-permute-start(bf16[8,128,128]{2,1,0:T(8,128)(2,1)S(1)} %shard_map.60), channel_id=1, source_target_pairs={{0,16},{4,8},{8,4},{12,28},{16,0},{20,24},{24,20},{28,12},{1,17},{... | collective-permute-start | bytes 786440 | tf_op jit(solution)/shard_map/ppermute | solution.py:464
  16.3 0.0 collective-permute-done.5.even_ref
  16.3 0.0 collective-permute-done.4.odd_ref
  16.3 0.1 shard_map.61
  16.4 1.6 %collective-permute-start.6 = (bf16[8,128,128]{2,1,0:T(8,128)(2,1)S(1)}, bf16[8,128,128]{2,1,0:T(8,128)(2,1)S(1)}, u32[]{:S(2)}, u32[]{:S(2)}) collective-permute-start(bf16[8,128,128]{2,1,0:T(8,128)(2,1)S(1)} %get-tuple-element.46), channel_id=1, source_target_pairs={{0,2},{2,0},{1,3},{3,1},{4,6},{6,4},{5,7},{7,5},{8,10},{10,8},{9,1... | collective-permute-start | bytes 786440 | tf_op jit(solution)/shard_map/ppermute | solution.py:467
  18.0 2.4 %shard_map.62 = (f32[128,2048]{1,0:T(8,128)S(1)}, bf16[128,2048]{1,0:T(8,128)(2,1)S(1)}) custom-call(s32[1]{0:T(128)} %bitcast.at_ref, bf16[3,128,128]{2,1,0:T(8,128)(2,1)S(1)} %get-tuple-element.47.m_ref, bf16[128,4096]{1,0:T(8,128)(2,1)} %q_hbm.3, bf16[128,4096]{1,0:T(8,128)(2,1)S(1)} %copy-done, bf16[128,4096]{1,0:T(8,128)(2,1)S(1)} %copy-done.1), custom_call_target="tpu_custom_call" | custom-call | tf_op jit(solution)/shard_map/pallas_call | solution.py:292
  20.3 0.9 %collective-permute-done.3.odd_ref = bf16[8,128,128]{2,1,0:T(8,128)(2,1)S(1)} collective-permute-done((bf16[8,128,128]{2,1,0:T(8,128)(2,1)S(1)}, bf16[8,128,128]{2,1,0:T(8,128)(2,1)S(1)}, u32[]{:S(2)}, u32[]{:S(2)}) %collective-permute-start.3) | collective-permute-done | bytes 262176 | tf_op jit(solution)/shard_map/ppermute | solution.py:463
  21.3 0.7 %collective-permute-done.7.even_ref = bf16[8,128,128]{2,1,0:T(8,128)(2,1)S(1)} collective-permute-done((bf16[8,128,128]{2,1,0:T(8,128)(2,1)S(1)}, bf16[8,128,128]{2,1,0:T(8,128)(2,1)S(1)}, u32[]{:S(2)}, u32[]{:S(2)}) %collective-permute-start.7) | collective-permute-done | bytes 262176 | tf_op jit(solution)/shard_map/ppermute | solution.py:464
  22.0 0.2 shard_map.63
  22.2 0.1 collective-permute-start.9
  22.3 1.1 %collective-permute-done.6.r3_ref = bf16[8,128,128]{2,1,0:T(8,128)(2,1)S(1)} collective-permute-done((bf16[8,128,128]{2,1,0:T(8,128)(2,1)S(1)}, bf16[8,128,128]{2,1,0:T(8,128)(2,1)S(1)}, u32[]{:S(2)}, u32[]{:S(2)}) %collective-permute-start.6) | collective-permute-done | bytes 262176 | tf_op jit(solution)/shard_map/ppermute | solution.py:467
  23.4 0.0 copy-start.2
  23.4 0.2 shard_map.64
  23.6 0.1 collective-permute-start.8
  23.7 0.1 collective-permute-done.9.refs_8_
  23.8 0.3 %copy-done.2 = f32[4096]{0:T(1024)S(1)} copy-done((f32[4096]{0:T(1024)S(1)}, f32[4096]{0:T(1024)}, u32[]{:S(2)}) %copy-start.2) | copy-done | bytes 16408
  24.2 0.5 %shard_map.65 = (f32[128,1024]{1,0:T(8,128)S(1)}, f32[128,1024]{1,0:T(8,128)S(1)}, f32[128,1024]{1,0:T(8,128)S(1)}, f32[128,128]{1,0:T(8,128)S(1)}) custom-call(s32[1]{0:T(128)} %bitcast.at_ref, f32[1,4096]{1,0:T(1,128)S(1)} %bitcast.2, f32[128,2048]{1,0:T(8,128)S(1)} %get-tuple-element.56.refs_0_.refs_3_, ...), custom_call_target="tpu_custom_call" | custom-call | flops 100663296 | bytes 2097152 | tf_op jit(solution)/shard_map/pallas_call | solution.py:390
  24.6 0.6 %collective-permute-done.8.p_ref = bf16[8,128,128]{2,1,0:T(8,128)(2,1)S(1)} collective-permute-done((bf16[8,128,128]{2,1,0:T(8,128)(2,1)S(1)}, bf16[8,128,128]{2,1,0:T(8,128)(2,1)S(1)}, u32[]{:S(2)}, u32[]{:S(2)}) %collective-permute-start.8) | collective-permute-done | bytes 262176 | tf_op jit(solution)/shard_map/ppermute | solution.py:476
  25.2 1.4 %shard_map.66 = bf16[128,4096]{1,0:T(8,128)(2,1)} custom-call(s32[1]{0:T(128)} %bitcast.at_ref, f32[1,4096]{1,0:T(1,128)S(1)} %bitcast.3, f32[128,2048]{1,0:T(8,128)S(1)} %get-tuple-element.49.refs_6_.loc_ref, bf16[128,2048]{1,0:T(8,128)(2,1)S(1)} %get-tuple-element.50.refs_7_.qm_ref, bf16[8,128,128]{2,1,0:T(8,128)(2,1)S(1)} %collective-permute-done.8.p_ref, ...), custom_call_target="tpu_custom_call" | custom-call | flops 67108864 | bytes 3145728 | tf_op jit(solution)/shard_map/pallas_call | solution.py:399
Async XLA Ops:
  0.0 2.0 %copy-start = (bf16[128,4096]{1,0:T(8,128)(2,1)S(1)}, bf16[128,4096]{1,0:T(8,128)(2,1)}, u32[]{:S(2)}) copy-start(bf16[128,4096]{1,0:T(8,128)(2,1)} %k_ref.5) | copy-start | bytes 3145732
  0.0 2.0 %copy-start.1 = (bf16[128,4096]{1,0:T(8,128)(2,1)S(1)}, bf16[128,4096]{1,0:T(8,128)(2,1)}, u32[]{:S(2)}) copy-start(bf16[128,4096]{1,0:T(8,128)(2,1)} %v_ref.5) | copy-start | bytes 3145732
  1.5 1.7 %collective-permute-start = (bf16[8,128,128]{2,1,0:T(8,128)(2,1)S(1)}, bf16[8,128,128]{2,1,0:T(8,128)(2,1)S(1)}, u32[]{:S(2)}, u32[]{:S(2)}) collective-permute-start(bf16[8,128,128]{2,1,0:T(8,128)(2,1)S(1)} %get-tuple-element.38), channel_id=1, source_target_pairs={{0,1},{1,0},{2,3},{3,2},{4,5},{5,4},{6,7},{7,6},{8,9},{9,8},{10,11... | collective-permute-start | bytes 786440 | tf_op jit(solution)/shard_map/ppermute | solution.py:451
  2.7 3.4 %collective-permute-start.2 = (bf16[8,128,128]{2,1,0:T(8,128)(2,1)S(1)}, bf16[8,128,128]{2,1,0:T(8,128)(2,1)S(1)}, u32[]{:S(2)}, u32[]{:S(2)}) collective-permute-start(bf16[8,128,128]{2,1,0:T(8,128)(2,1)S(1)} %get-tuple-element.39), channel_id=1, source_target_pairs={{0,1},{1,0},{2,3},{3,2},{4,5},{5,4},{6,7},{7,6},{8,9},{9,8},{10,11... | collective-permute-start | bytes 786440 | tf_op jit(solution)/shard_map/ppermute | solution.py:453
  3.3 9.5 %collective-permute-start.1 = (bf16[8,128,128]{2,1,0:T(8,128)(2,1)S(1)}, bf16[8,128,128]{2,1,0:T(8,128)(2,1)S(1)}, u32[]{:S(2)}, u32[]{:S(2)}) collective-permute-start(bf16[8,128,128]{2,1,0:T(8,128)(2,1)S(1)} %shard_map.57.b_ref), channel_id=1, source_target_pairs={{0,2},{2,0},{1,3},{3,1},{4,6},{6,4},{5,7},{7,5},{8,10},{10,8},{9,1... | collective-permute-start | bytes 786440 | tf_op jit(solution)/shard_map/ppermute | solution.py:455
  6.3 10.0 %collective-permute-start.5 = (bf16[8,128,128]{2,1,0:T(8,128)(2,1)S(1)}, bf16[8,128,128]{2,1,0:T(8,128)(2,1)S(1)}, u32[]{:S(2)}, u32[]{:S(2)}) collective-permute-start(bf16[8,128,128]{2,1,0:T(8,128)(2,1)S(1)} %shard_map.58.a_ref), channel_id=1, source_target_pairs={{0,16},{4,8},{8,4},{12,28},{16,0},{20,24},{24,20},{28,12},{1,17},{... | collective-permute-start | bytes 786440 | tf_op jit(solution)/shard_map/ppermute | solution.py:458
  7.8 8.4 %collective-permute-start.4 = (bf16[8,128,128]{2,1,0:T(8,128)(2,1)S(1)}, bf16[8,128,128]{2,1,0:T(8,128)(2,1)S(1)}, u32[]{:S(2)}, u32[]{:S(2)}) collective-permute-start(bf16[8,128,128]{2,1,0:T(8,128)(2,1)S(1)} %shard_map.58.a_ref), channel_id=1, source_target_pairs={{0,4},{4,0},{8,12},{12,8},{16,20},{20,16},{24,28},{28,24},{1,5},{5... | collective-permute-start | bytes 786440 | tf_op jit(solution)/shard_map/ppermute | solution.py:457
  12.9 8.4 %collective-permute-start.3 = (bf16[8,128,128]{2,1,0:T(8,128)(2,1)S(1)}, bf16[8,128,128]{2,1,0:T(8,128)(2,1)S(1)}, u32[]{:S(2)}, u32[]{:S(2)}) collective-permute-start(bf16[8,128,128]{2,1,0:T(8,128)(2,1)S(1)} %shard_map.60), channel_id=1, source_target_pairs={{0,4},{4,0},{8,12},{12,8},{16,20},{20,16},{24,28},{28,24},{1,5},{5... | collective-permute-start | bytes 786440 | tf_op jit(solution)/shard_map/ppermute | solution.py:463
  14.8 7.2 %collective-permute-start.7 = (bf16[8,128,128]{2,1,0:T(8,128)(2,1)S(1)}, bf16[8,128,128]{2,1,0:T(8,128)(2,1)S(1)}, u32[]{:S(2)}, u32[]{:S(2)}) collective-permute-start(bf16[8,128,128]{2,1,0:T(8,128)(2,1)S(1)} %shard_map.60), channel_id=1, source_target_pairs={{0,16},{4,8},{8,4},{12,28},{16,0},{20,24},{24,20},{28,12},{1,17},{... | collective-permute-start | bytes 786440 | tf_op jit(solution)/shard_map/ppermute | solution.py:464
  16.4 7.0 %collective-permute-start.6 = (bf16[8,128,128]{2,1,0:T(8,128)(2,1)S(1)}, bf16[8,128,128]{2,1,0:T(8,128)(2,1)S(1)}, u32[]{:S(2)}, u32[]{:S(2)}) collective-permute-start(bf16[8,128,128]{2,1,0:T(8,128)(2,1)S(1)} %get-tuple-element.46), channel_id=1, source_target_pairs={{0,2},{2,0},{1,3},{3,1},{4,6},{6,4},{5,7},{7,5},{8,10},{10,8},{9,1... | collective-permute-start | bytes 786440 | tf_op jit(solution)/shard_map/ppermute | solution.py:467
  22.2 1.6 %collective-permute-start.9 = (bf16[8,128,128]{2,1,0:T(8,128)(2,1)S(1)}, bf16[8,128,128]{2,1,0:T(8,128)(2,1)S(1)}, u32[]{:S(2)}, u32[]{:S(2)}) collective-permute-start(bf16[8,128,128]{2,1,0:T(8,128)(2,1)S(1)} %get-tuple-element.60), channel_id=1, source_target_pairs={{0,1},{1,0},{2,3},{3,2},{4,5},{5,4},{6,7},{7,6},{8,9},{9,8},{10,11... | collective-permute-start | bytes 786440 | tf_op jit(solution)/shard_map/ppermute | solution.py:473
  23.4 0.7 %copy-start.2 = (f32[4096]{0:T(1024)S(1)}, f32[4096]{0:T(1024)}, u32[]{:S(2)}) copy-start(f32[4096]{0:T(1024)} %param.9) | copy-start | bytes 49156
  23.6 1.6 %collective-permute-start.8 = (bf16[8,128,128]{2,1,0:T(8,128)(2,1)S(1)}, bf16[8,128,128]{2,1,0:T(8,128)(2,1)S(1)}, u32[]{:S(2)}, u32[]{:S(2)}) collective-permute-start(bf16[8,128,128]{2,1,0:T(8,128)(2,1)S(1)} %get-tuple-element.55), channel_id=1, source_target_pairs={{0,1},{1,0},{2,3},{3,2},{4,5},{5,4},{6,7},{7,6},{8,9},{9,8},{10,11... | collective-permute-start | bytes 786440 | tf_op jit(solution)/shard_map/ppermute | solution.py:476
